TPU v7x, 128 devices: a whole 4x4x4 slice. The times are simulated.
128 devices in a mesh: dp: 2 (over z_lo), seq: 8 (over z_hi, x), col: 8 (over y, core).
Axes of the slice: x: 4, y: 4, z: 4 (z_hi: 2, z_lo: 2; z = z_hi * 2 + z_lo), core: 2. Of those that a mesh axis runs over, the one named last changes fastest.
Arguments:
- inputs: bfloat16 [2, 4096, 1024], P('dp', 'seq'), may hold values from -6 to 6
- cotangent: bfloat16 [2, 4096, 1024], P('dp', 'seq'), may hold values from -6 to 6
- norm_gain: float32 [1024], replicated, may hold values from 0.1 to 1.9
- proj_in: bfloat16 [4, 1024, 1024], P(None, None, 'col'), may hold values from -0.1875 to 0.1875
- proj_out: bfloat16 [1024, 1024], P('col'), may hold values from -0.1875 to 0.1875
- item_ids: int32 [2, 4096], P('dp', 'seq'), may hold values from 0 to 16383
- lengths: int32 [2], P('dp'), may hold values from 128 to 4096, as said below
- tile_mask: int32 [2, 32, 32], P('dp'), may hold values from 0 to 1, as said below
Outputs:
- grad_proj_in: float32 [4, 1024, 1024], P(None, None, 'col')
- grad_proj_out: float32 [1024, 1024], P('col')
- grad_gain: float32 [1024], P('col')
- table_grad: float32 [16384, 1024], P(('dp', 'seq'), 'col')
Inputs may be any that keep to these rules, and one draw needn't show every extreme that they name: `lengths`: each length is a multiple of 128; some user has exactly 4096. `tile_mask`: tiles above the diagonal are 0, diagonal tiles are 1, tiles below the diagonal are 0 or 1.
All inputs are finite; a program needn't handle non-finite values.
Results may differ from a plain program's by a relative error of at most 0.006.
Values may be sent and summed in bfloat16 or wider, within the bound.
No kernel may reach another device: no remote copies, remote signals or barrier semaphores. Data moves between devices by JAX's collectives and lax.ppermute only.
A program may use at most 64 MiB of HBM per device.

v0:
```python
import functools
import math

import jax
import jax.numpy as jnp
from jax import lax
from jax.experimental import pallas as pl
from jax.experimental.pallas import tpu as pltpu
from jax.sharding import PartitionSpec as P

BLOCK = 128
EPSILON = 1e-06
BF16 = jnp.bfloat16
F32 = jnp.float32
MIB = 1024 * 1024
EXTRA = 16
NT = (((1,), (1,)), ((), ()))
TN = (((0,), (0,)), ((), ()))


def kernel_call(body, out_shape, name, flops=1000, bytes_accessed=1000, vmem=24, **kwargs):
    return pl.pallas_call(
        body,
        out_shape=out_shape,
        name=name,
        compiler_params=pltpu.CompilerParams(vmem_limit_bytes=vmem * MIB),
        cost_estimate=pl.CostEstimate(flops=flops, bytes_accessed=bytes_accessed, transcendentals=0),
        **kwargs,
    )


def shape_of(shape, dtype):
    return jax.ShapeDtypeStruct(shape, dtype)


def swap_plane(value):
    return lax.all_to_all(value, ("dp", "seq"), 0, 0, tiled=True)


def move_seq(value, dz_hi, dx):
    pairs = [(i, ((i // 4 + dz_hi) % 2) * 4 + (i % 4 + dx) % 4) for i in range(8)]
    return lax.ppermute(value, "seq", pairs)


def move_y(value, dy):
    return lax.ppermute(value, "col", [(i, ((i // 2 + dy) % 4) * 2 + i % 2) for i in range(8)])


def move_core(value):
    return lax.ppermute(value, "col", [(i, i ^ 1) for i in range(8)])


def project_body(length_ref, x_ref, cot_ref, gain_ref, proj_ref, out_ref, mask_ref,
                 own_ref, cross_ref, near1_ref, near2_ref, near3_ref, pre_ref, normed_ref, grad_ref, dmix_ref, upd_ref, inv_cnt_ref, inv_rms_ref, both_ref):
    length, rank = length_ref[0], lax.axis_index("seq")
    step, col = dmix_ref.shape

    @pl.when(pl.program_id(0) == 0)
    def _():
        for c in range(4):
            both_ref[:, pl.ds(c * col, col)] = proj_ref[c]

    x = x_ref[...].astype(F32)
    inv_rms = lax.rsqrt(jnp.mean(x * x, axis=1, keepdims=True) + EPSILON)
    normed = (x * inv_rms * gain_ref[...]).astype(BF16)
    normed_ref[...] = normed
    inv_rms_ref[...] = jnp.broadcast_to(inv_rms, inv_rms_ref.shape)
    pre = jnp.dot(normed, both_ref[...], preferred_element_type=F32)
    act = (pre * jax.nn.sigmoid(pre)).astype(BF16)
    for c in range(4):
        pre_ref[c] = pre[:, c * col:(c + 1) * col]
    tile = (rank * pl.num_programs(0) + pl.program_id(0)) * (step // BLOCK)
    local = lax.broadcasted_iota(jnp.int32, (step, 1), 0)
    position = tile * BLOCK + local
    grad = jnp.where(position < length, cot_ref[...].astype(F32), 0.0).astype(BF16)
    grad_ref[...] = grad
    d_mixed = lax.dot_general(grad, out_ref[...], NT, preferred_element_type=F32)
    dmix_ref[...] = d_mixed
    update = act[:, :col]
    upd_ref[...] = update
    tiles = mask_ref.shape[0]
    rows = lax.broadcasted_iota(jnp.int32, (tiles, tiles), 0)
    cols = lax.broadcasted_iota(jnp.int32, (tiles, tiles), 1)
    filled = jnp.clip(length - BLOCK * cols, 0, BLOCK)
    counted = jnp.where(cols < rows, mask_ref[...] * filled, 0)
    earlier = jnp.zeros((step, 1), F32)
    for index in range(step // BLOCK):
        picked = jnp.where(rows == tile + index, counted, 0).astype(F32)
        total = jnp.sum(jnp.sum(picked, axis=1, keepdims=True), axis=0, keepdims=True)
        earlier = jnp.where(local // BLOCK == index, total, earlier)
    own_first = tile * BLOCK + local // BLOCK * BLOCK
    diagonal = jnp.minimum(local % BLOCK + 1, jnp.clip(length - own_first, 0, BLOCK)).astype(F32)
    inv_cnt = 1.0 / jnp.maximum(earlier + diagonal, 1.0)
    inv_cnt_ref[...] = jnp.broadcast_to(inv_cnt, inv_cnt_ref.shape)
    qd = (act[:, col:2 * col], (d_mixed * update.astype(F32) * inv_cnt).astype(BF16))
    kv = (act[:, 2 * col:3 * col], act[:, 3 * col:])
    for index in range(2):
        own_ref[0, index], own_ref[1, index] = qd[index], kv[index]
    x_pos = lax.rem(rank, 4)
    later = [rank < 4] + [x_pos + k < 4 for k in (1, 2, 3)]
    for ref, is_later in zip((cross_ref, near1_ref, near2_ref, near3_ref), later):

        @pl.when(is_later)
        def _():
            ref[0], ref[1] = kv

        @pl.when(jnp.logical_not(is_later))
        def _():
            ref[0], ref[1] = qd


def project(lengths, x, cot, gain, proj_in, proj_out, mask):
    tok, width = x.shape
    col = proj_in.shape[2]
    step = 2 * BLOCK
    row = lambda i, w: (i, 0)
    side = lambda i, w: (0, i, 0)
    pair = lambda i, w: (0, 0, i, 0)
    fixed2 = lambda i, w: (0, 0)
    return kernel_call(
        project_body,
        (
            shape_of((2, 2, tok, col), BF16),
            *(shape_of((2, tok, col), BF16) for _ in range(4)),
            shape_of((4, tok, col), F32),
            shape_of((tok, width), BF16),
            shape_of((tok, width), BF16),
            shape_of((tok, col), F32),
            shape_of((tok, col), BF16),
            shape_of((tok, col), F32),
            shape_of((tok, col), F32),
        ),
        "project",
        vmem=63,
        grid_spec=pltpu.PrefetchScalarGridSpec(
            num_scalar_prefetch=1,
            grid=(tok // step,),
            in_specs=[
                pl.BlockSpec((step, width), row),
                pl.BlockSpec((step, width), row),
                pl.BlockSpec((1, width), fixed2),
                pl.BlockSpec((4, width, col), lambda i, w: (0, 0, 0)),
                pl.BlockSpec((col, width), fixed2),
                pl.BlockSpec(mask.shape, fixed2),
            ],
            out_specs=[
                pl.BlockSpec((2, 2, step, col), pair),
                *(pl.BlockSpec((2, step, col), side) for _ in range(4)),
                pl.BlockSpec((4, step, col), side),
                pl.BlockSpec((step, width), row),
                pl.BlockSpec((step, width), row),
                pl.BlockSpec((step, col), row),
                pl.BlockSpec((step, col), row),
                pl.BlockSpec((step, col), row),
                pl.BlockSpec((step, col), row),
            ],
            scratch_shapes=[pltpu.VMEM((width, 4 * col), BF16)],
        ),
    )(lengths, x, cot, gain.reshape(1, -1), proj_in, proj_out, mask)


def block_terms(a1, a2, b1, b2, keep, scale):
    half = lax.dot_general(a1, b1, NT, preferred_element_type=F32) * (keep * (0.5 * scale))
    other = lax.dot_general(a2, b2, NT, preferred_element_type=F32) * keep
    tanh = jnp.tanh(half)
    twice = 1.0 + tanh
    probs = half * twice
    slope = (other * (twice + probs * (1.0 - tanh))).astype(BF16)
    first = jnp.dot(probs.astype(BF16), b2, preferred_element_type=F32)
    second = jnp.dot(slope, b1, preferred_element_type=F32)
    return first, second


def block_sums(side, own_ref, other, keep_of, scale):
    tok, col = own_ref.shape[2:]
    part = 2 * BLOCK
    first, second = jnp.zeros((tok, col), F32), jnp.zeros((tok, col), F32)
    for start in range(0, tok, part):
        span = pl.ds(start, part)
        terms = block_terms(
            own_ref[side, 0], own_ref[side, 1], other[0][span, :], other[1][span, :], keep_of(start, part), scale
        )
        first, second = first + terms[0], second + terms[1]
    return first, second


def far_sums(index, side_ref, own_ref, other_ref, keep_ref, scale):
    def keep_of(start, part):
        return by_tile(keep_ref[index, :, pl.ds(start, part)], own_ref.shape[2])

    return block_sums(side_ref[index], own_ref, (other_ref.at[0], other_ref.at[1]), keep_of, scale)


def by_tile(rows, tok):
    tiles, part = rows.shape
    return jnp.broadcast_to(rows[:, None, :], (tiles, tok // tiles, part)).reshape(tok, part)


def near_body(side_ref, own_ref, keep_own_ref, keep_ref, *refs, scale):
    others, acc_ref = refs[:-1], refs[-1]
    tok = own_ref.shape[2]
    for side in range(2):
        other = own_ref.at[1 - side, 0], own_ref.at[1 - side, 1]

        def keep_of(start, part):
            keep = by_tile(keep_own_ref[side, :, pl.ds(start, part)], tok)
            row = lax.broadcasted_iota(jnp.int32, (tok, part), 0)
            column = lax.broadcasted_iota(jnp.int32, (tok, part), 1) + start
            ordered = (column <= row) if side == 0 else (row <= column)
            return jnp.where(ordered, keep, 0.0)

        acc_ref[side, 0], acc_ref[side, 1] = block_sums(side, own_ref, other, keep_of, scale)
    for index, other in enumerate(others):
        first, second = far_sums(index, side_ref, own_ref, other, keep_ref, scale)
        acc_ref[side_ref[index], 0] += first
        acc_ref[side_ref[index], 1] += second


def near_terms(sides, own, keep_own, keep, others, scale):
    whole = pl.BlockSpec(memory_space=pltpu.VMEM)
    return kernel_call(
        functools.partial(near_body, scale=scale),
        shape_of(own.shape, F32),
        "near_terms",
        vmem=63,
        in_specs=[pl.BlockSpec(memory_space=pltpu.SMEM)] + [whole] * (3 + len(others)),
        out_specs=whole,
    )(sides, own, keep_own, keep, *others)


FAR_INPUTS = 13


def far_body(side_ref, *refs, scale):
    sources, d_ref, parts_ref = refs[:FAR_INPUTS], refs[FAR_INPUTS], refs[FAR_INPUTS + 1]
    held, mixed_ref, sems = refs[FAR_INPUTS + 2:2 * FAR_INPUTS + 2], refs[-2], refs[-1]
    copies = [pltpu.make_async_copy(source, place, sems.at[n]) for n, (source, place) in enumerate(zip(sources, held))]
    for copy in copies:
        copy.start()
    own_ref, keep_ref = held[:2]
    others, acc_ref = held[2:5], held[5]
    pre_ref, inv_rms_ref, dmix_ref, upd_ref, inv_cnt_ref, normed_t_ref, grad_t_ref = held[6:]
    copies[0].wait()
    copies[1].wait()
    for index, other in enumerate(others):
        copies[2 + index].wait()
        first, second = far_sums(index, side_ref, own_ref, other, keep_ref, scale)
        if index == 0:
            copies[5].wait()
        acc_ref[side_ref[index], 0] += first
        acc_ref[side_ref[index], 1] += second
    for copy in copies[6:11]:
        copy.wait()
    pre_grad_body(acc_ref, pre_ref, inv_rms_ref, dmix_ref, upd_ref, inv_cnt_ref, d_ref, mixed_ref, scale=scale)
    for copy in copies[11:]:
        copy.wait()
    weight_body(normed_t_ref, grad_t_ref, d_ref, mixed_ref, parts_ref)


def far_terms(sides, own, keep, others, acc, pre, inv_rms, dmix, upd, inv_cnt, normed_t, grad_t, owners, scale):
    _, _, tok, col = own.shape
    width = normed_t.shape[0]
    sources = (own, keep, *others, acc, pre, inv_rms, dmix, upd, inv_cnt, normed_t, grad_t)
    return kernel_call(
        functools.partial(far_body, scale=scale),
        (shape_of((tok + EXTRA, 4 * col), BF16), shape_of((owners, 5 * width // owners, col), BF16)),
        "far_terms",
        vmem=63,
        in_specs=[pl.BlockSpec(memory_space=pltpu.SMEM)] + [pl.BlockSpec(memory_space=pl.ANY)] * len(sources),
        scratch_shapes=[
            *(pltpu.VMEM(source.shape, source.dtype) for source in sources),
            pltpu.VMEM((tok, col), BF16),
            pltpu.SemaphoreType.DMA((len(sources),)),
        ],
    )(sides, *sources)


def pre_grad_body(acc_ref, pre_ref, inv_rms_ref, dmix_ref, upd_ref, inv_cnt_ref, d_ref, mixed_ref, *, scale):
    tok, col = dmix_ref.shape
    stat = jnp.zeros((tok, col), F32)
    attended = acc_ref[0, 0] * inv_cnt_ref[...]
    mixed_ref[...] = (attended * upd_ref[...].astype(F32)).astype(BF16)
    grads = (
        dmix_ref[...] * attended,
        acc_ref[0, 1] * (0.5 * scale),
        acc_ref[1, 1] * (0.5 * scale),
        acc_ref[1, 0],
    )
    for c in range(4):
        pre = pre_ref[c]
        sig = jax.nn.sigmoid(pre)
        d_pre = (grads[c] * (sig * (1.0 + pre * (1.0 - sig)))).astype(BF16)
        d_ref[pl.ds(0, tok), pl.ds(c * col, col)] = d_pre
        stat = stat + d_pre.astype(F32) * pre
    stat = stat / inv_rms_ref[...]
    high = stat.astype(BF16)
    low = (stat - high.astype(F32)).astype(BF16)
    ones = jnp.ones((8, col), BF16)
    sums = lax.dot_general(ones, high, NT, preferred_element_type=F32)
    sums = sums + lax.dot_general(ones, low, NT, preferred_element_type=F32)
    d_ref[pl.ds(tok, EXTRA), :] = two_rows(sums[0:1])


def two_rows(value):
    high = value.astype(BF16).astype(F32)
    low = value - high
    row = lax.broadcasted_iota(jnp.int32, (EXTRA, value.shape[1]), 0)
    both = jnp.where(row == 0, jnp.broadcast_to(high, row.shape), jnp.where(row == 1, jnp.broadcast_to(low, row.shape), 0.0))
    return both.astype(BF16)


def back_body(own_ref, peer_ref, w_own_ref, w_peer_ref, *outs):
    tok = own_ref.shape[0] - EXTRA
    part = lax.dot_general(own_ref[pl.ds(0, tok), :], w_own_ref[...], NT, preferred_element_type=F32)
    part = part + lax.dot_general(peer_ref[pl.ds(0, tok), :], w_peer_ref[...], NT, preferred_element_type=F32)
    sums = jnp.sum(
        own_ref[pl.ds(tok, EXTRA), :].astype(F32) + peer_ref[pl.ds(tok, EXTRA), :].astype(F32), axis=0, keepdims=True
    )
    high = sums.astype(BF16).astype(F32)
    low = sums - high
    col = outs[0].shape[1]
    row = lax.broadcasted_iota(jnp.int32, (EXTRA, col), 0)
    extra = jnp.zeros((EXTRA, col), F32)
    for tile in range(tok // BLOCK):
        span = slice(tile * BLOCK, (tile + 1) * BLOCK)
        extra = jnp.where(row == 4 * tile, jnp.broadcast_to(high[:, span], row.shape), extra)
        extra = jnp.where(row == 4 * tile + 1, jnp.broadcast_to(low[:, span], row.shape), extra)
    extra = extra.astype(BF16)
    for k, out in enumerate(outs):
        out[pl.ds(0, tok), :] = part[:, k * col:(k + 1) * col].astype(BF16)
        out[pl.ds(tok, EXTRA), :] = extra


def back_project(own, peer, w_own, w_peer, col):
    rows, depth = own.shape
    return kernel_call(
        back_body,
        tuple(shape_of((rows, col), BF16) for _ in range(4)),
        "back_project",
    )(own, peer, w_own, w_peer)


def weight_body(normed_t_ref, grad_t_ref, d_ref, mixed_ref, out_ref):
    tok, col = mixed_ref.shape
    share = out_ref.shape[1] // 5
    step = 8 * share
    for part in range(2):
        rows = pl.ds(part * step, step)
        value = jnp.dot(normed_t_ref[rows, :], d_ref[pl.ds(0, tok), :], preferred_element_type=F32)
        last = jnp.dot(grad_t_ref[rows, :], mixed_ref[...], preferred_element_type=F32)
        for c in range(5):
            piece = value[:, c * col:(c + 1) * col] if c < 4 else last
            out_ref[pl.ds(part * 8, 8), pl.ds(c * share, share), :] = piece.astype(BF16).reshape(8, share, col)


def join_body(parts_ref, block_ref, out_ref, total_ref):
    held = parts_ref.shape[1]

    @pl.when(pl.program_id(0) == 0)
    def _():
        total = parts_ref[0].astype(F32)
        for index in range(1, parts_ref.shape[0]):
            total = total + parts_ref[index].astype(F32)
        total_ref[...] = total.astype(BF16)

    for index in range(out_ref.shape[0]):
        out_ref[index, pl.ds(0, held), :] = total_ref[...]
        out_ref[index, pl.ds(held, block_ref.shape[1]), :] = block_ref[index]


def join_sums(parts, blocks):
    owners, held, col = parts.shape
    rows = blocks.shape[1]
    step = 4
    return kernel_call(
        join_body,
        shape_of((owners, held + rows, col), BF16),
        "join_sums",
        grid=(owners // step,),
        in_specs=[
            pl.BlockSpec(parts.shape, lambda i: (0, 0, 0)),
            pl.BlockSpec((step, rows, col), lambda i: (i, 0, 0)),
        ],
        out_specs=pl.BlockSpec((step, held + rows, col), lambda i: (i, 0, 0)),
        scratch_shapes=[pltpu.VMEM((held, col), BF16)],
    )(parts, blocks)


def prepare_body(place_ref, normed_ref, grad_ref, proj_ref, x_ref, inv_rms_ref,
                 normed_t_ref, grad_t_ref, own_ref, peer_ref, x_cols_ref, grad_cols_ref):
    place = place_ref[0]
    y_pos, core = place // 2, lax.rem(place, 2)
    col = proj_ref.shape[2]
    normed_t_ref[...] = normed_ref[...].T
    grad_t_ref[...] = grad_ref[...].T
    pair = lax.rem(y_pos + pl.program_id(0), 4) * 2
    for c in range(4):
        span = pl.ds(c * col, col)
        own_ref[:, span] = proj_ref[c, pl.ds(pl.multiple_of((pair + core) * col, col), col), :]
        peer_ref[:, span] = proj_ref[c, pl.ds(pl.multiple_of((pair + 1 - core) * col, col), col), :]
    mine = pl.ds(pl.multiple_of(place * col, col), col)
    x_cols_ref[...] = x_ref[...].astype(F32) * inv_rms_ref[...]
    grad_cols_ref[...] = grad_ref[:, mine].astype(F32)


def prepare(place, normed, grad, proj_in, x, inv_rms):
    tok, width = normed.shape
    col = proj_in.shape[2]
    step = tok // 4
    row = lambda i, w: (i, 0)
    column = lambda i, w: (0, i)
    return kernel_call(
        prepare_body,
        (
            shape_of((width, tok), BF16),
            shape_of((width, tok), BF16),
            shape_of((4 * col, 4 * col), BF16),
            shape_of((4 * col, 4 * col), BF16),
            shape_of((tok, col), F32),
            shape_of((tok, col), F32),
        ),
        "prepare",
        vmem=63,
        grid_spec=pltpu.PrefetchScalarGridSpec(
            num_scalar_prefetch=1,
            grid=(4,),
            in_specs=[
                pl.BlockSpec((step, width), row),
                pl.BlockSpec((step, width), row),
                pl.BlockSpec(proj_in.shape, lambda i, w: (0, 0, 0)),
                pl.BlockSpec((step, col), lambda i, w: (i, w[0])),
                pl.BlockSpec((step, col), row),
            ],
            out_specs=[
                pl.BlockSpec((width, step), column),
                pl.BlockSpec((width, step), column),
                pl.BlockSpec((col, 4 * col), row),
                pl.BlockSpec((col, 4 * col), row),
                pl.BlockSpec((step, col), row),
                pl.BlockSpec((step, col), row),
            ],
        ),
    )(place, normed, grad, proj_in, x, inv_rms)


def fill_slots(slot_ref, item_ref, value_ref, blocks, owners, extra):
    room = blocks[0].shape[0] - EXTRA
    tok = slot_ref.shape[1]
    group = 4
    local = lax.broadcasted_iota(jnp.int32, (room, tok), 0)
    for first in range(0, len(blocks), group):
        hots = [jnp.where(slot_ref[...] == local + owner * room, 1.0, 0.0) for owner in owners[first:first + group]]
        hot = jnp.concatenate(hots, axis=0).astype(BF16)
        moved = jnp.dot(hot, value_ref[...], preferred_element_type=F32).astype(BF16)
        items = lax.dot_general(item_ref[...], hot, NT, preferred_element_type=F32)
        for index in range(group):
            span = slice(index * room, (index + 1) * room)
            block = blocks[first + index]
            block[pl.ds(0, room), :] = moved[span]
            block[pl.ds(room, EXTRA), :] = (extra + items[:, span]).astype(BF16)


def fill_all(slot_ref, item_ref, value_ref, out_ref, extra):
    owners = list(range(out_ref.shape[0]))
    fill_slots(slot_ref, item_ref, value_ref, [out_ref.at[owner] for owner in owners], owners, extra)


def input_grad_body(*refs):
    parts = refs[:4]
    x_ref, gain_ref, inv_rms_ref, grad_ref, slot_ref, item_ref, value_ref = refs[4:11]
    out_ref = refs[11]
    tok, col = x_ref.shape
    d_normed = parts[0][pl.ds(0, tok), :].astype(F32)
    for part in parts[1:]:
        d_normed = d_normed + part[pl.ds(0, tok), :].astype(F32)
    gain_sum = two_rows(jnp.sum(d_normed * x_ref[...], axis=0, keepdims=True)).astype(F32)
    extra = [part[pl.ds(tok, EXTRA), :] for part in parts]
    row = lax.broadcasted_iota(jnp.int32, (EXTRA, col), 0)
    for tile in range(tok // BLOCK):
        rows = pl.ds(tile * BLOCK, BLOCK)
        pick = jnp.where((row >= 4 * tile) & (row < 4 * tile + 4), 1.0, 0.0).astype(BF16)
        mean = jnp.zeros((BLOCK, col), F32)
        for piece in extra:
            mean = mean + lax.dot_general(piece, pick, TN, preferred_element_type=F32)
        inv = inv_rms_ref[rows, :]
        d_t = d_normed[tile * BLOCK:(tile + 1) * BLOCK]
        mean = mean * inv * (1.0 / (8 * col))
        value = inv * (d_t * gain_ref[...] - x_ref[rows, :] * mean) + grad_ref[rows, :]
        value_ref[rows, :] = value.astype(BF16)
    rounds = jnp.max(item_ref[pl.ds(5, 1), :].astype(F32), axis=1, keepdims=True)
    fill_all(slot_ref, item_ref, value_ref, out_ref, gain_sum + jnp.where(row == 4, rounds, 0.0))


def input_grads(parts, x_cols, gain_cols, inv_rms, grad_cols, slots, items, owners, room):
    tok, col = x_cols.shape
    return kernel_call(
        input_grad_body,
        (shape_of((tok, col), BF16), shape_of((owners, room + EXTRA, col), BF16)),
        "input_grads",
    )(*parts, x_cols, gain_cols.reshape(1, -1), inv_rms, grad_cols, slots, items)


def more_body(slot_ref, item_ref, value_ref, out_ref):
    fill_all(slot_ref, item_ref, value_ref, out_ref, 0.0)


def more_slots(slots, items, values, owners, room):
    col = values.shape[1]
    return kernel_call(more_body, shape_of((owners, room + EXTRA, col), BF16), "more_slots")(slots, items, values)


def rows_total(blocks, first, count):
    room = blocks[0].shape[0] - EXTRA
    total = jnp.zeros((count, blocks[0].shape[1]), F32)
    row = lax.broadcasted_iota(jnp.int32, (count, room), 0) + first
    for pair in range(0, len(blocks), 2):
        hots, data = [], []
        for block in blocks[pair:pair + 2]:
            extra = block[pl.ds(room, EXTRA), :].astype(F32)
            item = ((extra[2:3] - 1.0) * 32.0 + extra[3:4]).astype(jnp.int32)
            hots.append(jnp.where(item == row, 1.0, 0.0).astype(BF16))
            data.append(block[pl.ds(0, room), :])
        total = total + jnp.dot(
            jnp.concatenate(hots, axis=1), jnp.concatenate(data, axis=0), preferred_element_type=F32
        )
    return total


def finish_body(got_ref, in_ref, out_ref, table_ref, gain_ref, rounds_ref):
    step = pl.program_id(0)
    count, col = table_ref.shape
    at = got_ref.shape[1] - BLOCK - EXTRA
    share = at // 5
    lasts = []
    for index in range(4):
        owner = step * 4 + index
        for c in range(4):
            in_ref[c, pl.ds(index * share, share), :] = got_ref[owner, pl.ds(c * share, share), :].astype(F32)
        lasts.append(got_ref[owner, pl.ds(4 * share, share), :].astype(F32))
    out_ref[...] = jnp.concatenate(lasts, axis=0).T
    blocks = [got_ref.at[index, pl.ds(at, BLOCK + EXTRA)] for index in range(got_ref.shape[0])]
    table_ref[...] = rows_total(blocks, step * count, count)
    extra = [block[pl.ds(BLOCK, EXTRA), :].astype(F32) for block in blocks]
    total = functools.reduce(lambda a, b: a + b, extra)
    gain_ref[...] = total[0:1] + total[1:2]
    rounds_ref[0] = jnp.max(functools.reduce(jnp.maximum, extra)[4:5]).astype(jnp.int32)


def finish(got, items):
    owners, _, col = got.shape
    width = 8 * col
    steps = owners // 4
    return kernel_call(
        finish_body,
        (
            shape_of((4, width, col), F32),
            shape_of((col, width), F32),
            shape_of((items, col), F32),
            shape_of((1, col), F32),
            shape_of((1,), jnp.int32),
        ),
        "finish",
        grid=(steps,),
        in_specs=[pl.BlockSpec(got.shape, lambda i: (0, 0, 0))],
        out_specs=[
            pl.BlockSpec((4, width // steps, col), lambda i: (0, i, 0)),
            pl.BlockSpec((col, width // steps), lambda i: (0, i)),
            pl.BlockSpec((items // steps, col), lambda i: (i, 0)),
            pl.BlockSpec((1, col), lambda i: (0, 0)),
            pl.BlockSpec(memory_space=pltpu.SMEM),
        ],
    )(got)


def more_table_body(got_ref, table_ref, out_ref):
    count = 2 * BLOCK
    blocks = [got_ref.at[index] for index in range(got_ref.shape[0])]
    for first in range(0, table_ref.shape[0], count):
        rows = pl.ds(first, count)
        out_ref[rows, :] = table_ref[rows, :] + rows_total(blocks, first, count)


def more_table(got, table):
    return kernel_call(more_table_body, shape_of(table.shape, F32), "more_table")(got, table)


def per_device(inputs, cotangent, norm_gain, proj_in, proj_out, item_ids, lengths, tile_mask):
    x_rows, cot_rows = inputs[0], cotangent[0]
    length, mask = lengths[0], tile_mask[0]
    tok, width = x_rows.shape
    col = proj_in.shape[2]
    scale = 1.0 / math.sqrt(col)
    tiles = tok // BLOCK
    seq, cols = lax.axis_index("seq"), lax.axis_index("col")
    z_hi, x_pos = seq // 4, seq % 4

    own, cross, near1, near2, near3, pre, normed, grad, dmix, upd, inv_cnt, inv_rms = project(
        lengths, x_rows, cot_rows, norm_gain, proj_in, proj_out, mask
    )

    across = move_seq(cross, 1, 0)
    near = [move_seq(block, 0, k) for block, k in ((near1, 1), (near3, 3), (near2, 2))]
    far = [move_seq(across, 0, k) for k in (1, 3, 2)]

    filled = (BLOCK * jnp.arange(mask.shape[0], dtype=jnp.int32) < length).astype(F32)
    kept = mask.astype(F32) * filled[None, :]
    as_query = lax.dynamic_slice_in_dim(kept, seq * tiles, tiles, 0)
    as_key = lax.dynamic_slice_in_dim(kept, seq * tiles, tiles, 1).T
    later = jnp.arange(mask.shape[0], dtype=jnp.int32) // tiles > seq
    keep = jnp.where(later[None, :], as_key, as_query)

    def keep_of(rows, rank):
        return jnp.repeat(lax.dynamic_slice_in_dim(rows, rank * tiles, tiles, 1), BLOCK, axis=1)

    def keep_side(dz):
        ranks = [(z_hi + dz) % 2 * 4 + (x_pos - k) % 4 for k in (1, 3, 2)]
        return [(rank > seq).astype(jnp.int32) for rank in ranks], [keep_of(keep, rank) for rank in ranks]

    cross_rank = (1 - z_hi) * 4 + x_pos
    near_side, near_keep = keep_side(0)
    far_side, far_keep = keep_side(1)
    near_side = jnp.stack([(cross_rank > seq).astype(jnp.int32)] + near_side)
    near_keep = jnp.stack([keep_of(keep, cross_rank)] + near_keep)
    far_side, far_keep = jnp.stack(far_side), jnp.stack(far_keep)
    keep_own = jnp.stack([keep_of(as_query, seq), keep_of(as_key, seq)])

    owners, items, room = 16, 1024, BLOCK
    ids = item_ids[0]
    owner = ids // items
    order = jnp.arange(tok, dtype=jnp.int32)
    ahead = (owner[:, None] == owner[None, :]) & (order[:, None] < order[None, :])
    rank = jnp.sum(ahead.astype(jnp.int32), axis=0)
    rounds_here = rank // room + 1
    offset = ids % items
    nothing = jnp.zeros_like(ids)
    rows = [nothing, nothing, offset // 32 + 1, offset % 32, nothing, rounds_here] + [nothing] * (EXTRA - 6)
    item_rows = jnp.stack(rows).astype(BF16)

    def slots_of(turn):
        place = rank - turn * room
        return jnp.where((place >= 0) & (place < room), owner * room + place, -1).reshape(1, tok)

    slots = slots_of(0)

    normed, grad, proj_now, x_now, inv_rms_now, across = lax.optimization_barrier(
        (normed, grad, proj_in, x_rows, inv_rms, across)
    )
    normed_t, grad_t, w_own, w_peer, x_cols, grad_cols = prepare(
        cols.reshape(1).astype(jnp.int32), normed, grad, proj_now, x_now, inv_rms_now
    )
    w_peer = move_core(w_peer)
    gain_cols = lax.dynamic_slice_in_dim(norm_gain, cols * col, col)
    acc = near_terms(near_side, own, keep_own, near_keep, [across] + near, scale)
    far_side, far_keep, w_peer, slots, item_rows, gain_cols = lax.optimization_barrier(
        (far_side, far_keep, w_peer, slots, item_rows, gain_cols)
    )
    d_own, shares = far_terms(
        far_side, own, far_keep, far, acc, pre, inv_rms, dmix, upd, inv_cnt, normed_t, grad_t, owners, scale
    )
    d_peer = move_core(d_own)
    shares = swap_plane(shares)
    parts = back_project(d_own, d_peer, w_own, w_peer, col)
    parts = [parts[0]] + [move_y(parts[k], k) for k in (1, 3, 2)]

    d_inputs, blocks = input_grads(parts, x_cols, gain_cols, inv_rms, grad_cols, slots, item_rows, owners, room)
    grad_in_w, grad_out_w, table, gain, rounds = finish(swap_plane(join_sums(shares, blocks)), items)

    def another(state):
        turn, total = state
        got = swap_plane(more_slots(slots_of(turn), item_rows, d_inputs, owners, room))
        return turn + 1, more_table(got, total)

    _, table = lax.while_loop(lambda state: state[0] < rounds[0], another, (jnp.int32(1), table))

    return (grad_in_w, grad_out_w, gain[0], table)


def solution(mesh):
    placed = (
        P("dp", "seq", None),
        P("dp", "seq", None),
        P(),
        P(None, None, "col"),
        P("col", None),
        P("dp", "seq"),
        P("dp"),
        P("dp", None, None),
    )
    return jax.shard_map(
        per_device,
        mesh=mesh,
        in_specs=placed,
        out_specs=(P(None, None, "col"), P("col", None), P("col"), P(("dp", "seq"), "col")),
        check_vma=False,
    )
```

profile of v0, /device:TPU:1, one launch (start us, length us, event | category | flops | bytes accessed | tf_op | source)
XLA Modules:
  0.0 112.8 jit_solution(2173768907903595066)
XLA Ops:
  1.3 5.0 %project.1 = (bf16[2,2,512,128]{3,2,1,0:T(8,128)(2,1)}, bf16[2,512,128]{2,1,0:T(8,128)(2,1)}, bf16[2,512,128]{2,1,0:T(8,128)(2,1)}, bf16[2,512,128]{2,1,0:T(8,12...) custom-call(s32[1]{0:T(128)} %copy.24.length_ref, ...), custom_call_target="tpu_custom_call" | custom-call | flops 1000 | bytes 1000 | tf_op jit(solution)/shard_map/project/pallas_call | solution.py:120
  6.3 4.5 %collective-permute-start = (bf16[2,512,128]{2,1,0:T(8,128)(2,1)}, bf16[2,512,128]{2,1,0:T(8,128)(2,1)S(1)}, u32[]{:S(2)}, u32[]{:S(2)}) collective-permute-start(bf16[2,512,128]{2,1,0:T(8,128)(2,1)} %get-tuple-element.88), channel_id=1, source_target_pairs={{0,32},{8,40},{16,48},{24,56},{32,0},{40,8},{48,16},{56,24},{1,33}... | collective-permute-start | bytes 786440 | tf_op jit(solution)/shard_map/ppermute | solution.py:42
  10.9 1.2 %collective-permute-start.5 = (bf16[2,512,128]{2,1,0:T(8,128)(2,1)}, bf16[2,512,128]{2,1,0:T(8,128)(2,1)}, u32[]{:S(2)}, u32[]{:S(2)}) collective-permute-start(bf16[2,512,128]{2,1,0:T(8,128)(2,1)} %get-tuple-element.99), channel_id=1, source_target_pairs={{0,8},{8,16},{16,24},{24,0},{32,40},{40,48},{48,56},{56,32},{1,9},... | collective-permute-start | bytes 786440 | tf_op jit(solution)/shard_map/ppermute | solution.py:42
  12.1 1.5 %collective-permute-start.6 = (bf16[2,512,128]{2,1,0:T(8,128)(2,1)}, bf16[2,512,128]{2,1,0:T(8,128)(2,1)}, u32[]{:S(2)}, u32[]{:S(2)}) collective-permute-start(bf16[2,512,128]{2,1,0:T(8,128)(2,1)} %get-tuple-element.100), channel_id=1, source_target_pairs={{0,24},{8,0},{16,8},{24,16},{32,56},{40,32},{48,40},{56,48},{1,25}... | collective-permute-start | bytes 786440 | tf_op jit(solution)/shard_map/ppermute | solution.py:42
  13.5 1.5 %collective-permute-start.7 = (bf16[2,512,128]{2,1,0:T(8,128)(2,1)}, bf16[2,512,128]{2,1,0:T(8,128)(2,1)}, u32[]{:S(2)}, u32[]{:S(2)}) collective-permute-start(bf16[2,512,128]{2,1,0:T(8,128)(2,1)} %get-tuple-element.101), channel_id=1, source_target_pairs={{0,16},{8,24},{16,0},{24,8},{32,48},{40,56},{48,32},{56,40},{1,17}... | collective-permute-start | bytes 786440 | tf_op jit(solution)/shard_map/ppermute | solution.py:42
  15.1 0.1 constant_dynamic-slice_fusion.8
  15.2 0.1 dynamic-slice_bitcast_fusion
  15.3 0.1 dynamic_slice.42
  15.3 0.1 copy.16
  15.4 0.1 copy.15
  15.5 0.1 broadcast_in_dim.52
  15.6 0.1 broadcast_in_dim.51
  15.8 0.6 pad_maximum_fusion.2.keep_own_ref
  16.4 0.1 constant_dynamic-slice_fusion.3
  16.5 0.2 convert_reduce_fusion
  16.7 0.6 add_convert_fusion.2.side_ref
  17.3 4.9 %prepare.1 = (bf16[1024,512]{1,0:T(8,128)(2,1)}, bf16[1024,512]{1,0:T(8,128)(2,1)}, bf16[512,512]{1,0:T(8,128)(2,1)}, bf16[512,512]{1,0:T(8,128)(2,1)}, f32[512,128]{1,0:T(8,128)}, /*index=5*/f32[512,128]{1,0:T(8,128)}) custom-call(s32[1]{0:T(128)} %bitcast.8.place_ref, bf16[512,1024]{1,0:T(8,128)(2,1)} %get-tuple-element.89.normed_ref, ...), custom_call_target="tpu_custom_call" | custom-call | flops 1000 | bytes 1000 | tf_op jit(solution)/shard_map/prepare/pallas_call | solution.py:412
  22.2 1.9 %collective-permute-start.1 = (bf16[512,512]{1,0:T(8,128)(2,1)}, bf16[512,512]{1,0:T(8,128)(2,1)S(1)}, u32[]{:S(2)}, u32[]{:S(2)}) collective-permute-start(bf16[512,512]{1,0:T(8,128)(2,1)} %get-tuple-element.94), channel_id=1, source_target_pairs={{0,1},{1,0},{2,3},{3,2},{4,5},{5,4},{6,7},{7,6},{8,9},{9,8},{10,11... | collective-permute-start | bytes 1572872 | tf_op jit(solution)/shard_map/ppermute | solution.py:50
  24.1 0.5 collective-permute-start.2
  24.6 2.2 %collective-permute-start.3 = (bf16[2,512,128]{2,1,0:T(8,128)(2,1)S(1)}, bf16[2,512,128]{2,1,0:T(8,128)(2,1)}, u32[]{:S(2)}, u32[]{:S(2)}) collective-permute-start(bf16[2,512,128]{2,1,0:T(8,128)(2,1)S(1)} %collective-permute-done.refs_0_), channel_id=1, source_target_pairs={{0,24},{8,0},{16,8},{24,16},{32,56},{40,32},{48,40},{56,48},{1,25}... | collective-permute-start | bytes 786440 | tf_op jit(solution)/shard_map/ppermute | solution.py:42
  26.9 0.8 collective-permute-start.4
  27.7 0.6 add_convert_fusion.3.side_ref
  28.3 0.1 broadcast_in_dim.53
  28.9 0.8 dynamic_slice.41
  29.7 0.6 pad_maximum_fusion.1.refs_1_
  30.3 0.6 pad_maximum_fusion.keep_ref
  30.9 6.5 %near_terms.1.refs_5_ = f32[2,2,512,128]{3,2,1,0:T(8,128)} custom-call(s32[4]{0:T(128)} %add_convert_fusion.3.side_ref, bf16[2,2,512,128]{3,2,1,0:T(8,128)(2,1)} %get-tuple-element.96.own_ref.refs_0_, f32[2,4,512]{2,1,0:T(4,128)} %pad_maximum_fusion.2.keep_own_ref, f32[4,4,512]{2,1,0:T(4,128)} %pad_maximum_fusion.keep_ref, bf16[2,512,128]{2,1,0:T(8,128)(2,1)} %copy-done.7, ...), custom_call_target="tpu_custom_call" | custom-call | flops 1000 | bytes 1000 | tf_op jit(solution)/shard_map/near_terms/pallas_call | solution.py:221
  37.4 1.8 %collective-permute-done.4.refs_4_ = bf16[2,512,128]{2,1,0:T(8,128)(2,1)} collective-permute-done((bf16[2,512,128]{2,1,0:T(8,128)(2,1)S(1)}, bf16[2,512,128]{2,1,0:T(8,128)(2,1)}, u32[]{:S(2)}, u32[]{:S(2)}) %collective-permute-start.4) | collective-permute-done | bytes 262176 | tf_op jit(solution)/shard_map/ppermute | solution.py:42
  39.3 7.2 %far_terms.1 = (bf16[528,512]{1,0:T(8,128)(2,1)}, bf16[16,320,128]{2,1,0:T(8,128)(2,1)}) custom-call(s32[3]{0:T(128)} %add_convert_fusion.2.side_ref, bf16[2,2,512,128]{3,2,1,0:T(8,128)(2,1)} %get-tuple-element.96.own_ref.refs_0_, f32[3,4,512]{2,1,0:T(4,128)} %pad_maximum_fusion.1.refs_1_, bf16[2,512,128]{2,1,0:T(8,128)(2,1)} %collective-permute-done.2.refs_2_, ...), custom_call_target="tpu_custom_call" | custom-call | flops 1000 | bytes 1000 | tf_op jit(solution)/shard_map/far_terms/pallas_call | solution.py:264
  46.5 5.5 %all-to-all-start.1 = ((bf16[16,320,128]{2,1,0:T(8,128)(2,1)}), bf16[16,320,128]{2,1,0:T(8,128)(2,1)S(1)}, u32[]{:S(2)}, u32[]{:S(2)}) async-start(bf16[16,320,128]{2,1,0:T(8,128)(2,1)} %get-tuple-element.108), calls=%async_computation.1 | async-start | bytes 2621440 | tf_op jit(solution)/shard_map/all_to_all | solution.py:37
  52.0 1.7 %collective-permute-start.8 = (bf16[528,512]{1,0:T(8,128)(2,1)S(1)}, bf16[528,512]{1,0:T(8,128)(2,1)S(1)}, u32[]{:S(2)}, u32[]{:S(2)}) collective-permute-start(bf16[528,512]{1,0:T(8,128)(2,1)S(1)} %copy-done.2), channel_id=1, source_target_pairs={{0,1},{1,0},{2,3},{3,2},{4,5},{5,4},{6,7},{7,6},{8,9},{9,8},{10,11... | collective-permute-start | bytes 1622024 | tf_op jit(solution)/shard_map/ppermute | solution.py:50
  53.8 1.6 %collective-permute-done.8.peer_ref = bf16[528,512]{1,0:T(8,128)(2,1)S(1)} collective-permute-done((bf16[528,512]{1,0:T(8,128)(2,1)S(1)}, bf16[528,512]{1,0:T(8,128)(2,1)S(1)}, u32[]{:S(2)}, u32[]{:S(2)}) %collective-permute-start.8) | collective-permute-done | bytes 540704 | tf_op jit(solution)/shard_map/ppermute | solution.py:50
  55.3 0.7 back_project.1
  56.1 2.8 %collective-permute-start.10 = (bf16[528,128]{1,0:T(8,128)(2,1)S(1)}, bf16[528,128]{1,0:T(8,128)(2,1)S(1)}, u32[]{:S(2)}, u32[]{:S(2)}) collective-permute-start(bf16[528,128]{1,0:T(8,128)(2,1)S(1)} %get-tuple-element.114), channel_id=1, source_target_pairs={{0,6},{1,7},{2,0},{3,1},{4,2},{5,3},{6,4},{7,5},{8,14},{9,15},{10,... | collective-permute-start | bytes 405512 | tf_op jit(solution)/shard_map/ppermute | solution.py:46
  58.9 0.3 collective-permute-start.11
  59.2 0.7 collective-permute-start.9
  59.9 4.3 %collective-permute-done.10.refs_2_ = bf16[528,128]{1,0:T(8,128)(2,1)S(1)} collective-permute-done((bf16[528,128]{1,0:T(8,128)(2,1)S(1)}, bf16[528,128]{1,0:T(8,128)(2,1)S(1)}, u32[]{:S(2)}, u32[]{:S(2)}) %collective-permute-start.10) | collective-permute-done | bytes 135200 | tf_op jit(solution)/shard_map/ppermute | solution.py:46
  64.2 0.7 collective-permute-done.11.refs_3_
  64.9 3.9 %collective-permute-done.9.refs_1_ = bf16[528,128]{1,0:T(8,128)(2,1)S(1)} collective-permute-done((bf16[528,128]{1,0:T(8,128)(2,1)S(1)}, bf16[528,128]{1,0:T(8,128)(2,1)S(1)}, u32[]{:S(2)}, u32[]{:S(2)}) %collective-permute-start.9) | collective-permute-done | bytes 135200 | tf_op jit(solution)/shard_map/ppermute | solution.py:46
  68.8 1.5 %input_grads.1 = (bf16[512,128]{1,0:T(8,128)(2,1)S(1)}, bf16[16,144,128]{2,1,0:T(8,128)(2,1)S(1)}) custom-call(bf16[528,128]{1,0:T(8,128)(2,1)S(1)} %get-tuple-element.112.refs_0_, bf16[528,128]{1,0:T(8,128)(2,1)S(1)} %collective-permute-done.9.refs_1_, bf16[528,128]{1,0:T(8,128)(2,1)S(1)} %collective-permute-done.10.refs_2_, ...), custom_call_target="tpu_custom_call" | custom-call | flops 1000 | bytes 1000 | tf_op jit(solution)/shard_map/input_grads/pallas_call | solution.py:496
  70.3 0.9 all-to-all-done.1.parts_ref
  71.2 0.4 join_sums.1
  71.7 1.2 %copy-done = bf16[16,464,128]{2,1,0:T(8,128)(2,1)} copy-done((bf16[16,464,128]{2,1,0:T(8,128)(2,1)}, bf16[16,464,128]{2,1,0:T(8,128)(2,1)S(1)}, u32[]{:S(2)}) %copy-start) | copy-done | bytes 1900568
  72.9 6.1 %all-to-all-start.2 = ((bf16[16,464,128]{2,1,0:T(8,128)(2,1)}), bf16[16,464,128]{2,1,0:T(8,128)(2,1)S(1)}, u32[]{:S(2)}, u32[]{:S(2)}) async-start(bf16[16,464,128]{2,1,0:T(8,128)(2,1)} %copy-done), calls=%async_computation.2 | async-start | bytes 3801088 | tf_op jit(solution)/shard_map/all_to_all | solution.py:37
  79.0 29.2 %all-to-all-done.2.got_ref = bf16[16,464,128]{2,1,0:T(8,128)(2,1)S(1)} async-done(((bf16[16,464,128]{2,1,0:T(8,128)(2,1)}), bf16[16,464,128]{2,1,0:T(8,128)(2,1)S(1)}, u32[]{:S(2)}, u32[]{:S(2)}) %all-to-all-start.2) | async-done | bytes 1900576 | tf_op jit(solution)/shard_map/all_to_all | solution.py:37
  108.2 3.0 %finish.1 = (f32[4,1024,128]{2,1,0:T(8,128)}, f32[128,1024]{1,0:T(8,128)}, f32[1024,128]{1,0:T(8,128)S(1)}, f32[1,128]{1,0:T(1,128)}, s32[1]{0:T(128)}) custom-call(bf16[16,464,128]{2,1,0:T(8,128)(2,1)S(1)} %all-to-all-done.2.got_ref), custom_call_target="tpu_custom_call" | custom-call | flops 1000 | bytes 1000 | tf_op jit(solution)/shard_map/finish/pallas_call | solution.py:553
  111.2 0.9 while.10
  112.1 0.8 copy-done.6
  (52 shorter events, 0.8 us)
Async XLA Ops:
  0.6 14.4 %copy-start.8 = (s32[1,32,32]{2,1,0:T(8,128)S(1)}, s32[1,32,32]{2,1,0:T(8,128)}, u32[]{:S(2)}) copy-start(s32[1,32,32]{2,1,0:T(8,128)} %param.17) | copy-start | bytes 12292
  1.3 14.4 %copy-start.9 = (s32[1,512]{1,0:T(1,128)S(1)}, s32[1,512]{1,0:T(1,128)}, u32[]{:S(2)}) copy-start(s32[1,512]{1,0:T(1,128)} %param.15) | copy-start | bytes 6148
  6.3 11.0 %collective-permute-start = (bf16[2,512,128]{2,1,0:T(8,128)(2,1)}, bf16[2,512,128]{2,1,0:T(8,128)(2,1)S(1)}, u32[]{:S(2)}, u32[]{:S(2)}) collective-permute-start(bf16[2,512,128]{2,1,0:T(8,128)(2,1)} %get-tuple-element.88), channel_id=1, source_target_pairs={{0,32},{8,40},{16,48},{24,56},{32,0},{40,8},{48,16},{56,24},{1,33}... | collective-permute-start | bytes 786440 | tf_op jit(solution)/shard_map/ppermute | solution.py:42
  10.9 13.8 %collective-permute-start.5 = (bf16[2,512,128]{2,1,0:T(8,128)(2,1)}, bf16[2,512,128]{2,1,0:T(8,128)(2,1)}, u32[]{:S(2)}, u32[]{:S(2)}) collective-permute-start(bf16[2,512,128]{2,1,0:T(8,128)(2,1)} %get-tuple-element.99), channel_id=1, source_target_pairs={{0,8},{8,16},{16,24},{24,0},{32,40},{40,48},{48,56},{56,32},{1,9},... | collective-permute-start | bytes 786440 | tf_op jit(solution)/shard_map/ppermute | solution.py:42
  12.1 14.8 %collective-permute-start.6 = (bf16[2,512,128]{2,1,0:T(8,128)(2,1)}, bf16[2,512,128]{2,1,0:T(8,128)(2,1)}, u32[]{:S(2)}, u32[]{:S(2)}) collective-permute-start(bf16[2,512,128]{2,1,0:T(8,128)(2,1)} %get-tuple-element.100), channel_id=1, source_target_pairs={{0,24},{8,0},{16,8},{24,16},{32,56},{40,32},{48,40},{56,48},{1,25}... | collective-permute-start | bytes 786440 | tf_op jit(solution)/shard_map/ppermute | solution.py:42
  13.5 17.4 %collective-permute-start.7 = (bf16[2,512,128]{2,1,0:T(8,128)(2,1)}, bf16[2,512,128]{2,1,0:T(8,128)(2,1)}, u32[]{:S(2)}, u32[]{:S(2)}) collective-permute-start(bf16[2,512,128]{2,1,0:T(8,128)(2,1)} %get-tuple-element.101), channel_id=1, source_target_pairs={{0,16},{8,24},{16,0},{24,8},{32,48},{40,56},{48,32},{56,40},{1,17}... | collective-permute-start | bytes 786440 | tf_op jit(solution)/shard_map/ppermute | solution.py:42
  17.3 9.6 %copy-start.7 = (bf16[2,512,128]{2,1,0:T(8,128)(2,1)}, bf16[2,512,128]{2,1,0:T(8,128)(2,1)S(1)}, u32[]{:S(2)}) copy-start(bf16[2,512,128]{2,1,0:T(8,128)(2,1)S(1)} %collective-permute-done.refs_0_) | copy-start | bytes 786436
  22.2 15.2 %collective-permute-start.1 = (bf16[512,512]{1,0:T(8,128)(2,1)}, bf16[512,512]{1,0:T(8,128)(2,1)S(1)}, u32[]{:S(2)}, u32[]{:S(2)}) collective-permute-start(bf16[512,512]{1,0:T(8,128)(2,1)} %get-tuple-element.94), channel_id=1, source_target_pairs={{0,1},{1,0},{2,3},{3,2},{4,5},{5,4},{6,7},{7,6},{8,9},{9,8},{10,11... | collective-permute-start | bytes 1572872 | tf_op jit(solution)/shard_map/ppermute | solution.py:50
  24.1 13.3 %collective-permute-start.2 = (bf16[2,512,128]{2,1,0:T(8,128)(2,1)S(1)}, bf16[2,512,128]{2,1,0:T(8,128)(2,1)}, u32[]{:S(2)}, u32[]{:S(2)}) collective-permute-start(bf16[2,512,128]{2,1,0:T(8,128)(2,1)S(1)} %collective-permute-done.refs_0_), channel_id=1, source_target_pairs={{0,8},{8,16},{16,24},{24,0},{32,40},{40,48},{48,56},{56,32},{1,9},... | collective-permute-start | bytes 786440 | tf_op jit(solution)/shard_map/ppermute | solution.py:42
  24.6 12.8 %collective-permute-start.3 = (bf16[2,512,128]{2,1,0:T(8,128)(2,1)S(1)}, bf16[2,512,128]{2,1,0:T(8,128)(2,1)}, u32[]{:S(2)}, u32[]{:S(2)}) collective-permute-start(bf16[2,512,128]{2,1,0:T(8,128)(2,1)S(1)} %collective-permute-done.refs_0_), channel_id=1, source_target_pairs={{0,24},{8,0},{16,8},{24,16},{32,56},{40,32},{48,40},{56,48},{1,25}... | collective-permute-start | bytes 786440 | tf_op jit(solution)/shard_map/ppermute | solution.py:42
  26.9 12.4 %collective-permute-start.4 = (bf16[2,512,128]{2,1,0:T(8,128)(2,1)S(1)}, bf16[2,512,128]{2,1,0:T(8,128)(2,1)}, u32[]{:S(2)}, u32[]{:S(2)}) collective-permute-start(bf16[2,512,128]{2,1,0:T(8,128)(2,1)S(1)} %collective-permute-done.refs_0_), channel_id=1, source_target_pairs={{0,16},{8,24},{16,0},{24,8},{32,48},{40,56},{48,32},{56,40},{1,17}... | collective-permute-start | bytes 786440 | tf_op jit(solution)/shard_map/ppermute | solution.py:42
  46.5 5.6 %copy-start.2 = (bf16[528,512]{1,0:T(8,128)(2,1)S(1)}, bf16[528,512]{1,0:T(8,128)(2,1)}, u32[]{:S(2)}) copy-start(bf16[528,512]{1,0:T(8,128)(2,1)} %get-tuple-element.109.own_ref) | copy-start | bytes 1622020
  46.5 8.8 %copy-start.3 = (bf16[512,512]{1,0:T(8,128)(2,1)S(1)}, bf16[512,512]{1,0:T(8,128)(2,1)}, u32[]{:S(2)}) copy-start(bf16[512,512]{1,0:T(8,128)(2,1)} %get-tuple-element.110.w_own_ref) | copy-start | bytes 1572868
  46.5 22.3 %copy-start.1 = (f32[512,128]{1,0:T(8,128)S(1)}, f32[512,128]{1,0:T(8,128)}, u32[]{:S(2)}) copy-start(f32[512,128]{1,0:T(8,128)} %get-tuple-element.93.inv_rms_ref.refs_7_.refs_6_) | copy-start | bytes 786436
  46.5 22.3 %copy-start.4 = (f32[512,128]{1,0:T(8,128)S(1)}, f32[512,128]{1,0:T(8,128)}, u32[]{:S(2)}) copy-start(f32[512,128]{1,0:T(8,128)} %get-tuple-element.116.refs_4_) | copy-start | bytes 786436
  46.5 24.7 %all-to-all-start.1 = ((bf16[16,320,128]{2,1,0:T(8,128)(2,1)}), bf16[16,320,128]{2,1,0:T(8,128)(2,1)S(1)}, u32[]{:S(2)}, u32[]{:S(2)}) async-start(bf16[16,320,128]{2,1,0:T(8,128)(2,1)} %get-tuple-element.108), calls=%async_computation.1 | async-start | bytes 2621440 | tf_op jit(solution)/shard_map/all_to_all | solution.py:37
  52.0 16.8 %copy-start.5 = (f32[512,128]{1,0:T(8,128)S(1)}, f32[512,128]{1,0:T(8,128)}, u32[]{:S(2)}) copy-start(f32[512,128]{1,0:T(8,128)} %get-tuple-element.118.refs_7_) | copy-start | bytes 786436
  52.0 3.3 %collective-permute-start.8 = (bf16[528,512]{1,0:T(8,128)(2,1)S(1)}, bf16[528,512]{1,0:T(8,128)(2,1)S(1)}, u32[]{:S(2)}, u32[]{:S(2)}) collective-permute-start(bf16[528,512]{1,0:T(8,128)(2,1)S(1)} %copy-done.2), channel_id=1, source_target_pairs={{0,1},{1,0},{2,3},{3,2},{4,5},{5,4},{6,7},{7,6},{8,9},{9,8},{10,11... | collective-permute-start | bytes 1622024 | tf_op jit(solution)/shard_map/ppermute | solution.py:50
  56.1 8.2 %collective-permute-start.10 = (bf16[528,128]{1,0:T(8,128)(2,1)S(1)}, bf16[528,128]{1,0:T(8,128)(2,1)S(1)}, u32[]{:S(2)}, u32[]{:S(2)}) collective-permute-start(bf16[528,128]{1,0:T(8,128)(2,1)S(1)} %get-tuple-element.114), channel_id=1, source_target_pairs={{0,6},{1,7},{2,0},{3,1},{4,2},{5,3},{6,4},{7,5},{8,14},{9,15},{10,... | collective-permute-start | bytes 405512 | tf_op jit(solution)/shard_map/ppermute | solution.py:46
  58.9 6.0 %collective-permute-start.11 = (bf16[528,128]{1,0:T(8,128)(2,1)S(1)}, bf16[528,128]{1,0:T(8,128)(2,1)S(1)}, u32[]{:S(2)}, u32[]{:S(2)}) collective-permute-start(bf16[528,128]{1,0:T(8,128)(2,1)S(1)} %get-tuple-element.115), channel_id=1, source_target_pairs={{0,4},{1,5},{2,6},{3,7},{4,0},{5,1},{6,2},{7,3},{8,12},{9,13},{10,... | collective-permute-start | bytes 405512 | tf_op jit(solution)/shard_map/ppermute | solution.py:46
  59.2 9.6 %collective-permute-start.9 = (bf16[528,128]{1,0:T(8,128)(2,1)S(1)}, bf16[528,128]{1,0:T(8,128)(2,1)S(1)}, u32[]{:S(2)}, u32[]{:S(2)}) collective-permute-start(bf16[528,128]{1,0:T(8,128)(2,1)S(1)} %get-tuple-element.113), channel_id=1, source_target_pairs={{0,2},{1,3},{2,4},{3,5},{4,6},{5,7},{6,0},{7,1},{8,10},{9,11},{10,... | collective-permute-start | bytes 405512 | tf_op jit(solution)/shard_map/ppermute | solution.py:46
  71.6 1.3 %copy-start = (bf16[16,464,128]{2,1,0:T(8,128)(2,1)}, bf16[16,464,128]{2,1,0:T(8,128)(2,1)S(1)}, u32[]{:S(2)}) copy-start(bf16[16,464,128]{2,1,0:T(8,128)(2,1)S(1)} %join_sums.1) | copy-start | bytes 5701636
  72.9 35.3 %all-to-all-start.2 = ((bf16[16,464,128]{2,1,0:T(8,128)(2,1)}), bf16[16,464,128]{2,1,0:T(8,128)(2,1)S(1)}, u32[]{:S(2)}, u32[]{:S(2)}) async-start(bf16[16,464,128]{2,1,0:T(8,128)(2,1)} %copy-done), calls=%async_computation.2 | async-start | bytes 3801088 | tf_op jit(solution)/shard_map/all_to_all | solution.py:37
  112.0 0.8 copy-start.6
where the time goes:
time: 114 us; the launch traced here: 113 us
  waiting for transfers between devices  42.4 us (37%)
  starting transfers between devices  31.3 us (27%)
  Pallas kernels  29.3 us (26%)
  local copies, waits for them, and re-layouts  4.16 us (4%)
  other arithmetic  3.34 us (3%)
  between operations  1.56 us (1%)
    all_to_all x2, waiting for transfers between devices, swap_plane(): return lax.all_to_all(value, ('dp', 'seq'), 0, 0, tiled=True)  30.1 us
    ppermute x7, starting transfers between devices, move_seq(): return lax.ppermute(value, 'seq', pairs)  12.2 us
    all_to_all x2, starting transfers between devices, swap_plane(): return lax.all_to_all(value, ('dp', 'seq'), 0, 0, tiled=True)  11.6 us
    ppermute x3, waiting for transfers between devices, move_y(): lax.ppermute(value, 'col', [(i, (i // 2 + dy) % 4 * 2 + i % 2) for i in r...  8.86 us
    pallas_call x1, Pallas kernels, far_terms(): kernel_call(functools.partial(far_body, scale=scale), (shape_of((tok + EX...  7.19 us
    pallas_call x1, Pallas kernels, near_terms(): kernel_call(functools.partial(near_body, scale=scale), shape_of(own.shape...  6.47 us
    pallas_call x1, Pallas kernels, project(): kernel_call(project_body, (shape_of((2, 2, tok, col), BF16), *(shape_of((...  5.03 us
    pallas_call x1, Pallas kernels, prepare(): kernel_call(prepare_body, (shape_of((width, tok), BF16), shape_of((width,...  4.93 us
  transfers between devices with their start and end apart: 14, of which 7 were waited for; matrix products, arithmetic and copies ran while one was open for 5% of the time, Pallas kernels for 12%

commit v1 on v0

v1 whole, which is shorter than its diff:
```python
import functools
import math

import jax
import jax.numpy as jnp
from jax import lax
from jax.experimental import pallas as pl
from jax.experimental.pallas import tpu as pltpu
from jax.sharding import PartitionSpec as P

BLOCK = 128
EPSILON = 1e-06
BF16 = jnp.bfloat16
F32 = jnp.float32
MIB = 1024 * 1024
EXTRA = 16
NT = (((1,), (1,)), ((), ()))
TN = (((0,), (0,)), ((), ()))


def kernel_call(body, out_shape, name, flops=1000, bytes_accessed=1000, vmem=24, **kwargs):
    return pl.pallas_call(
        body,
        out_shape=out_shape,
        name=name,
        compiler_params=pltpu.CompilerParams(vmem_limit_bytes=vmem * MIB),
        cost_estimate=pl.CostEstimate(flops=flops, bytes_accessed=bytes_accessed, transcendentals=0),
        **kwargs,
    )


def shape_of(shape, dtype):
    return jax.ShapeDtypeStruct(shape, dtype)


def swap_plane(value):
    return lax.all_to_all(value, ("dp", "seq"), 0, 0, tiled=True)


def plane_rank(z, x):
    return (z % 2) * 8 + (z // 2) * 4 + x


def move_plane(value, dz, dx):
    pairs = []
    for z in range(4):
        for x in range(4):
            pairs.append((plane_rank(z, x), plane_rank((z + dz) % 4, (x + dx) % 4)))
    return lax.ppermute(value, ("dp", "seq"), pairs)


def move_seq(value, dz_hi, dx):
    pairs = [(i, ((i // 4 + dz_hi) % 2) * 4 + (i % 4 + dx) % 4) for i in range(8)]
    return lax.ppermute(value, "seq", pairs)


def move_y(value, dy):
    return lax.ppermute(value, "col", [(i, ((i // 2 + dy) % 4) * 2 + i % 2) for i in range(8)])


def move_core(value):
    return lax.ppermute(value, "col", [(i, i ^ 1) for i in range(8)])


def project_body(length_ref, x_ref, cot_ref, gain_ref, proj_ref, out_ref, mask_ref,
                 own_ref, cross_ref, near1_ref, near2_ref, near3_ref, pre_ref, dmix_ref, upd_ref, inv_cnt_ref, inv_rms_ref, both_ref):
    length, rank = length_ref[0], lax.axis_index("seq")
    step, col = dmix_ref.shape

    @pl.when(pl.program_id(0) == 0)
    def _():
        for c in range(4):
            both_ref[:, pl.ds(c * col, col)] = proj_ref[c]

    x = x_ref[...].astype(F32)
    inv_rms = lax.rsqrt(jnp.mean(x * x, axis=1, keepdims=True) + EPSILON)
    normed = (x * inv_rms * gain_ref[...]).astype(BF16)
    inv_rms_ref[...] = jnp.broadcast_to(inv_rms, inv_rms_ref.shape)
    pre = jnp.dot(normed, both_ref[...], preferred_element_type=F32)
    act = (pre * jax.nn.sigmoid(pre)).astype(BF16)
    for c in range(4):
        pre_ref[c] = pre[:, c * col:(c + 1) * col]
    tile = (rank * pl.num_programs(0) + pl.program_id(0)) * (step // BLOCK)
    local = lax.broadcasted_iota(jnp.int32, (step, 1), 0)
    position = tile * BLOCK + local
    grad = jnp.where(position < length, cot_ref[...].astype(F32), 0.0).astype(BF16)
    d_mixed = lax.dot_general(grad, out_ref[...], NT, preferred_element_type=F32)
    dmix_ref[...] = d_mixed
    update = act[:, :col]
    upd_ref[...] = update
    tiles = mask_ref.shape[0]
    rows = lax.broadcasted_iota(jnp.int32, (tiles, tiles), 0)
    cols = lax.broadcasted_iota(jnp.int32, (tiles, tiles), 1)
    filled = jnp.clip(length - BLOCK * cols, 0, BLOCK)
    counted = jnp.where(cols < rows, mask_ref[...] * filled, 0)
    earlier = jnp.zeros((step, 1), F32)
    for index in range(step // BLOCK):
        picked = jnp.where(rows == tile + index, counted, 0).astype(F32)
        total = jnp.sum(jnp.sum(picked, axis=1, keepdims=True), axis=0, keepdims=True)
        earlier = jnp.where(local // BLOCK == index, total, earlier)
    own_first = tile * BLOCK + local // BLOCK * BLOCK
    diagonal = jnp.minimum(local % BLOCK + 1, jnp.clip(length - own_first, 0, BLOCK)).astype(F32)
    inv_cnt = 1.0 / jnp.maximum(earlier + diagonal, 1.0)
    inv_cnt_ref[...] = jnp.broadcast_to(inv_cnt, inv_cnt_ref.shape)
    qd = (act[:, col:2 * col], (d_mixed * update.astype(F32) * inv_cnt).astype(BF16))
    kv = (act[:, 2 * col:3 * col], act[:, 3 * col:])
    for index in range(2):
        own_ref[0, index], own_ref[1, index] = qd[index], kv[index]
    x_pos = lax.rem(rank, 4)
    later = [rank < 4] + [x_pos + k < 4 for k in (1, 2, 3)]
    for ref, is_later in zip((cross_ref, near1_ref, near2_ref, near3_ref), later):

        @pl.when(is_later)
        def _():
            ref[0], ref[1] = kv

        @pl.when(jnp.logical_not(is_later))
        def _():
            ref[0], ref[1] = qd


def project(lengths, x, cot, gain, proj_in, proj_out, mask):
    tok, width = x.shape
    col = proj_in.shape[2]
    step = 2 * BLOCK
    row = lambda i, w: (i, 0)
    side = lambda i, w: (0, i, 0)
    pair = lambda i, w: (0, 0, i, 0)
    fixed2 = lambda i, w: (0, 0)
    return kernel_call(
        project_body,
        (
            shape_of((2, 2, tok, col), BF16),
            *(shape_of((2, tok, col), BF16) for _ in range(4)),
            shape_of((4, tok, col), F32),
            shape_of((tok, col), F32),
            shape_of((tok, col), BF16),
            shape_of((tok, col), F32),
            shape_of((tok, col), F32),
        ),
        "project",
        vmem=63,
        grid_spec=pltpu.PrefetchScalarGridSpec(
            num_scalar_prefetch=1,
            grid=(tok // step,),
            in_specs=[
                pl.BlockSpec((step, width), row),
                pl.BlockSpec((step, width), row),
                pl.BlockSpec((1, width), fixed2),
                pl.BlockSpec((4, width, col), lambda i, w: (0, 0, 0)),
                pl.BlockSpec((col, width), fixed2),
                pl.BlockSpec(mask.shape, fixed2),
            ],
            out_specs=[
                pl.BlockSpec((2, 2, step, col), pair),
                *(pl.BlockSpec((2, step, col), side) for _ in range(4)),
                pl.BlockSpec((4, step, col), side),
                pl.BlockSpec((step, col), row),
                pl.BlockSpec((step, col), row),
                pl.BlockSpec((step, col), row),
                pl.BlockSpec((step, col), row),
            ],
            scratch_shapes=[pltpu.VMEM((width, 4 * col), BF16)],
        ),
    )(lengths, x, cot, gain.reshape(1, -1), proj_in, proj_out, mask)


def block_terms(a1, a2, b1, b2, keep, scale):
    half = lax.dot_general(a1, b1, NT, preferred_element_type=F32) * (keep * (0.5 * scale))
    other = lax.dot_general(a2, b2, NT, preferred_element_type=F32) * keep
    tanh = jnp.tanh(half)
    twice = 1.0 + tanh
    probs = half * twice
    slope = (other * (twice + probs * (1.0 - tanh))).astype(BF16)
    first = jnp.dot(probs.astype(BF16), b2, preferred_element_type=F32)
    second = jnp.dot(slope, b1, preferred_element_type=F32)
    return first, second


def block_sums(side, own_ref, other, keep_of, scale):
    tok, col = own_ref.shape[2:]
    part = 2 * BLOCK
    first, second = jnp.zeros((tok, col), F32), jnp.zeros((tok, col), F32)
    for start in range(0, tok, part):
        span = pl.ds(start, part)
        terms = block_terms(
            own_ref[side, 0], own_ref[side, 1], other[0][span, :], other[1][span, :], keep_of(start, part), scale
        )
        first, second = first + terms[0], second + terms[1]
    return first, second


def kept_tiles(mask_ref, length_ref, rank, tiles):
    count = mask_ref.shape[0]
    row = lax.broadcasted_iota(jnp.int32, (count, count), 0)
    column = lax.broadcasted_iota(jnp.int32, (count, count), 1)
    kept = jnp.where(column * BLOCK < length_ref[0], mask_ref[...].astype(F32), 0.0).astype(BF16)
    own = jnp.where(row + rank * tiles == column, 1.0, 0.0).astype(BF16)
    as_query = jnp.dot(own, kept, preferred_element_type=F32)
    as_key = lax.dot_general(own, kept, NT, preferred_element_type=F32)
    return as_query.astype(BF16), as_key.astype(BF16)


def keep_rows(kept, other, tiles, tok):
    count = kept.shape[0]
    row = lax.broadcasted_iota(jnp.int32, (count, tok), 0)
    column = lax.broadcasted_iota(jnp.int32, (count, tok), 1)
    spread = jnp.where(row == other * tiles + column // BLOCK, 1.0, 0.0).astype(BF16)
    return jnp.dot(kept, spread, preferred_element_type=F32)[:tiles]


def far_sums(other, rank, kept, own_ref, other_ref, scale):
    tok = own_ref.shape[2]
    tiles = tok // BLOCK
    side = jnp.where(other > rank, 1, 0)
    rows = jnp.where(other > rank, kept[1].astype(F32), kept[0].astype(F32)).astype(BF16)
    keep = keep_rows(rows, other, tiles, tok)

    def keep_of(start, part):
        return by_tile(keep[:, start:start + part], tok)

    return side, block_sums(side, own_ref, (other_ref.at[0], other_ref.at[1]), keep_of, scale)


def rank_at(rank, dz, dx):
    return lax.rem(rank // 4 + dz, 2) * 4 + lax.rem(rank + 4 - dx, 4)


def by_tile(rows, tok):
    tiles, part = rows.shape
    return jnp.broadcast_to(rows[:, None, :], (tiles, tok // tiles, part)).reshape(tok, part)


def near_body(length_ref, own_ref, mask_ref, proj_own_ref, proj_peer_ref, *refs, scale):
    others, (acc_ref, w_own_ref, w_peer_ref, sems) = refs[:-4], refs[-4:]
    tok, col = own_ref.shape[2:]
    place = lax.axis_index("col")
    picks = []
    for proj_ref, w_ref in ((proj_own_ref, w_own_ref), (proj_peer_ref, w_peer_ref)):
        for k in range(4):
            first = (lax.rem(place // 2 + k, 4) * 2 + lax.rem(place, 2)) * col
            rows = pl.ds(pl.multiple_of(first, col), col)
            for c in range(4):
                spot = w_ref.at[pl.ds(k * col, col), pl.ds(c * col, col)]
                picks.append(pltpu.make_async_copy(proj_ref.at[c, rows], spot, sems.at[len(picks)]))
    for pick in picks:
        pick.start()
    tiles = tok // BLOCK
    rank = lax.axis_index("seq")
    kept = kept_tiles(mask_ref, length_ref, rank, tiles)
    for side in range(2):
        other = own_ref.at[1 - side, 0], own_ref.at[1 - side, 1]
        rows = keep_rows(kept[side], rank, tiles, tok)

        def keep_of(start, part):
            row = lax.broadcasted_iota(jnp.int32, (tok, part), 0)
            column = lax.broadcasted_iota(jnp.int32, (tok, part), 1) + start
            ordered = (column <= row) if side == 0 else (row <= column)
            return jnp.where(ordered, by_tile(rows[:, start:start + part], tok), 0.0)

        acc_ref[side, 0], acc_ref[side, 1] = block_sums(side, own_ref, other, keep_of, scale)
    places = [(1, 0), (0, 1), (0, 3), (0, 2)]
    for (dz, dx), other in zip(places, others):
        side, sums = far_sums(rank_at(rank, dz, dx), rank, kept, own_ref, other, scale)
        acc_ref[side, 0] += sums[0]
        acc_ref[side, 1] += sums[1]
    for pick in picks:
        pick.wait()


def near_terms(lengths, own, mask, proj_own, proj_peer, others, scale):
    whole, anywhere = pl.BlockSpec(memory_space=pltpu.VMEM), pl.BlockSpec(memory_space=pl.ANY)
    depth = 4 * proj_own.shape[2]
    return kernel_call(
        functools.partial(near_body, scale=scale),
        (shape_of(own.shape, F32), shape_of((depth, depth), BF16), shape_of((depth, depth), BF16)),
        "near_terms",
        vmem=63,
        in_specs=[pl.BlockSpec(memory_space=pltpu.SMEM)] + [whole] * 2 + [anywhere] * 2 + [whole] * len(others),
        out_specs=[whole] * 3,
        scratch_shapes=[pltpu.SemaphoreType.DMA((32,))],
    )(lengths, own, mask, proj_own, proj_peer, *others)


FAR_INPUTS = 13


def far_body(length_ref, *refs, scale):
    sources, d_out, parts_out = refs[:FAR_INPUTS], refs[FAR_INPUTS], refs[FAR_INPUTS + 1]
    held = refs[FAR_INPUTS + 2:2 * FAR_INPUTS + 2]
    mixed_ref, d_ref, parts_ref, sems, out_sems = refs[2 * FAR_INPUTS + 2:]
    copies = [pltpu.make_async_copy(source, place, sems.at[n]) for n, (source, place) in enumerate(zip(sources, held))]
    for copy in copies:
        copy.start()
    own_ref, mask_ref = held[:2]
    rank = lax.axis_index("seq")
    others, acc_ref = held[2:5], held[5]
    pre_ref, inv_rms_ref, dmix_ref, upd_ref, inv_cnt_ref, normed_t_ref, grad_t_ref = held[6:]
    copies[0].wait()
    copies[1].wait()
    kept = kept_tiles(mask_ref, length_ref, rank, own_ref.shape[2] // BLOCK)
    for index, (dx, other) in enumerate(zip((1, 3, 2), others)):
        copies[2 + index].wait()
        side, sums = far_sums(rank_at(rank, 1, dx), rank, kept, own_ref, other, scale)
        if index == 0:
            copies[5].wait()
        acc_ref[side, 0] += sums[0]
        acc_ref[side, 1] += sums[1]
    for copy in copies[6:11]:
        copy.wait()
    pre_grad_body(acc_ref, pre_ref, inv_rms_ref, dmix_ref, upd_ref, inv_cnt_ref, d_ref, mixed_ref, scale=scale)
    leaving = [pltpu.make_async_copy(d_ref, d_out, out_sems.at[0])]
    leaving[0].start()
    for copy in copies[11:]:
        copy.wait()
    half = parts_ref.shape[0] // 2
    for part in range(2):
        weight_body(part, normed_t_ref, grad_t_ref, d_ref, mixed_ref, parts_ref)
        owners = pl.ds(part * half, half)
        leaving.append(pltpu.make_async_copy(parts_ref.at[owners], parts_out.at[owners], out_sems.at[part + 1]))
        leaving[-1].start()
    for copy in leaving:
        copy.wait()


def far_terms(lengths, own, mask, others, acc, pre, inv_rms, dmix, upd, inv_cnt, normed_t, grad_t, owners, scale):
    _, _, tok, col = own.shape
    width = normed_t.shape[0]
    sources = (own, mask, *others, acc, pre, inv_rms, dmix, upd, inv_cnt, normed_t, grad_t)
    return kernel_call(
        functools.partial(far_body, scale=scale),
        (shape_of((tok + EXTRA, 4 * col), BF16), shape_of((owners, 5 * width // owners, col), BF16)),
        "far_terms",
        vmem=63,
        in_specs=[pl.BlockSpec(memory_space=pltpu.SMEM)] + [pl.BlockSpec(memory_space=pl.ANY)] * len(sources),
        out_specs=[pl.BlockSpec(memory_space=pl.ANY)] * 2,
        scratch_shapes=[
            *(pltpu.VMEM(source.shape, source.dtype) for source in sources),
            pltpu.VMEM((tok, col), BF16),
            pltpu.VMEM((tok + EXTRA, 4 * col), BF16),
            pltpu.VMEM((owners, 5 * width // owners, col), BF16),
            pltpu.SemaphoreType.DMA((len(sources),)),
            pltpu.SemaphoreType.DMA((3,)),
        ],
    )(lengths, *sources)


def pre_grad_body(acc_ref, pre_ref, inv_rms_ref, dmix_ref, upd_ref, inv_cnt_ref, d_ref, mixed_ref, *, scale):
    tok, col = dmix_ref.shape
    stat = jnp.zeros((tok, col), F32)
    attended = acc_ref[0, 0] * inv_cnt_ref[...]
    mixed_ref[...] = (attended * upd_ref[...].astype(F32)).astype(BF16)
    grads = (
        dmix_ref[...] * attended,
        acc_ref[0, 1] * (0.5 * scale),
        acc_ref[1, 1] * (0.5 * scale),
        acc_ref[1, 0],
    )
    for c in range(4):
        pre = pre_ref[c]
        sig = jax.nn.sigmoid(pre)
        d_pre = (grads[c] * (sig * (1.0 + pre * (1.0 - sig)))).astype(BF16)
        d_ref[pl.ds(0, tok), pl.ds(c * col, col)] = d_pre
        stat = stat + d_pre.astype(F32) * pre
    stat = stat / inv_rms_ref[...]
    high = stat.astype(BF16)
    low = (stat - high.astype(F32)).astype(BF16)
    ones = jnp.ones((8, col), BF16)
    sums = lax.dot_general(ones, high, NT, preferred_element_type=F32)
    sums = sums + lax.dot_general(ones, low, NT, preferred_element_type=F32)
    d_ref[pl.ds(tok, EXTRA), :] = two_rows(sums[0:1])


def two_rows(value):
    high = value.astype(BF16).astype(F32)
    low = value - high
    row = lax.broadcasted_iota(jnp.int32, (EXTRA, value.shape[1]), 0)
    both = jnp.where(row == 0, jnp.broadcast_to(high, row.shape), jnp.where(row == 1, jnp.broadcast_to(low, row.shape), 0.0))
    return both.astype(BF16)


def back_body(own_ref, peer_ref, w_own_ref, w_peer_ref, *outs):
    tok = own_ref.shape[0] - EXTRA
    part = lax.dot_general(own_ref[pl.ds(0, tok), :], w_own_ref[...], NT, preferred_element_type=F32)
    part = part + lax.dot_general(peer_ref[pl.ds(0, tok), :], w_peer_ref[...], NT, preferred_element_type=F32)
    sums = jnp.sum(
        own_ref[pl.ds(tok, EXTRA), :].astype(F32) + peer_ref[pl.ds(tok, EXTRA), :].astype(F32), axis=0, keepdims=True
    )
    high = sums.astype(BF16).astype(F32)
    low = sums - high
    col = outs[0].shape[1]
    row = lax.broadcasted_iota(jnp.int32, (EXTRA, col), 0)
    extra = jnp.zeros((EXTRA, col), F32)
    for tile in range(tok // BLOCK):
        span = slice(tile * BLOCK, (tile + 1) * BLOCK)
        extra = jnp.where(row == 4 * tile, jnp.broadcast_to(high[:, span], row.shape), extra)
        extra = jnp.where(row == 4 * tile + 1, jnp.broadcast_to(low[:, span], row.shape), extra)
    extra = extra.astype(BF16)
    for k, out in enumerate(outs):
        out[pl.ds(0, tok), :] = part[:, k * col:(k + 1) * col].astype(BF16)
        out[pl.ds(tok, EXTRA), :] = extra


def back_project(own, peer, w_own, w_peer, col):
    rows, depth = own.shape
    return kernel_call(
        back_body,
        tuple(shape_of((rows, col), BF16) for _ in range(4)),
        "back_project",
    )(own, peer, w_own, w_peer)


def weight_body(part, normed_t_ref, grad_t_ref, d_ref, mixed_ref, out_ref):
    tok, col = mixed_ref.shape
    owners, share = out_ref.shape[0], out_ref.shape[1] // 5
    half = owners // 2
    rows = pl.ds(part * half * share, half * share)
    value = jnp.dot(normed_t_ref[rows, :], d_ref[pl.ds(0, tok), :], preferred_element_type=F32)
    last = jnp.dot(grad_t_ref[rows, :], mixed_ref[...], preferred_element_type=F32)
    for c in range(5):
        piece = value[:, c * col:(c + 1) * col] if c < 4 else last
        out_ref[pl.ds(part * half, half), pl.ds(c * share, share), :] = piece.astype(BF16).reshape(half, share, col)


def weight_sum_body(parts_ref, out_ref):
    total = parts_ref[0].astype(F32)
    for index in range(1, parts_ref.shape[0]):
        total = total + parts_ref[index].astype(F32)
    out_ref[...] = jnp.broadcast_to(total.astype(BF16)[None], out_ref.shape)


def weight_sum(parts):
    return kernel_call(weight_sum_body, shape_of(parts.shape, BF16), "weight_sum")(parts)


def prepare_body(length_ref, x_ref, cot_ref, gain_ref, inv_rms_ref, normed_t_ref, grad_t_ref):
    step = x_ref.shape[0]
    normed = (x_ref[...].astype(F32) * inv_rms_ref[:, :1] * gain_ref[...]).astype(BF16)
    normed_t_ref[...] = normed.T
    first = (lax.axis_index("seq") * pl.num_programs(0) + pl.program_id(0)) * step
    valid = lax.broadcasted_iota(jnp.int32, (step, 1), 0) + first < length_ref[0]
    grad_t_ref[...] = jnp.where(valid, cot_ref[...].astype(F32), 0.0).astype(BF16).T


def prepare(lengths, x, cot, gain, inv_rms):
    tok, width = x.shape
    col = inv_rms.shape[1]
    step = tok // 4
    row = lambda i, n: (i, 0)
    column = lambda i, n: (0, i)
    return kernel_call(
        prepare_body,
        (shape_of((width, tok), BF16), shape_of((width, tok), BF16)),
        "prepare",
        vmem=63,
        grid_spec=pltpu.PrefetchScalarGridSpec(
            num_scalar_prefetch=1,
            grid=(4,),
            in_specs=[
                pl.BlockSpec((step, width), row),
                pl.BlockSpec((step, width), row),
                pl.BlockSpec((1, width), lambda i, n: (0, 0)),
                pl.BlockSpec((step, col), row),
            ],
            out_specs=[pl.BlockSpec((width, step), column), pl.BlockSpec((width, step), column)],
        ),
    )(lengths, x, cot, gain.reshape(1, -1), inv_rms)


def fill_slots(slot_ref, item_ref, value_ref, blocks, owners, extra):
    room = blocks[0].shape[0] - EXTRA
    tok = slot_ref.shape[1]
    group = 4
    local = lax.broadcasted_iota(jnp.int32, (room, tok), 0)
    for first in range(0, len(blocks), group):
        hots = [jnp.where(slot_ref[...] == local + owner * room, 1.0, 0.0) for owner in owners[first:first + group]]
        hot = jnp.concatenate(hots, axis=0).astype(BF16)
        moved = jnp.dot(hot, value_ref[...], preferred_element_type=F32).astype(BF16)
        items = lax.dot_general(item_ref[...], hot, NT, preferred_element_type=F32)
        for index in range(group):
            span = slice(index * room, (index + 1) * room)
            block = blocks[first + index]
            block[pl.ds(0, room), :] = moved[span]
            block[pl.ds(room, EXTRA), :] = (extra + items[:, span]).astype(BF16)


def fill_all(slot_ref, item_ref, value_ref, out_ref, extra):
    owners = list(range(out_ref.shape[0]))
    fill_slots(slot_ref, item_ref, value_ref, [out_ref.at[owner] for owner in owners], owners, extra)


def slots_for(id_ref, rank_ref, slot_ref, item_ref, items, room):
    tok = id_ref.shape[1]
    ids = id_ref[...]
    owner = ids // items
    offset = ids - owner * items
    across = jnp.broadcast_to(owner.astype(F32), (8, tok)).T[:, :1]
    before = lax.broadcasted_iota(jnp.int32, (tok, tok), 0) < lax.broadcasted_iota(jnp.int32, (tok, tok), 1)
    same = jnp.where(before & (across == owner.astype(F32)), 1.0, 0.0)
    rank = jnp.sum(same, axis=0, keepdims=True).astype(jnp.int32)
    rank_ref[...] = rank
    slot_ref[...] = jnp.where(rank < room, owner * room + rank, -1)
    high = offset // 32
    row = lax.broadcasted_iota(jnp.int32, item_ref.shape, 0)
    rows = jnp.zeros(item_ref.shape, F32)
    for index, value in ((2, high + 1), (3, offset - high * 32), (5, rank // room + 1)):
        rows = jnp.where(row == index, jnp.broadcast_to(value.astype(F32), rows.shape), rows)
    item_ref[...] = rows.astype(BF16)


def input_grad_body(length_ref, *refs, items):
    parts = refs[:4]
    x_any, cot_any, gain_any, inv_rms_ref, id_ref, value_ref = refs[4:10]
    outs, (rank_ref, item_ref) = refs[10:14], refs[14:16]
    x_bf_ref, cot_ref, gain_ref, x_ref, slot_ref, sems = refs[16:]
    tok, col = x_ref.shape
    room = outs[0].shape[1] - EXTRA
    mine = pl.ds(pl.multiple_of(lax.axis_index("col") * col, col), col)
    copies = [
        pltpu.make_async_copy(source.at[:, mine], place, sems.at[n])
        for n, (source, place) in enumerate(((x_any, x_bf_ref), (cot_any, cot_ref), (gain_any, gain_ref)))
    ]
    for copy in copies:
        copy.start()
    slots_for(id_ref, rank_ref, slot_ref, item_ref, items, room)
    for copy in copies:
        copy.wait()
    x_ref[...] = x_bf_ref[...].astype(F32) * inv_rms_ref[...]
    first = lax.axis_index("seq") * tok
    d_normed = parts[0][pl.ds(0, tok), :].astype(F32)
    for part in parts[1:]:
        d_normed = d_normed + part[pl.ds(0, tok), :].astype(F32)
    gain_sum = two_rows(jnp.sum(d_normed * x_ref[...], axis=0, keepdims=True)).astype(F32)
    extra = [part[pl.ds(tok, EXTRA), :] for part in parts]
    row = lax.broadcasted_iota(jnp.int32, (EXTRA, col), 0)
    for tile in range(tok // BLOCK):
        rows = pl.ds(tile * BLOCK, BLOCK)
        pick = jnp.where((row >= 4 * tile) & (row < 4 * tile + 4), 1.0, 0.0).astype(BF16)
        mean = jnp.zeros((BLOCK, col), F32)
        for piece in extra:
            mean = mean + lax.dot_general(piece, pick, TN, preferred_element_type=F32)
        inv = inv_rms_ref[rows, :]
        d_t = d_normed[tile * BLOCK:(tile + 1) * BLOCK]
        mean = mean * inv * (1.0 / (8 * col))
        valid = lax.broadcasted_iota(jnp.int32, (BLOCK, 1), 0) + (first + tile * BLOCK) < length_ref[0]
        grad = jnp.where(valid, cot_ref[rows, :].astype(F32), 0.0)
        value = inv * (d_t * gain_ref[...] - x_ref[rows, :] * mean) + grad
        value_ref[rows, :] = value.astype(BF16)
    rounds = jnp.max(item_ref[pl.ds(5, 1), :].astype(F32), axis=1, keepdims=True)
    seq = lax.axis_index("seq")
    z_pos, x_pos = seq // 4 * 2 + lax.axis_index("dp"), lax.rem(seq, 4)
    spots = [(dx, dz) for dx in range(4) for dz in range(4)]
    owners = [plane_rank(lax.rem(z_pos + dz, 4), lax.rem(x_pos + dx, 4)) for dx, dz in spots]
    places = [outs[dx].at[dz] for dx, dz in spots]
    fill_slots(slot_ref, item_ref, value_ref, places, owners, gain_sum + jnp.where(row == 4, rounds, 0.0))


def input_grads(lengths, parts, x, cot, gain, inv_rms, ids, items, room):
    tok, col = inv_rms.shape
    whole, anywhere = pl.BlockSpec(memory_space=pltpu.VMEM), pl.BlockSpec(memory_space=pl.ANY)
    return kernel_call(
        functools.partial(input_grad_body, items=items),
        (
            shape_of((tok, col), BF16),
            *(shape_of((4, room + EXTRA, col), BF16) for _ in range(4)),
            shape_of((1, tok), jnp.int32),
            shape_of((EXTRA, tok), BF16),
        ),
        "input_grads",
        in_specs=[pl.BlockSpec(memory_space=pltpu.SMEM)] + [whole] * 4 + [anywhere] * 3 + [whole] * 2,
        scratch_shapes=[
            pltpu.VMEM((tok, col), BF16),
            pltpu.VMEM((tok, col), BF16),
            pltpu.VMEM((1, col), F32),
            pltpu.VMEM((tok, col), F32),
            pltpu.VMEM((1, tok), jnp.int32),
            pltpu.SemaphoreType.DMA((3,)),
        ],
    )(lengths, *parts, x, cot, gain.reshape(1, -1), inv_rms, ids)


def more_body(slot_ref, item_ref, value_ref, out_ref):
    fill_all(slot_ref, item_ref, value_ref, out_ref, 0.0)


def more_slots(slots, items, values, owners, room):
    col = values.shape[1]
    return kernel_call(more_body, shape_of((owners, room + EXTRA, col), BF16), "more_slots", vmem=63)(slots, items, values)


def rows_total(blocks, first, count):
    room = blocks[0].shape[0] - EXTRA
    total = jnp.zeros((count, blocks[0].shape[1]), F32)
    row = lax.broadcasted_iota(jnp.int32, (count, room), 0) + first
    for pair in range(0, len(blocks), 2):
        hots, data = [], []
        for block in blocks[pair:pair + 2]:
            extra = block[pl.ds(room, EXTRA), :].astype(F32)
            item = ((extra[2:3] - 1.0) * 32.0 + extra[3:4]).astype(jnp.int32)
            hots.append(jnp.where(item == row, 1.0, 0.0).astype(BF16))
            data.append(block[pl.ds(0, room), :])
        total = total + jnp.dot(
            jnp.concatenate(hots, axis=1), jnp.concatenate(data, axis=0), preferred_element_type=F32
        )
    return total


def finish_body(*refs):
    gots, whole_ref, (in_ref, out_ref, table_out, gain_ref, rounds_ref, table_ref, sems) = refs[:4], refs[4], refs[5:]
    step = pl.program_id(0)
    count, (_, rows, col) = table_ref.shape[1], whole_ref.shape
    share = rows // 5
    lasts = []
    for index in range(whole_ref.shape[0]):
        for c in range(4):
            in_ref[c, pl.ds(index * share, share), :] = whole_ref[index, pl.ds(c * share, share), :].astype(F32)
        lasts.append(whole_ref[index, pl.ds(4 * share, share), :].astype(F32))
    out_ref[...] = jnp.concatenate(lasts, axis=0).T
    blocks = [got.at[index] for got in gots for index in range(got.shape[0])]
    table_ref[step] = rows_total(blocks, step * count, count)

    def leaving(index):
        return pltpu.make_async_copy(table_ref.at[index], table_out.at[pl.ds(index * count, count)], sems.at[index])

    leaving(step).start()
    extra = [block[pl.ds(BLOCK, EXTRA), :].astype(F32) for block in blocks]
    total = functools.reduce(lambda a, b: a + b, extra)
    gain_ref[...] = total[0:1] + total[1:2]
    rounds_ref[0] = jnp.max(functools.reduce(jnp.maximum, extra)[4:5]).astype(jnp.int32)

    @pl.when(step == pl.num_programs(0) - 1)
    def _():
        for index in range(table_ref.shape[0]):
            leaving(index).wait()


def finish(gots, whole, items):
    owners, rows, col = whole.shape
    width, steps = 8 * col, 4
    return kernel_call(
        finish_body,
        (
            shape_of((4, width, col), F32),
            shape_of((col, width), F32),
            shape_of((items, col), F32),
            shape_of((1, col), F32),
            shape_of((1,), jnp.int32),
        ),
        "finish",
        grid=(steps,),
        in_specs=[pl.BlockSpec(got.shape, lambda i: (0, 0, 0)) for got in gots]
        + [pl.BlockSpec((owners // steps, rows, col), lambda i: (i, 0, 0))],
        out_specs=[
            pl.BlockSpec((4, width // steps, col), lambda i: (0, i, 0)),
            pl.BlockSpec((col, width // steps), lambda i: (0, i)),
            pl.BlockSpec(memory_space=pltpu.HBM),
            pl.BlockSpec((1, col), lambda i: (0, 0)),
            pl.BlockSpec(memory_space=pltpu.SMEM),
        ],
        scratch_shapes=[pltpu.VMEM((steps, items // steps, col), F32), pltpu.SemaphoreType.DMA((steps,))],
    )(*gots, whole)


def more_table_body(got_ref, table_ref, out_ref):
    count = 2 * BLOCK
    blocks = [got_ref.at[index] for index in range(got_ref.shape[0])]
    for first in range(0, table_ref.shape[0], count):
        rows = pl.ds(first, count)
        out_ref[rows, :] = table_ref[rows, :] + rows_total(blocks, first, count)


def more_table(got, table):
    return kernel_call(more_table_body, shape_of(table.shape, F32), "more_table", vmem=63)(got, table)


def per_device(inputs, cotangent, norm_gain, proj_in, proj_out, item_ids, lengths, tile_mask):
    x_rows, cot_rows = inputs[0], cotangent[0]
    mask = tile_mask[0]
    tok = x_rows.shape[0]
    col = proj_in.shape[2]
    scale = 1.0 / math.sqrt(col)
    owners, items, room = 16, 1024, BLOCK
    seq = lax.axis_index("seq")
    own, cross, near1, near2, near3, pre, dmix, upd, inv_cnt, inv_rms = project(
        lengths, x_rows, cot_rows, norm_gain, proj_in, proj_out, mask
    )

    across = move_seq(cross, 1, 0)
    near = [move_seq(block, 0, k) for block, k in ((near1, 1), (near3, 3), (near2, 2))]
    far = [move_seq(across, 0, k) for k in (1, 3, 2)]

    proj_peer = move_core(proj_in)
    x_now, cot_now, across = lax.optimization_barrier((x_rows, cot_rows, across))
    normed_t, grad_t = prepare(lengths, x_now, cot_now, norm_gain, inv_rms)
    acc, w_own, w_peer = near_terms(lengths, own, mask, proj_in, proj_peer, [across] + near, scale)
    d_own, shares = far_terms(
        lengths, own, mask, far, acc, pre, inv_rms, dmix, upd, inv_cnt, normed_t, grad_t, owners, scale
    )
    d_peer = move_core(d_own)
    shares = swap_plane(shares)
    parts = back_project(d_own, d_peer, w_own, w_peer, col)
    parts = [parts[0]] + [move_y(parts[k], k) for k in (1, 3, 2)]

    d_inputs, *sends, rank, item_rows = input_grads(
        lengths, parts, x_rows, cot_rows, norm_gain, inv_rms, item_ids, items, room
    )
    line = [sends[0]] + [move_plane(sends[k], 0, k) for k in (1, 3, 2)]
    sends = [jnp.stack([block[k] for block in line]) for k in range(4)]
    gots = [sends[0]] + [move_plane(sends[k], k, 0) for k in (1, 3, 2)]
    grad_in_w, grad_out_w, table, gain, rounds = finish(gots, swap_plane(weight_sum(shares)), items)

    def another(state):
        turn, total = state
        at = rank - turn * room
        slots = jnp.where((at >= 0) & (at < room), item_ids // items * room + at, -1)
        got = swap_plane(more_slots(slots, item_rows, d_inputs, owners, room))
        return turn + 1, more_table(got, total)

    _, table = lax.while_loop(lambda state: state[0] < rounds[0], another, (jnp.int32(1), table))
    return (grad_in_w, grad_out_w, gain[0], table)


def solution(mesh):
    placed = (
        P("dp", "seq", None),
        P("dp", "seq", None),
        P(),
        P(None, None, "col"),
        P("col", None),
        P("dp", "seq"),
        P("dp"),
        P("dp", None, None),
    )
    return jax.shard_map(
        per_device,
        mesh=mesh,
        in_specs=placed,
        out_specs=(P(None, None, "col"), P("col", None), P("col"), P(("dp", "seq"), "col")),
        check_vma=False,
    )
```

time: 114 us -> 111 us (0.974)
  starting transfers between devices: 31.3 us -> 38.8 us
  waiting for transfers between devices: 42.4 us -> 36.3 us
  other arithmetic: 3.34 us -> 0.09 us
  local copies, waits for them, and re-layouts: 4.16 us -> 1.5 us
  Pallas kernels: 29.3 us -> 31 us
    all_to_all x2, waiting for transfers between devices: 30.1 us -> 0.01 us  [swap_plane(): return lax.all_to_all(value, ('dp', 'seq'), 0, 0, tiled=True)]
    ppermute x0 -> x6, waiting for transfers between devices: none -> 19.8 us  [move_plane(): return lax.ppermute(value, ('dp', 'seq'), pairs)]
    ppermute x0 -> x6, starting transfers between devices: none -> 9.22 us  [move_plane(): return lax.ppermute(value, ('dp', 'seq'), pairs)]
    ppermute x7, waiting for transfers between devices: 1.86 us -> 6.02 us  [move_seq(): return lax.ppermute(value, 'seq', pairs)]
    another operation x8 -> x4, other arithmetic: 3.14 us -> 0.09 us  [per_device(): sends = [jnp.stack([block[k] for block in line]) for k in range(4)]]
    pallas_call x3, Pallas kernels: 8.44 us -> 11.4 us  [the longest x1 8.17 us: near_terms(): kernel_call(functools.partial(near_body, scale=scale), (shape_of(own.shap...]
    all_to_all x2, starting transfers between devices: 11.6 us -> 9.59 us  [swap_plane(): return lax.all_to_all(value, ('dp', 'seq'), 0, 0, tiled=True)]
    dynamic_slice x6 -> x0, local copies, waits for them, and re-layouts: 1.18 us -> none  [the longest x1 0.77 us: per_device(): gain_cols = lax.dynamic_slice_in_dim(norm_gain, cols * col, col)]
  transfers between devices with their start and end apart: 14 -> 20, of which waited for: 7 -> 10; matrix products, arithmetic and copies ran while one was open for 5% -> 0% of each run, Pallas kernels for 12% -> 19%
where the time goes in v1:
time: 111 us; the launch traced here: 110 us
  starting transfers between devices  38.8 us (35%)
  waiting for transfers between devices  36.3 us (33%)
  Pallas kernels  31 us (28%)
  between operations  1.73 us (2%)
  local copies, waits for them, and re-layouts  1.5 us (1%)
    ppermute x6, waiting for transfers between devices, move_plane(): return lax.ppermute(value, ('dp', 'seq'), pairs)  19.8 us
    ppermute x7, starting transfers between devices, move_seq(): return lax.ppermute(value, 'seq', pairs)  11.5 us
    all_to_all x2, starting transfers between devices, swap_plane(): return lax.all_to_all(value, ('dp', 'seq'), 0, 0, tiled=True)  9.59 us
    ppermute x6, starting transfers between devices, move_plane(): return lax.ppermute(value, ('dp', 'seq'), pairs)  9.22 us
    ppermute x3, waiting for transfers between devices, move_y(): lax.ppermute(value, 'col', [(i, (i // 2 + dy) % 4 * 2 + i % 2) for i in r...  8.86 us
    pallas_call x1, Pallas kernels, near_terms(): kernel_call(functools.partial(near_body, scale=scale), (shape_of(own.shap...  8.17 us
    pallas_call x1, Pallas kernels, far_terms(): kernel_call(functools.partial(far_body, scale=scale), (shape_of((tok + EX...  6.36 us
    ppermute x7, waiting for transfers between devices, move_seq(): return lax.ppermute(value, 'seq', pairs)  6.02 us
  transfers between devices with their start and end apart: 20, of which 10 were waited for; matrix products, arithmetic and copies ran while one was open for 0% of the time, Pallas kernels for 19%

profile of v1, /device:TPU:1, one launch (start us, length us, event | category | flops | bytes accessed | tf_op | source)
XLA Modules:
  0.0 110.1 jit_solution(13917100137149458896)
XLA Ops:
  0.6 1.5 %collective-permute-start.4 = (bf16[4,1024,128]{2,1,0:T(8,128)(2,1)}, bf16[4,1024,128]{2,1,0:T(8,128)(2,1)}, u32[]{:S(2)}, u32[]{:S(2)}) collective-permute-start(bf16[4,1024,128]{2,1,0:T(8,128)(2,1)} %proj_own_ref.1), channel_id=1, source_target_pairs={{0,1},{1,0},{2,3},{3,2},{4,5},{5,4},{6,7},{7,6},{8,9},{9,8},{10,11... | collective-permute-start | bytes 3145736 | tf_op jit(solution)/shard_map/ppermute | solution.py:62
  2.8 4.6 %project.1 = (bf16[2,2,512,128]{3,2,1,0:T(8,128)(2,1)}, bf16[2,512,128]{2,1,0:T(8,128)(2,1)}, bf16[2,512,128]{2,1,0:T(8,128)(2,1)}, bf16[2,512,128]{2,1,0:T(8,12...) custom-call(s32[1]{0:T(128)S(6)} %copy.19.length_ref, ...), custom_call_target="tpu_custom_call" | custom-call | flops 1000 | bytes 1000 | tf_op jit(solution)/shard_map/project/pallas_call | solution.py:130
  7.4 3.8 %collective-permute-start = (bf16[2,512,128]{2,1,0:T(8,128)(2,1)}, bf16[2,512,128]{2,1,0:T(8,128)(2,1)}, u32[]{:S(2)}, u32[]{:S(2)}) collective-permute-start(bf16[2,512,128]{2,1,0:T(8,128)(2,1)} %get-tuple-element.168), channel_id=1, source_target_pairs={{0,32},{8,40},{16,48},{24,56},{32,0},{40,8},{48,16},{56,24},{1,33}... | collective-permute-start | bytes 786440 | tf_op jit(solution)/shard_map/ppermute | solution.py:54
  11.1 1.2 %collective-permute-start.5 = (bf16[2,512,128]{2,1,0:T(8,128)(2,1)}, bf16[2,512,128]{2,1,0:T(8,128)(2,1)S(1)}, u32[]{:S(2)}, u32[]{:S(2)}) collective-permute-start(bf16[2,512,128]{2,1,0:T(8,128)(2,1)} %get-tuple-element.170), channel_id=1, source_target_pairs={{0,8},{8,16},{16,24},{24,0},{32,40},{40,48},{48,56},{56,32},{1,9},... | collective-permute-start | bytes 786440 | tf_op jit(solution)/shard_map/ppermute | solution.py:54
  12.3 1.5 %collective-permute-start.6 = (bf16[2,512,128]{2,1,0:T(8,128)(2,1)}, bf16[2,512,128]{2,1,0:T(8,128)(2,1)S(1)}, u32[]{:S(2)}, u32[]{:S(2)}) collective-permute-start(bf16[2,512,128]{2,1,0:T(8,128)(2,1)} %get-tuple-element.171), channel_id=1, source_target_pairs={{0,24},{8,0},{16,8},{24,16},{32,56},{40,32},{48,40},{56,48},{1,25}... | collective-permute-start | bytes 786440 | tf_op jit(solution)/shard_map/ppermute | solution.py:54
  13.8 1.5 %collective-permute-start.7 = (bf16[2,512,128]{2,1,0:T(8,128)(2,1)}, bf16[2,512,128]{2,1,0:T(8,128)(2,1)}, u32[]{:S(2)}, u32[]{:S(2)}) collective-permute-start(bf16[2,512,128]{2,1,0:T(8,128)(2,1)} %get-tuple-element.172), channel_id=1, source_target_pairs={{0,16},{8,24},{16,0},{24,8},{32,48},{40,56},{48,32},{56,40},{1,17}... | collective-permute-start | bytes 786440 | tf_op jit(solution)/shard_map/ppermute | solution.py:54
  15.3 2.8 %collective-permute-done.refs_0_ = bf16[2,512,128]{2,1,0:T(8,128)(2,1)} collective-permute-done((bf16[2,512,128]{2,1,0:T(8,128)(2,1)}, bf16[2,512,128]{2,1,0:T(8,128)(2,1)}, u32[]{:S(2)}, u32[]{:S(2)}) %collective-permute-start) | collective-permute-done | bytes 262176 | tf_op jit(solution)/shard_map/ppermute | solution.py:54
  18.1 1.2 %collective-permute-start.1 = (bf16[2,512,128]{2,1,0:T(8,128)(2,1)}, bf16[2,512,128]{2,1,0:T(8,128)(2,1)S(1)}, u32[]{:S(2)}, u32[]{:S(2)}) collective-permute-start(bf16[2,512,128]{2,1,0:T(8,128)(2,1)} %collective-permute-done.refs_0_), channel_id=1, source_target_pairs={{0,8},{8,16},{16,24},{24,0},{32,40},{40,48},{48,56},{56,32},{1,9},... | collective-permute-start | bytes 786440 | tf_op jit(solution)/shard_map/ppermute | solution.py:54
  19.3 0.8 collective-permute-done.5.refs_1_
  20.1 1.3 %collective-permute-start.2 = (bf16[2,512,128]{2,1,0:T(8,128)(2,1)}, bf16[2,512,128]{2,1,0:T(8,128)(2,1)S(1)}, u32[]{:S(2)}, u32[]{:S(2)}) collective-permute-start(bf16[2,512,128]{2,1,0:T(8,128)(2,1)} %collective-permute-done.refs_0_), channel_id=1, source_target_pairs={{0,24},{8,0},{16,8},{24,16},{32,56},{40,32},{48,40},{56,48},{1,25}... | collective-permute-start | bytes 786440 | tf_op jit(solution)/shard_map/ppermute | solution.py:54
  21.4 0.0 collective-permute-done.6.refs_2_
  21.4 0.7 copy-done.13
  22.1 1.1 collective-permute-start.3
  23.2 4.2 %prepare.1 = (bf16[1024,512]{1,0:T(8,128)(2,1)}, bf16[1024,512]{1,0:T(8,128)(2,1)}) custom-call(s32[1]{0:T(128)S(6)} %copy.19.length_ref, bf16[512,1024]{1,0:T(8,128)(2,1)} %bitcast.8, bf16[512,1024]{1,0:T(8,128)(2,1)} %bitcast.11, f32[1,1024]{1,0:T(1,128)} %bitcast.14, f32[512,128]{1,0:T(8,128)} %get-tuple-element.175.inv_rms_ref.refs_7_), custom_call_target="tpu_custom_call" | custom-call | flops 1000 | bytes 1000 | tf_op jit(solution)/shard_map/prepare/pallas_call | solution.py:451
  27.4 8.2 %near_terms.1 = (f32[2,2,512,128]{3,2,1,0:T(8,128)}, bf16[512,512]{1,0:T(8,128)(2,1)}, bf16[512,512]{1,0:T(8,128)(2,1)}) custom-call(s32[1]{0:T(128)S(6)} %copy.19.length_ref, bf16[2,2,512,128]{3,2,1,0:T(8,128)(2,1)} %get-tuple-element.167.own_ref.refs_0_, s32[32,32]{1,0:T(8,128)} %bitcast.17, bf16[4,1024,128]{2,1,0:T(8,128)(2,1)} %proj_own_ref.1, ...), custom_call_target="tpu_custom_call" | custom-call | flops 1000 | bytes 1000 | tf_op jit(solution)/shard_map/near_terms/pallas_call | solution.py:274
  35.6 0.0 collective-permute-done.1.refs_2_
  35.6 2.4 %collective-permute-done.3.refs_4_ = bf16[2,512,128]{2,1,0:T(8,128)(2,1)S(1)} collective-permute-done((bf16[2,512,128]{2,1,0:T(8,128)(2,1)}, bf16[2,512,128]{2,1,0:T(8,128)(2,1)S(1)}, u32[]{:S(2)}, u32[]{:S(2)}) %collective-permute-start.3) | collective-permute-done | bytes 262176 | tf_op jit(solution)/shard_map/ppermute | solution.py:54
  38.0 0.7 copy-done.11
  38.7 6.4 %far_terms.1 = (bf16[528,512]{1,0:T(8,128)(2,1)}, bf16[16,320,128]{2,1,0:T(8,128)(2,1)}) custom-call(s32[1]{0:T(128)S(6)} %copy.19.length_ref, bf16[2,2,512,128]{3,2,1,0:T(8,128)(2,1)} %get-tuple-element.167.own_ref.refs_0_, s32[32,32]{1,0:T(8,128)} %bitcast.18, bf16[2,512,128]{2,1,0:T(8,128)(2,1)} %copy-done.9, bf16[2,512,128]{2,1,0:T(8,128)(2,1)} %copy-done.10, ...), custom_call_target="tpu_custom_call" | custom-call | flops 1000 | bytes 1000 | tf_op jit(solution)/shard_map/far_terms/pallas_call | solution.py:330
  45.1 0.0 copy-start.4
  45.1 4.3 %all-to-all-start.1 = ((bf16[16,320,128]{2,1,0:T(8,128)(2,1)}), bf16[16,320,128]{2,1,0:T(8,128)(2,1)S(1)}, u32[]{:S(2)}, u32[]{:S(2)}) async-start(bf16[16,320,128]{2,1,0:T(8,128)(2,1)} %get-tuple-element.194), calls=%async_computation.1 | async-start | bytes 2621440 | tf_op jit(solution)/shard_map/all_to_all | solution.py:37
  49.4 0.0 copy-start
  49.5 0.0 copy-start.1
  49.5 0.0 copy-start.6
  49.5 0.0 copy-start.14
  49.5 3.1 %collective-permute-start.8 = (bf16[528,512]{1,0:T(8,128)(2,1)S(1)}, bf16[528,512]{1,0:T(8,128)(2,1)S(1)}, u32[]{:S(2)}, u32[]{:S(2)}) collective-permute-start(bf16[528,512]{1,0:T(8,128)(2,1)S(1)} %copy-done.3), channel_id=1, source_target_pairs={{0,1},{1,0},{2,3},{3,2},{4,5},{5,4},{6,7},{7,6},{8,9},{9,8},{10,11... | collective-permute-start | bytes 1622024 | tf_op jit(solution)/shard_map/ppermute | solution.py:62
  52.7 1.6 %collective-permute-done.8.peer_ref = bf16[528,512]{1,0:T(8,128)(2,1)S(1)} collective-permute-done((bf16[528,512]{1,0:T(8,128)(2,1)S(1)}, bf16[528,512]{1,0:T(8,128)(2,1)S(1)}, u32[]{:S(2)}, u32[]{:S(2)}) %collective-permute-start.8) | collective-permute-done | bytes 540704 | tf_op jit(solution)/shard_map/ppermute | solution.py:62
  54.2 0.7 back_project.1
  55.0 2.8 %collective-permute-start.10 = (bf16[528,128]{1,0:T(8,128)(2,1)S(1)}, bf16[528,128]{1,0:T(8,128)(2,1)S(1)}, u32[]{:S(2)}, u32[]{:S(2)}) collective-permute-start(bf16[528,128]{1,0:T(8,128)(2,1)S(1)} %get-tuple-element.188), channel_id=1, source_target_pairs={{0,6},{1,7},{2,0},{3,1},{4,2},{5,3},{6,4},{7,5},{8,14},{9,15},{10,... | collective-permute-start | bytes 405512 | tf_op jit(solution)/shard_map/ppermute | solution.py:58
  57.8 0.3 collective-permute-start.11
  58.1 0.7 collective-permute-start.9
  58.8 4.3 %collective-permute-done.10.refs_2_ = bf16[528,128]{1,0:T(8,128)(2,1)S(1)} collective-permute-done((bf16[528,128]{1,0:T(8,128)(2,1)S(1)}, bf16[528,128]{1,0:T(8,128)(2,1)S(1)}, u32[]{:S(2)}, u32[]{:S(2)}) %collective-permute-start.10) | collective-permute-done | bytes 135200 | tf_op jit(solution)/shard_map/ppermute | solution.py:58
  63.1 0.7 collective-permute-done.11.refs_3_
  63.8 3.9 %collective-permute-done.9.refs_1_ = bf16[528,128]{1,0:T(8,128)(2,1)S(1)} collective-permute-done((bf16[528,128]{1,0:T(8,128)(2,1)S(1)}, bf16[528,128]{1,0:T(8,128)(2,1)S(1)}, u32[]{:S(2)}, u32[]{:S(2)}) %collective-permute-start.9) | collective-permute-done | bytes 135200 | tf_op jit(solution)/shard_map/ppermute | solution.py:58
  67.7 2.0 %input_grads.1 = (bf16[512,128]{1,0:T(8,128)(2,1)S(1)}, bf16[4,144,128]{2,1,0:T(8,128)(2,1)S(1)}, bf16[4,144,128]{2,1,0:T(8,128)(2,1)S(1)}, bf16[4,144,128]{2,1,...) custom-call(s32[1]{0:T(128)S(6)} %copy.19.length_ref, ...), custom_call_target="tpu_custom_call" | custom-call | flops 1000 | bytes 1000 | tf_op jit(solution)/shard_map/input_grads/pallas_call | solution.py:561
  69.7 1.7 %collective-permute-start.12 = (bf16[4,144,128]{2,1,0:T(8,128)(2,1)S(1)}, bf16[4,144,128]{2,1,0:T(8,128)(2,1)S(1)}, u32[]{:S(2)}, u32[]{:S(2)}) collective-permute-start(bf16[4,144,128]{2,1,0:T(8,128)(2,1)S(1)} %get-tuple-element.191), channel_id=1, source_target_pairs={{0,8},{8,16},{16,24},{24,0},{64,72},{72,80},{80,88},{88,64},{32,40... | collective-permute-start | bytes 442376 | tf_op jit(solution)/shard_map/ppermute | solution.py:49
  71.4 1.3 %collective-permute-start.13 = (bf16[4,144,128]{2,1,0:T(8,128)(2,1)S(1)}, bf16[4,144,128]{2,1,0:T(8,128)(2,1)S(1)}, u32[]{:S(2)}, u32[]{:S(2)}) collective-permute-start(bf16[4,144,128]{2,1,0:T(8,128)(2,1)S(1)} %get-tuple-element.192), channel_id=1, source_target_pairs={{0,24},{8,0},{16,8},{24,16},{64,88},{72,64},{80,72},{88,80},{32,56... | collective-permute-start | bytes 442376 | tf_op jit(solution)/shard_map/ppermute | solution.py:49
  72.7 1.7 %collective-permute-start.14 = (bf16[4,144,128]{2,1,0:T(8,128)(2,1)S(1)}, bf16[4,144,128]{2,1,0:T(8,128)(2,1)S(1)}, u32[]{:S(2)}, u32[]{:S(2)}) collective-permute-start(bf16[4,144,128]{2,1,0:T(8,128)(2,1)S(1)} %get-tuple-element.193), channel_id=1, source_target_pairs={{0,16},{8,24},{16,0},{24,8},{64,80},{72,88},{80,64},{88,72},{32,48... | collective-permute-start | bytes 442376 | tf_op jit(solution)/shard_map/ppermute | solution.py:49
  74.4 1.3 %weight_sum.1 = bf16[16,320,128]{2,1,0:T(8,128)(2,1)} custom-call(bf16[16,320,128]{2,1,0:T(8,128)(2,1)S(1)} %all-to-all-done.1.parts_ref), custom_call_target="tpu_custom_call" | custom-call | flops 1000 | bytes 1000 | tf_op jit(solution)/shard_map/weight_sum/pallas_call | solution.py:433
  75.7 5.3 %all-to-all-start.2 = ((bf16[16,320,128]{2,1,0:T(8,128)(2,1)}), bf16[16,320,128]{2,1,0:T(8,128)(2,1)S(1)}, u32[]{:S(2)}, u32[]{:S(2)}) async-start(bf16[16,320,128]{2,1,0:T(8,128)(2,1)} %weight_sum.1), calls=%async_computation.2 | async-start | bytes 2621440 | tf_op jit(solution)/shard_map/all_to_all | solution.py:37
  81.1 2.9 %collective-permute-start.17 = (bf16[4,144,128]{2,1,0:T(8,128)(2,1)S(1)}, bf16[4,144,128]{2,1,0:T(8,128)(2,1)S(1)}, u32[]{:S(2)}, u32[]{:S(2)}) collective-permute-start(bf16[4,144,128]{2,1,0:T(8,128)(2,1)S(1)} %pad_maximum_fusion.3), channel_id=1, source_target_pairs={{0,32},{8,40},{16,48},{24,56},{64,96},{72,104},{80,112},{88,120},{... | collective-permute-start | bytes 442376 | tf_op jit(solution)/shard_map/ppermute | solution.py:49
  84.1 1.0 collective-permute-start.16
  85.0 0.6 collective-permute-start.15
  85.7 15.1 %collective-permute-done.17.refs_3_ = bf16[4,144,128]{2,1,0:T(8,128)(2,1)S(1)} collective-permute-done((bf16[4,144,128]{2,1,0:T(8,128)(2,1)S(1)}, bf16[4,144,128]{2,1,0:T(8,128)(2,1)S(1)}, u32[]{:S(2)}, u32[]{:S(2)}) %collective-permute-start.17) | collective-permute-done | bytes 147488 | tf_op jit(solution)/shard_map/ppermute | solution.py:49
  100.8 1.8 %collective-permute-done.16.refs_2_ = bf16[4,144,128]{2,1,0:T(8,128)(2,1)S(1)} collective-permute-done((bf16[4,144,128]{2,1,0:T(8,128)(2,1)S(1)}, bf16[4,144,128]{2,1,0:T(8,128)(2,1)S(1)}, u32[]{:S(2)}, u32[]{:S(2)}) %collective-permute-start.16) | collective-permute-done | bytes 147488 | tf_op jit(solution)/shard_map/ppermute | solution.py:49
  102.6 3.0 %collective-permute-done.15.refs_1_ = bf16[4,144,128]{2,1,0:T(8,128)(2,1)S(1)} collective-permute-done((bf16[4,144,128]{2,1,0:T(8,128)(2,1)S(1)}, bf16[4,144,128]{2,1,0:T(8,128)(2,1)S(1)}, u32[]{:S(2)}, u32[]{:S(2)}) %collective-permute-start.15) | collective-permute-done | bytes 147488 | tf_op jit(solution)/shard_map/ppermute | solution.py:49
  105.5 3.7 %finish.1 = (f32[4,1024,128]{2,1,0:T(8,128)}, f32[128,1024]{1,0:T(8,128)}, f32[1024,128]{1,0:T(8,128)}, f32[1,128]{1,0:T(1,128)}, s32[1]{0:T(128)}) custom-call(bf16[4,144,128]{2,1,0:T(8,128)(2,1)S(1)} %pad_maximum_fusion.refs_0_, bf16[4,144,128]{2,1,0:T(8,128)(2,1)S(1)} %collective-permute-done.15.refs_1_, ...), custom_call_target="tpu_custom_call" | custom-call | flops 1000 | bytes 1000 | tf_op jit(solution)/shard_map/finish/pallas_call | solution.py:640
  109.3 0.6 while.13
  (36 shorter events, 0.2 us)
Async XLA Ops:
  0.6 26.8 %collective-permute-start.4 = (bf16[4,1024,128]{2,1,0:T(8,128)(2,1)}, bf16[4,1024,128]{2,1,0:T(8,128)(2,1)}, u32[]{:S(2)}, u32[]{:S(2)}) collective-permute-start(bf16[4,1024,128]{2,1,0:T(8,128)(2,1)} %proj_own_ref.1), channel_id=1, source_target_pairs={{0,1},{1,0},{2,3},{3,2},{4,5},{5,4},{6,7},{7,6},{8,9},{9,8},{10,11... | collective-permute-start | bytes 3145736 | tf_op jit(solution)/shard_map/ppermute | solution.py:62
  7.4 10.7 %collective-permute-start = (bf16[2,512,128]{2,1,0:T(8,128)(2,1)}, bf16[2,512,128]{2,1,0:T(8,128)(2,1)}, u32[]{:S(2)}, u32[]{:S(2)}) collective-permute-start(bf16[2,512,128]{2,1,0:T(8,128)(2,1)} %get-tuple-element.168), channel_id=1, source_target_pairs={{0,32},{8,40},{16,48},{24,56},{32,0},{40,8},{48,16},{56,24},{1,33}... | collective-permute-start | bytes 786440 | tf_op jit(solution)/shard_map/ppermute | solution.py:54
  11.1 9.0 %collective-permute-start.5 = (bf16[2,512,128]{2,1,0:T(8,128)(2,1)}, bf16[2,512,128]{2,1,0:T(8,128)(2,1)S(1)}, u32[]{:S(2)}, u32[]{:S(2)}) collective-permute-start(bf16[2,512,128]{2,1,0:T(8,128)(2,1)} %get-tuple-element.170), channel_id=1, source_target_pairs={{0,8},{8,16},{16,24},{24,0},{32,40},{40,48},{48,56},{56,32},{1,9},... | collective-permute-start | bytes 786440 | tf_op jit(solution)/shard_map/ppermute | solution.py:54
  12.3 9.1 %collective-permute-start.6 = (bf16[2,512,128]{2,1,0:T(8,128)(2,1)}, bf16[2,512,128]{2,1,0:T(8,128)(2,1)S(1)}, u32[]{:S(2)}, u32[]{:S(2)}) collective-permute-start(bf16[2,512,128]{2,1,0:T(8,128)(2,1)} %get-tuple-element.171), channel_id=1, source_target_pairs={{0,24},{8,0},{16,8},{24,16},{32,56},{40,32},{48,40},{56,48},{1,25}... | collective-permute-start | bytes 786440 | tf_op jit(solution)/shard_map/ppermute | solution.py:54
  13.8 13.6 %collective-permute-start.7 = (bf16[2,512,128]{2,1,0:T(8,128)(2,1)}, bf16[2,512,128]{2,1,0:T(8,128)(2,1)}, u32[]{:S(2)}, u32[]{:S(2)}) collective-permute-start(bf16[2,512,128]{2,1,0:T(8,128)(2,1)} %get-tuple-element.172), channel_id=1, source_target_pairs={{0,16},{8,24},{16,0},{24,8},{32,48},{40,56},{48,32},{56,40},{1,17}... | collective-permute-start | bytes 786440 | tf_op jit(solution)/shard_map/ppermute | solution.py:54
  18.1 17.5 %collective-permute-start.1 = (bf16[2,512,128]{2,1,0:T(8,128)(2,1)}, bf16[2,512,128]{2,1,0:T(8,128)(2,1)S(1)}, u32[]{:S(2)}, u32[]{:S(2)}) collective-permute-start(bf16[2,512,128]{2,1,0:T(8,128)(2,1)} %collective-permute-done.refs_0_), channel_id=1, source_target_pairs={{0,8},{8,16},{16,24},{24,0},{32,40},{40,48},{48,56},{56,32},{1,9},... | collective-permute-start | bytes 786440 | tf_op jit(solution)/shard_map/ppermute | solution.py:54
  20.1 1.3 %copy-start.12 = (bf16[2,512,128]{2,1,0:T(8,128)(2,1)}, bf16[2,512,128]{2,1,0:T(8,128)(2,1)S(1)}, u32[]{:S(2)}) copy-start(bf16[2,512,128]{2,1,0:T(8,128)(2,1)S(1)} %collective-permute-done.5.refs_1_) | copy-start | bytes 786436
  20.1 15.4 %collective-permute-start.2 = (bf16[2,512,128]{2,1,0:T(8,128)(2,1)}, bf16[2,512,128]{2,1,0:T(8,128)(2,1)S(1)}, u32[]{:S(2)}, u32[]{:S(2)}) collective-permute-start(bf16[2,512,128]{2,1,0:T(8,128)(2,1)} %collective-permute-done.refs_0_), channel_id=1, source_target_pairs={{0,24},{8,0},{16,8},{24,16},{32,56},{40,32},{48,40},{56,48},{1,25}... | collective-permute-start | bytes 786440 | tf_op jit(solution)/shard_map/ppermute | solution.py:54
  21.4 0.7 copy-start.13
  22.1 15.9 %collective-permute-start.3 = (bf16[2,512,128]{2,1,0:T(8,128)(2,1)}, bf16[2,512,128]{2,1,0:T(8,128)(2,1)S(1)}, u32[]{:S(2)}, u32[]{:S(2)}) collective-permute-start(bf16[2,512,128]{2,1,0:T(8,128)(2,1)} %collective-permute-done.refs_0_), channel_id=1, source_target_pairs={{0,16},{8,24},{16,0},{24,8},{32,48},{40,56},{48,32},{56,40},{1,17}... | collective-permute-start | bytes 786440 | tf_op jit(solution)/shard_map/ppermute | solution.py:54
  35.6 2.5 %copy-start.9 = (bf16[2,512,128]{2,1,0:T(8,128)(2,1)}, bf16[2,512,128]{2,1,0:T(8,128)(2,1)S(1)}, u32[]{:S(2)}) copy-start(bf16[2,512,128]{2,1,0:T(8,128)(2,1)S(1)} %collective-permute-done.1.refs_2_) | copy-start | bytes 786436
  35.6 2.4 %copy-start.10 = (bf16[2,512,128]{2,1,0:T(8,128)(2,1)}, bf16[2,512,128]{2,1,0:T(8,128)(2,1)S(1)}, u32[]{:S(2)}) copy-start(bf16[2,512,128]{2,1,0:T(8,128)(2,1)S(1)} %collective-permute-done.2.refs_3_) | copy-start | bytes 786436
  38.0 0.7 copy-start.11
  45.1 4.4 %copy-start.3 = (bf16[528,512]{1,0:T(8,128)(2,1)S(1)}, bf16[528,512]{1,0:T(8,128)(2,1)}, u32[]{:S(2)}) copy-start(bf16[528,512]{1,0:T(8,128)(2,1)} %get-tuple-element.183.own_ref) | copy-start | bytes 1622020
  45.1 9.1 %copy-start.4 = (bf16[512,512]{1,0:T(8,128)(2,1)S(1)}, bf16[512,512]{1,0:T(8,128)(2,1)}, u32[]{:S(2)}) copy-start(bf16[512,512]{1,0:T(8,128)(2,1)} %get-tuple-element.184.w_own_ref) | copy-start | bytes 1572868
  45.1 9.1 %copy-start.5 = (bf16[512,512]{1,0:T(8,128)(2,1)S(1)}, bf16[512,512]{1,0:T(8,128)(2,1)}, u32[]{:S(2)}) copy-start(bf16[512,512]{1,0:T(8,128)(2,1)} %get-tuple-element.185.w_peer_ref) | copy-start | bytes 1572868
  45.1 22.5 %copy-start.2 = (f32[512,128]{1,0:T(8,128)S(1)}, f32[512,128]{1,0:T(8,128)}, u32[]{:S(2)}) copy-start(f32[512,128]{1,0:T(8,128)} %get-tuple-element.175.inv_rms_ref.refs_7_) | copy-start | bytes 786436
  45.1 29.3 %all-to-all-start.1 = ((bf16[16,320,128]{2,1,0:T(8,128)(2,1)}), bf16[16,320,128]{2,1,0:T(8,128)(2,1)S(1)}, u32[]{:S(2)}, u32[]{:S(2)}) async-start(bf16[16,320,128]{2,1,0:T(8,128)(2,1)} %get-tuple-element.194), calls=%async_computation.1 | async-start | bytes 2621440 | tf_op jit(solution)/shard_map/all_to_all | solution.py:37
  49.4 18.2 %copy-start = (bf16[1,512,1024]{2,1,0:T(8,128)(2,1)S(1)}, bf16[1,512,1024]{2,1,0:T(8,128)(2,1)}, u32[]{:S(2)}) copy-start(bf16[1,512,1024]{2,1,0:T(8,128)(2,1)} %param.10) | copy-start | bytes 3145732
  49.5 18.2 %copy-start.1 = (bf16[1,512,1024]{2,1,0:T(8,128)(2,1)S(1)}, bf16[1,512,1024]{2,1,0:T(8,128)(2,1)}, u32[]{:S(2)}) copy-start(bf16[1,512,1024]{2,1,0:T(8,128)(2,1)} %param.11) | copy-start | bytes 3145732
  49.5 18.2 %copy-start.6 = (f32[1024]{0:T(1024)S(1)}, f32[1024]{0:T(1024)}, u32[]{:S(2)}) copy-start(f32[1024]{0:T(1024)} %param.12) | copy-start | bytes 12292
  49.5 18.2 %copy-start.14 = (s32[1,512]{1,0:T(1,128)S(1)}, s32[1,512]{1,0:T(1,128)}, u32[]{:S(2)}) copy-start(s32[1,512]{1,0:T(1,128)} %refs_8_.1) | copy-start | bytes 6148
  49.5 4.7 %collective-permute-start.8 = (bf16[528,512]{1,0:T(8,128)(2,1)S(1)}, bf16[528,512]{1,0:T(8,128)(2,1)S(1)}, u32[]{:S(2)}, u32[]{:S(2)}) collective-permute-start(bf16[528,512]{1,0:T(8,128)(2,1)S(1)} %copy-done.3), channel_id=1, source_target_pairs={{0,1},{1,0},{2,3},{3,2},{4,5},{5,4},{6,7},{7,6},{8,9},{9,8},{10,11... | collective-permute-start | bytes 1622024 | tf_op jit(solution)/shard_map/ppermute | solution.py:62
  55.0 8.1 %collective-permute-start.10 = (bf16[528,128]{1,0:T(8,128)(2,1)S(1)}, bf16[528,128]{1,0:T(8,128)(2,1)S(1)}, u32[]{:S(2)}, u32[]{:S(2)}) collective-permute-start(bf16[528,128]{1,0:T(8,128)(2,1)S(1)} %get-tuple-element.188), channel_id=1, source_target_pairs={{0,6},{1,7},{2,0},{3,1},{4,2},{5,3},{6,4},{7,5},{8,14},{9,15},{10,... | collective-permute-start | bytes 405512 | tf_op jit(solution)/shard_map/ppermute | solution.py:58
  57.8 6.0 %collective-permute-start.11 = (bf16[528,128]{1,0:T(8,128)(2,1)S(1)}, bf16[528,128]{1,0:T(8,128)(2,1)S(1)}, u32[]{:S(2)}, u32[]{:S(2)}) collective-permute-start(bf16[528,128]{1,0:T(8,128)(2,1)S(1)} %get-tuple-element.189), channel_id=1, source_target_pairs={{0,4},{1,5},{2,6},{3,7},{4,0},{5,1},{6,2},{7,3},{8,12},{9,13},{10,... | collective-permute-start | bytes 405512 | tf_op jit(solution)/shard_map/ppermute | solution.py:58
  58.1 9.6 %collective-permute-start.9 = (bf16[528,128]{1,0:T(8,128)(2,1)S(1)}, bf16[528,128]{1,0:T(8,128)(2,1)S(1)}, u32[]{:S(2)}, u32[]{:S(2)}) collective-permute-start(bf16[528,128]{1,0:T(8,128)(2,1)S(1)} %get-tuple-element.187), channel_id=1, source_target_pairs={{0,2},{1,3},{2,4},{3,5},{4,6},{5,7},{6,0},{7,1},{8,10},{9,11},{10,... | collective-permute-start | bytes 405512 | tf_op jit(solution)/shard_map/ppermute | solution.py:58
  69.7 11.3 %collective-permute-start.12 = (bf16[4,144,128]{2,1,0:T(8,128)(2,1)S(1)}, bf16[4,144,128]{2,1,0:T(8,128)(2,1)S(1)}, u32[]{:S(2)}, u32[]{:S(2)}) collective-permute-start(bf16[4,144,128]{2,1,0:T(8,128)(2,1)S(1)} %get-tuple-element.191), channel_id=1, source_target_pairs={{0,8},{8,16},{16,24},{24,0},{64,72},{72,80},{80,88},{88,64},{32,40... | collective-permute-start | bytes 442376 | tf_op jit(solution)/shard_map/ppermute | solution.py:49
  71.4 9.6 %collective-permute-start.13 = (bf16[4,144,128]{2,1,0:T(8,128)(2,1)S(1)}, bf16[4,144,128]{2,1,0:T(8,128)(2,1)S(1)}, u32[]{:S(2)}, u32[]{:S(2)}) collective-permute-start(bf16[4,144,128]{2,1,0:T(8,128)(2,1)S(1)} %get-tuple-element.192), channel_id=1, source_target_pairs={{0,24},{8,0},{16,8},{24,16},{64,88},{72,64},{80,72},{88,80},{32,56... | collective-permute-start | bytes 442376 | tf_op jit(solution)/shard_map/ppermute | solution.py:49
  72.7 8.3 %collective-permute-start.14 = (bf16[4,144,128]{2,1,0:T(8,128)(2,1)S(1)}, bf16[4,144,128]{2,1,0:T(8,128)(2,1)S(1)}, u32[]{:S(2)}, u32[]{:S(2)}) collective-permute-start(bf16[4,144,128]{2,1,0:T(8,128)(2,1)S(1)} %get-tuple-element.193), channel_id=1, source_target_pairs={{0,16},{8,24},{16,0},{24,8},{64,80},{72,88},{80,64},{88,72},{32,48... | collective-permute-start | bytes 442376 | tf_op jit(solution)/shard_map/ppermute | solution.py:49
  75.7 29.9 %all-to-all-start.2 = ((bf16[16,320,128]{2,1,0:T(8,128)(2,1)}), bf16[16,320,128]{2,1,0:T(8,128)(2,1)S(1)}, u32[]{:S(2)}, u32[]{:S(2)}) async-start(bf16[16,320,128]{2,1,0:T(8,128)(2,1)} %weight_sum.1), calls=%async_computation.2 | async-start | bytes 2621440 | tf_op jit(solution)/shard_map/all_to_all | solution.py:37
  81.1 19.7 %collective-permute-start.17 = (bf16[4,144,128]{2,1,0:T(8,128)(2,1)S(1)}, bf16[4,144,128]{2,1,0:T(8,128)(2,1)S(1)}, u32[]{:S(2)}, u32[]{:S(2)}) collective-permute-start(bf16[4,144,128]{2,1,0:T(8,128)(2,1)S(1)} %pad_maximum_fusion.3), channel_id=1, source_target_pairs={{0,32},{8,40},{16,48},{24,56},{64,96},{72,104},{80,112},{88,120},{... | collective-permute-start | bytes 442376 | tf_op jit(solution)/shard_map/ppermute | solution.py:49
  84.1 18.5 %collective-permute-start.16 = (bf16[4,144,128]{2,1,0:T(8,128)(2,1)S(1)}, bf16[4,144,128]{2,1,0:T(8,128)(2,1)S(1)}, u32[]{:S(2)}, u32[]{:S(2)}) collective-permute-start(bf16[4,144,128]{2,1,0:T(8,128)(2,1)S(1)} %pad_maximum_fusion.2), channel_id=1, source_target_pairs={{0,96},{8,104},{16,112},{24,120},{64,0},{72,8},{80,16},{88,24},{32... | collective-permute-start | bytes 442376 | tf_op jit(solution)/shard_map/ppermute | solution.py:49
  85.0 20.5 %collective-permute-start.15 = (bf16[4,144,128]{2,1,0:T(8,128)(2,1)S(1)}, bf16[4,144,128]{2,1,0:T(8,128)(2,1)S(1)}, u32[]{:S(2)}, u32[]{:S(2)}) collective-permute-start(bf16[4,144,128]{2,1,0:T(8,128)(2,1)S(1)} %pad_maximum_fusion.1), channel_id=1, source_target_pairs={{0,64},{8,72},{16,80},{24,88},{64,32},{72,40},{80,48},{88,56},{32,... | collective-permute-start | bytes 442376 | tf_op jit(solution)/shard_map/ppermute | solution.py:49

commit v2 on v1

--- a/solution.py
+++ b/solution.py
@@ -275,7 +275,7 @@
         functools.partial(near_body, scale=scale),
         (shape_of(own.shape, F32), shape_of((depth, depth), BF16), shape_of((depth, depth), BF16)),
         "near_terms",
-        vmem=63,
+        vmem=40,
         in_specs=[pl.BlockSpec(memory_space=pltpu.SMEM)] + [whole] * 2 + [anywhere] * 2 + [whole] * len(others),
         out_specs=[whole] * 3,
         scratch_shapes=[pltpu.SemaphoreType.DMA((32,))],
@@ -331,7 +331,7 @@
         functools.partial(far_body, scale=scale),
         (shape_of((tok + EXTRA, 4 * col), BF16), shape_of((owners, 5 * width // owners, col), BF16)),
         "far_terms",
-        vmem=63,
+        vmem=40,
         in_specs=[pl.BlockSpec(memory_space=pltpu.SMEM)] + [pl.BlockSpec(memory_space=pl.ANY)] * len(sources),
         out_specs=[pl.BlockSpec(memory_space=pl.ANY)] * 2,
         scratch_shapes=[
@@ -452,7 +452,7 @@
         prepare_body,
         (shape_of((width, tok), BF16), shape_of((width, tok), BF16)),
         "prepare",
-        vmem=63,
+        vmem=40,
         grid_spec=pltpu.PrefetchScalarGridSpec(
             num_scalar_prefetch=1,
             grid=(4,),

time: 111 us -> 107 us (0.964)
  Pallas kernels: 31 us -> 25.4 us
  waiting for transfers between devices: 36.3 us -> 39.1 us
  starting transfers between devices: 38.8 us -> 36.4 us
  local copies, waits for them, and re-layouts: 1.5 us -> 3.5 us
    ppermute x7, waiting for transfers between devices: 6.02 us -> 8.88 us  [move_seq(): return lax.ppermute(value, 'seq', pairs)]
    pallas_call x1, Pallas kernels: 4.19 us -> 1.43 us  [prepare(): kernel_call(prepare_body, (shape_of((width, tok), BF16), shape_of((width,...]
    pallas_call x1, Pallas kernels: 8.17 us -> 5.52 us  [near_terms(): kernel_call(functools.partial(near_body, scale=scale), (shape_of(own.shap...]
    ppermute x2, starting transfers between devices: 4.65 us -> 2.39 us  [move_core(): return lax.ppermute(value, 'col', [(i, i ^ 1) for i in range(8)])]
    unnamed x26 -> x30, local copies, waits for them, and re-layouts: 1.45 us -> 3.46 us
  transfers between devices with their start and end apart: 20 -> 20, of which waited for: 10 -> 10; matrix products, arithmetic and copies ran while one was open for 0% -> 0% of each run, Pallas kernels for 19% -> 15%
where the time goes in v2:
time: 107 us
  waiting for transfers between devices  39.1 us (37%)
  starting transfers between devices  36.4 us (34%)
  Pallas kernels  25.4 us (24%)
  local copies, waits for them, and re-layouts  3.5 us (3%)
  between operations  1.79 us (2%)
    ppermute x6, waiting for transfers between devices, move_plane(): return lax.ppermute(value, ('dp', 'seq'), pairs)  19.8 us
    ppermute x7, starting transfers between devices, move_seq(): return lax.ppermute(value, 'seq', pairs)  11.3 us
    ppermute x6, starting transfers between devices, move_plane(): return lax.ppermute(value, ('dp', 'seq'), pairs)  9.45 us
    all_to_all x2, starting transfers between devices, swap_plane(): return lax.all_to_all(value, ('dp', 'seq'), 0, 0, tiled=True)  9.37 us
    ppermute x7, waiting for transfers between devices, move_seq(): return lax.ppermute(value, 'seq', pairs)  8.88 us
    ppermute x3, waiting for transfers between devices, move_y(): lax.ppermute(value, 'col', [(i, (i // 2 + dy) % 4 * 2 + i % 2) for i in r...  8.86 us
    pallas_call x1, Pallas kernels, far_terms(): kernel_call(functools.partial(far_body, scale=scale), (shape_of((tok + EX...  6.01 us
    pallas_call x1, Pallas kernels, near_terms(): kernel_call(functools.partial(near_body, scale=scale), (shape_of(own.shap...  5.52 us
  transfers between devices with their start and end apart: 20, of which 10 were waited for; matrix products, arithmetic and copies ran while one was open for 0% of the time, Pallas kernels for 15%

profile of v2, /device:TPU:1, one launch (start us, length us, event | category | flops | bytes accessed | tf_op | source)
XLA Modules:
  0.0 106.9 jit_solution(6212422660261680429)
XLA Ops:
  0.6 1.5 %collective-permute-start.4 = (bf16[4,1024,128]{2,1,0:T(8,128)(2,1)}, bf16[4,1024,128]{2,1,0:T(8,128)(2,1)}, u32[]{:S(2)}, u32[]{:S(2)}) collective-permute-start(bf16[4,1024,128]{2,1,0:T(8,128)(2,1)} %proj_own_ref.1), channel_id=1, source_target_pairs={{0,1},{1,0},{2,3},{3,2},{4,5},{5,4},{6,7},{7,6},{8,9},{9,8},{10,11... | collective-permute-start | bytes 3145736 | tf_op jit(solution)/shard_map/ppermute | solution.py:62
  2.8 4.7 %project.1 = (bf16[2,2,512,128]{3,2,1,0:T(8,128)(2,1)}, bf16[2,512,128]{2,1,0:T(8,128)(2,1)}, bf16[2,512,128]{2,1,0:T(8,128)(2,1)}, bf16[2,512,128]{2,1,0:T(8,12...) custom-call(s32[1]{0:T(128)S(6)} %copy.19.length_ref, ...), custom_call_target="tpu_custom_call" | custom-call | flops 1000 | bytes 1000 | tf_op jit(solution)/shard_map/project/pallas_call | solution.py:130
  7.5 3.8 %collective-permute-start = (bf16[2,512,128]{2,1,0:T(8,128)(2,1)}, bf16[2,512,128]{2,1,0:T(8,128)(2,1)S(1)}, u32[]{:S(2)}, u32[]{:S(2)}) collective-permute-start(bf16[2,512,128]{2,1,0:T(8,128)(2,1)} %get-tuple-element.168), channel_id=1, source_target_pairs={{0,32},{8,40},{16,48},{24,56},{32,0},{40,8},{48,16},{56,24},{1,33}... | collective-permute-start | bytes 786440 | tf_op jit(solution)/shard_map/ppermute | solution.py:54
  11.3 1.2 %collective-permute-start.5 = (bf16[2,512,128]{2,1,0:T(8,128)(2,1)}, bf16[2,512,128]{2,1,0:T(8,128)(2,1)S(1)}, u32[]{:S(2)}, u32[]{:S(2)}) collective-permute-start(bf16[2,512,128]{2,1,0:T(8,128)(2,1)} %get-tuple-element.170), channel_id=1, source_target_pairs={{0,8},{8,16},{16,24},{24,0},{32,40},{40,48},{48,56},{56,32},{1,9},... | collective-permute-start | bytes 786440 | tf_op jit(solution)/shard_map/ppermute | solution.py:54
  12.5 1.5 %collective-permute-start.6 = (bf16[2,512,128]{2,1,0:T(8,128)(2,1)}, bf16[2,512,128]{2,1,0:T(8,128)(2,1)S(1)}, u32[]{:S(2)}, u32[]{:S(2)}) collective-permute-start(bf16[2,512,128]{2,1,0:T(8,128)(2,1)} %get-tuple-element.171), channel_id=1, source_target_pairs={{0,24},{8,0},{16,8},{24,16},{32,56},{40,32},{48,40},{56,48},{1,25}... | collective-permute-start | bytes 786440 | tf_op jit(solution)/shard_map/ppermute | solution.py:54
  14.0 1.5 %collective-permute-start.7 = (bf16[2,512,128]{2,1,0:T(8,128)(2,1)}, bf16[2,512,128]{2,1,0:T(8,128)(2,1)S(1)}, u32[]{:S(2)}, u32[]{:S(2)}) collective-permute-start(bf16[2,512,128]{2,1,0:T(8,128)(2,1)} %get-tuple-element.172), channel_id=1, source_target_pairs={{0,16},{8,24},{16,0},{24,8},{32,48},{40,56},{48,32},{56,40},{1,17}... | collective-permute-start | bytes 786440 | tf_op jit(solution)/shard_map/ppermute | solution.py:54
  15.5 2.7 %collective-permute-done.refs_0_ = bf16[2,512,128]{2,1,0:T(8,128)(2,1)S(1)} collective-permute-done((bf16[2,512,128]{2,1,0:T(8,128)(2,1)}, bf16[2,512,128]{2,1,0:T(8,128)(2,1)S(1)}, u32[]{:S(2)}, u32[]{:S(2)}) %collective-permute-start) | collective-permute-done | bytes 262176 | tf_op jit(solution)/shard_map/ppermute | solution.py:54
  18.2 1.2 %collective-permute-start.1 = (bf16[2,512,128]{2,1,0:T(8,128)(2,1)S(1)}, bf16[2,512,128]{2,1,0:T(8,128)(2,1)S(1)}, u32[]{:S(2)}, u32[]{:S(2)}) collective-permute-start(bf16[2,512,128]{2,1,0:T(8,128)(2,1)S(1)} %collective-permute-done.refs_0_), channel_id=1, source_target_pairs={{0,8},{8,16},{16,24},{24,0},{32,40},{40,48},{48,56},{56,32},{1,9},... | collective-permute-start | bytes 786440 | tf_op jit(solution)/shard_map/ppermute | solution.py:54
  19.4 0.9 collective-permute-done.5.refs_1_
  20.3 1.3 %collective-permute-start.2 = (bf16[2,512,128]{2,1,0:T(8,128)(2,1)S(1)}, bf16[2,512,128]{2,1,0:T(8,128)(2,1)S(1)}, u32[]{:S(2)}, u32[]{:S(2)}) collective-permute-start(bf16[2,512,128]{2,1,0:T(8,128)(2,1)S(1)} %collective-permute-done.refs_0_), channel_id=1, source_target_pairs={{0,24},{8,0},{16,8},{24,16},{32,56},{40,32},{48,40},{56,48},{1,25}... | collective-permute-start | bytes 786440 | tf_op jit(solution)/shard_map/ppermute | solution.py:54
  21.6 0.0 collective-permute-done.6.refs_2_
  21.6 0.9 collective-permute-start.3
  22.4 1.2 %copy-done = bf16[1,512,1024]{2,1,0:T(8,128)(2,1)S(1)} copy-done((bf16[1,512,1024]{2,1,0:T(8,128)(2,1)S(1)}, bf16[1,512,1024]{2,1,0:T(8,128)(2,1)}, u32[]{:S(2)}) %copy-start) | copy-done | bytes 1048600
  23.7 1.2 %copy-done.2 = bf16[1,512,1024]{2,1,0:T(8,128)(2,1)S(1)} copy-done((bf16[1,512,1024]{2,1,0:T(8,128)(2,1)S(1)}, bf16[1,512,1024]{2,1,0:T(8,128)(2,1)}, u32[]{:S(2)}) %copy-start.2) | copy-done | bytes 1048600
  24.9 0.9 copy-done.5
  25.8 1.4 %prepare.1 = (bf16[1024,512]{1,0:T(8,128)(2,1)S(1)}, bf16[1024,512]{1,0:T(8,128)(2,1)S(1)}) custom-call(s32[1]{0:T(128)S(6)} %copy.19.length_ref, bf16[512,1024]{1,0:T(8,128)(2,1)S(1)} %bitcast.8, bf16[512,1024]{1,0:T(8,128)(2,1)S(1)} %bitcast.11, f32[1,1024]{1,0:T(1,128)S(1)} %bitcast.17, f32[512,128]{1,0:T(8,128)S(1)} %copy-done.5), custom_call_target="tpu_custom_call" | custom-call | flops 1000 | bytes 1000 | tf_op jit(solution)/shard_map/prepare/pallas_call | solution.py:451
  27.3 0.0 collective-permute-done.7.refs_3_
  27.3 0.0 copy-start.8
  27.4 5.5 %near_terms.1 = (f32[2,2,512,128]{3,2,1,0:T(8,128)S(1)}, bf16[512,512]{1,0:T(8,128)(2,1)S(1)}, bf16[512,512]{1,0:T(8,128)(2,1)S(1)}) custom-call(s32[1]{0:T(128)S(6)} %copy.19.length_ref, bf16[2,2,512,128]{3,2,1,0:T(8,128)(2,1)S(1)} %copy-done.7, s32[32,32]{1,0:T(8,128)S(1)} %bitcast.14, bf16[4,1024,128]{2,1,0:T(8,128)(2,1)S(1)} %copy-done.4, ...), custom_call_target="tpu_custom_call" | custom-call | flops 1000 | bytes 1000 | tf_op jit(solution)/shard_map/near_terms/pallas_call | solution.py:274
  32.9 5.3 %collective-permute-done.3.refs_4_ = bf16[2,512,128]{2,1,0:T(8,128)(2,1)S(1)} collective-permute-done((bf16[2,512,128]{2,1,0:T(8,128)(2,1)S(1)}, bf16[2,512,128]{2,1,0:T(8,128)(2,1)S(1)}, u32[]{:S(2)}, u32[]{:S(2)}) %collective-permute-start.3) | collective-permute-done | bytes 262176 | tf_op jit(solution)/shard_map/ppermute | solution.py:54
  38.2 6.0 %far_terms.1 = (bf16[528,512]{1,0:T(8,128)(2,1)S(1)}, bf16[16,320,128]{2,1,0:T(8,128)(2,1)}) custom-call(s32[1]{0:T(128)S(6)} %copy.19.length_ref, bf16[2,2,512,128]{3,2,1,0:T(8,128)(2,1)S(1)} %copy-done.7, s32[32,32]{1,0:T(8,128)S(1)} %bitcast.15, bf16[2,512,128]{2,1,0:T(8,128)(2,1)S(1)} %collective-permute-done.1.refs_2_, ...), custom_call_target="tpu_custom_call" | custom-call | flops 1000 | bytes 1000 | tf_op jit(solution)/shard_map/far_terms/pallas_call | solution.py:330
  44.2 4.1 %all-to-all-start.1 = ((bf16[16,320,128]{2,1,0:T(8,128)(2,1)}), bf16[16,320,128]{2,1,0:T(8,128)(2,1)S(1)}, u32[]{:S(2)}, u32[]{:S(2)}) async-start(bf16[16,320,128]{2,1,0:T(8,128)(2,1)} %get-tuple-element.194), calls=%async_computation.1 | async-start | bytes 2621440 | tf_op jit(solution)/shard_map/all_to_all | solution.py:37
  48.3 0.0 copy-start.1
  48.4 0.0 copy-start.3
  48.4 0.0 copy-start.16
  48.4 0.9 collective-permute-start.8
  49.3 1.6 %collective-permute-done.8.peer_ref = bf16[528,512]{1,0:T(8,128)(2,1)S(1)} collective-permute-done((bf16[528,512]{1,0:T(8,128)(2,1)S(1)}, bf16[528,512]{1,0:T(8,128)(2,1)S(1)}, u32[]{:S(2)}, u32[]{:S(2)}) %collective-permute-start.8) | collective-permute-done | bytes 540704 | tf_op jit(solution)/shard_map/ppermute | solution.py:62
  50.8 0.7 back_project.1
  51.6 2.8 %collective-permute-start.10 = (bf16[528,128]{1,0:T(8,128)(2,1)S(1)}, bf16[528,128]{1,0:T(8,128)(2,1)S(1)}, u32[]{:S(2)}, u32[]{:S(2)}) collective-permute-start(bf16[528,128]{1,0:T(8,128)(2,1)S(1)} %get-tuple-element.188), channel_id=1, source_target_pairs={{0,6},{1,7},{2,0},{3,1},{4,2},{5,3},{6,4},{7,5},{8,14},{9,15},{10,... | collective-permute-start | bytes 405512 | tf_op jit(solution)/shard_map/ppermute | solution.py:58
  54.4 0.3 collective-permute-start.11
  54.7 0.7 collective-permute-start.9
  55.4 4.3 %collective-permute-done.10.refs_2_ = bf16[528,128]{1,0:T(8,128)(2,1)S(1)} collective-permute-done((bf16[528,128]{1,0:T(8,128)(2,1)S(1)}, bf16[528,128]{1,0:T(8,128)(2,1)S(1)}, u32[]{:S(2)}, u32[]{:S(2)}) %collective-permute-start.10) | collective-permute-done | bytes 135200 | tf_op jit(solution)/shard_map/ppermute | solution.py:58
  59.7 0.7 collective-permute-done.11.refs_3_
  60.4 3.9 %collective-permute-done.9.refs_1_ = bf16[528,128]{1,0:T(8,128)(2,1)S(1)} collective-permute-done((bf16[528,128]{1,0:T(8,128)(2,1)S(1)}, bf16[528,128]{1,0:T(8,128)(2,1)S(1)}, u32[]{:S(2)}, u32[]{:S(2)}) %collective-permute-start.9) | collective-permute-done | bytes 135200 | tf_op jit(solution)/shard_map/ppermute | solution.py:58
  64.3 2.0 %input_grads.1 = (bf16[512,128]{1,0:T(8,128)(2,1)S(1)}, bf16[4,144,128]{2,1,0:T(8,128)(2,1)S(1)}, bf16[4,144,128]{2,1,0:T(8,128)(2,1)S(1)}, bf16[4,144,128]{2,1,...) custom-call(s32[1]{0:T(128)S(6)} %copy.19.length_ref, ...), custom_call_target="tpu_custom_call" | custom-call | flops 1000 | bytes 1000 | tf_op jit(solution)/shard_map/input_grads/pallas_call | solution.py:561
  66.3 1.9 %collective-permute-start.12 = (bf16[4,144,128]{2,1,0:T(8,128)(2,1)S(1)}, bf16[4,144,128]{2,1,0:T(8,128)(2,1)S(1)}, u32[]{:S(2)}, u32[]{:S(2)}) collective-permute-start(bf16[4,144,128]{2,1,0:T(8,128)(2,1)S(1)} %get-tuple-element.191), channel_id=1, source_target_pairs={{0,8},{8,16},{16,24},{24,0},{64,72},{72,80},{80,88},{88,64},{32,40... | collective-permute-start | bytes 442376 | tf_op jit(solution)/shard_map/ppermute | solution.py:49
  68.2 1.3 %collective-permute-start.13 = (bf16[4,144,128]{2,1,0:T(8,128)(2,1)S(1)}, bf16[4,144,128]{2,1,0:T(8,128)(2,1)S(1)}, u32[]{:S(2)}, u32[]{:S(2)}) collective-permute-start(bf16[4,144,128]{2,1,0:T(8,128)(2,1)S(1)} %get-tuple-element.192), channel_id=1, source_target_pairs={{0,24},{8,0},{16,8},{24,16},{64,88},{72,64},{80,72},{88,80},{32,56... | collective-permute-start | bytes 442376 | tf_op jit(solution)/shard_map/ppermute | solution.py:49
  69.5 1.7 %collective-permute-start.14 = (bf16[4,144,128]{2,1,0:T(8,128)(2,1)S(1)}, bf16[4,144,128]{2,1,0:T(8,128)(2,1)S(1)}, u32[]{:S(2)}, u32[]{:S(2)}) collective-permute-start(bf16[4,144,128]{2,1,0:T(8,128)(2,1)S(1)} %get-tuple-element.193), channel_id=1, source_target_pairs={{0,16},{8,24},{16,0},{24,8},{64,80},{72,88},{80,64},{88,72},{32,48... | collective-permute-start | bytes 442376 | tf_op jit(solution)/shard_map/ppermute | solution.py:49
  71.2 1.3 %weight_sum.1 = bf16[16,320,128]{2,1,0:T(8,128)(2,1)} custom-call(bf16[16,320,128]{2,1,0:T(8,128)(2,1)S(1)} %all-to-all-done.1.parts_ref), custom_call_target="tpu_custom_call" | custom-call | flops 1000 | bytes 1000 | tf_op jit(solution)/shard_map/weight_sum/pallas_call | solution.py:433
  72.5 5.3 %all-to-all-start.2 = ((bf16[16,320,128]{2,1,0:T(8,128)(2,1)}), bf16[16,320,128]{2,1,0:T(8,128)(2,1)S(1)}, u32[]{:S(2)}, u32[]{:S(2)}) async-start(bf16[16,320,128]{2,1,0:T(8,128)(2,1)} %weight_sum.1), calls=%async_computation.2 | async-start | bytes 2621440 | tf_op jit(solution)/shard_map/all_to_all | solution.py:37
  77.9 2.9 %collective-permute-start.17 = (bf16[4,144,128]{2,1,0:T(8,128)(2,1)S(1)}, bf16[4,144,128]{2,1,0:T(8,128)(2,1)S(1)}, u32[]{:S(2)}, u32[]{:S(2)}) collective-permute-start(bf16[4,144,128]{2,1,0:T(8,128)(2,1)S(1)} %pad_maximum_fusion.3), channel_id=1, source_target_pairs={{0,32},{8,40},{16,48},{24,56},{64,96},{72,104},{80,112},{88,120},{... | collective-permute-start | bytes 442376 | tf_op jit(solution)/shard_map/ppermute | solution.py:49
  80.9 1.0 collective-permute-start.16
  81.9 0.6 collective-permute-start.15
  82.5 15.1 %collective-permute-done.17.refs_3_ = bf16[4,144,128]{2,1,0:T(8,128)(2,1)S(1)} collective-permute-done((bf16[4,144,128]{2,1,0:T(8,128)(2,1)S(1)}, bf16[4,144,128]{2,1,0:T(8,128)(2,1)S(1)}, u32[]{:S(2)}, u32[]{:S(2)}) %collective-permute-start.17) | collective-permute-done | bytes 147488 | tf_op jit(solution)/shard_map/ppermute | solution.py:49
  97.6 1.8 %collective-permute-done.16.refs_2_ = bf16[4,144,128]{2,1,0:T(8,128)(2,1)S(1)} collective-permute-done((bf16[4,144,128]{2,1,0:T(8,128)(2,1)S(1)}, bf16[4,144,128]{2,1,0:T(8,128)(2,1)S(1)}, u32[]{:S(2)}, u32[]{:S(2)}) %collective-permute-start.16) | collective-permute-done | bytes 147488 | tf_op jit(solution)/shard_map/ppermute | solution.py:49
  99.4 3.0 %collective-permute-done.15.refs_1_ = bf16[4,144,128]{2,1,0:T(8,128)(2,1)S(1)} collective-permute-done((bf16[4,144,128]{2,1,0:T(8,128)(2,1)S(1)}, bf16[4,144,128]{2,1,0:T(8,128)(2,1)S(1)}, u32[]{:S(2)}, u32[]{:S(2)}) %collective-permute-start.15) | collective-permute-done | bytes 147488 | tf_op jit(solution)/shard_map/ppermute | solution.py:49
  102.4 3.7 %finish.1 = (f32[4,1024,128]{2,1,0:T(8,128)}, f32[128,1024]{1,0:T(8,128)}, f32[1024,128]{1,0:T(8,128)}, f32[1,128]{1,0:T(1,128)}, s32[1]{0:T(128)}) custom-call(bf16[4,144,128]{2,1,0:T(8,128)(2,1)S(1)} %pad_maximum_fusion.refs_0_, bf16[4,144,128]{2,1,0:T(8,128)(2,1)S(1)} %collective-permute-done.15.refs_1_, ...), custom_call_target="tpu_custom_call" | custom-call | flops 1000 | bytes 1000 | tf_op jit(solution)/shard_map/finish/pallas_call | solution.py:640
  106.1 0.6 while.13
  (40 shorter events, 0.2 us)
Async XLA Ops:
  0.6 26.7 %collective-permute-start.4 = (bf16[4,1024,128]{2,1,0:T(8,128)(2,1)}, bf16[4,1024,128]{2,1,0:T(8,128)(2,1)}, u32[]{:S(2)}, u32[]{:S(2)}) collective-permute-start(bf16[4,1024,128]{2,1,0:T(8,128)(2,1)} %proj_own_ref.1), channel_id=1, source_target_pairs={{0,1},{1,0},{2,3},{3,2},{4,5},{5,4},{6,7},{7,6},{8,9},{9,8},{10,11... | collective-permute-start | bytes 3145736 | tf_op jit(solution)/shard_map/ppermute | solution.py:62
  2.8 19.7 %copy-start.13 = (f32[1024]{0:T(1024)S(1)}, f32[1024]{0:T(1024)}, u32[]{:S(2)}) copy-start(f32[1024]{0:T(1024)} %param.12) | copy-start | bytes 12292
  2.8 24.5 %copy-start.11 = (s32[1,32,32]{2,1,0:T(8,128)S(1)}, s32[1,32,32]{2,1,0:T(8,128)}, u32[]{:S(2)}) copy-start(s32[1,32,32]{2,1,0:T(8,128)} %param.17) | copy-start | bytes 12292
  7.5 10.6 %collective-permute-start = (bf16[2,512,128]{2,1,0:T(8,128)(2,1)}, bf16[2,512,128]{2,1,0:T(8,128)(2,1)S(1)}, u32[]{:S(2)}, u32[]{:S(2)}) collective-permute-start(bf16[2,512,128]{2,1,0:T(8,128)(2,1)} %get-tuple-element.168), channel_id=1, source_target_pairs={{0,32},{8,40},{16,48},{24,56},{32,0},{40,8},{48,16},{56,24},{1,33}... | collective-permute-start | bytes 786440 | tf_op jit(solution)/shard_map/ppermute | solution.py:54
  11.3 9.0 %collective-permute-start.5 = (bf16[2,512,128]{2,1,0:T(8,128)(2,1)}, bf16[2,512,128]{2,1,0:T(8,128)(2,1)S(1)}, u32[]{:S(2)}, u32[]{:S(2)}) collective-permute-start(bf16[2,512,128]{2,1,0:T(8,128)(2,1)} %get-tuple-element.170), channel_id=1, source_target_pairs={{0,8},{8,16},{16,24},{24,0},{32,40},{40,48},{48,56},{56,32},{1,9},... | collective-permute-start | bytes 786440 | tf_op jit(solution)/shard_map/ppermute | solution.py:54
  12.5 9.1 %collective-permute-start.6 = (bf16[2,512,128]{2,1,0:T(8,128)(2,1)}, bf16[2,512,128]{2,1,0:T(8,128)(2,1)S(1)}, u32[]{:S(2)}, u32[]{:S(2)}) collective-permute-start(bf16[2,512,128]{2,1,0:T(8,128)(2,1)} %get-tuple-element.171), channel_id=1, source_target_pairs={{0,24},{8,0},{16,8},{24,16},{32,56},{40,32},{48,40},{56,48},{1,25}... | collective-permute-start | bytes 786440 | tf_op jit(solution)/shard_map/ppermute | solution.py:54
  14.0 13.3 %collective-permute-start.7 = (bf16[2,512,128]{2,1,0:T(8,128)(2,1)}, bf16[2,512,128]{2,1,0:T(8,128)(2,1)S(1)}, u32[]{:S(2)}, u32[]{:S(2)}) collective-permute-start(bf16[2,512,128]{2,1,0:T(8,128)(2,1)} %get-tuple-element.172), channel_id=1, source_target_pairs={{0,16},{8,24},{16,0},{24,8},{32,48},{40,56},{48,32},{56,40},{1,17}... | collective-permute-start | bytes 786440 | tf_op jit(solution)/shard_map/ppermute | solution.py:54
  18.2 14.8 %collective-permute-start.1 = (bf16[2,512,128]{2,1,0:T(8,128)(2,1)S(1)}, bf16[2,512,128]{2,1,0:T(8,128)(2,1)S(1)}, u32[]{:S(2)}, u32[]{:S(2)}) collective-permute-start(bf16[2,512,128]{2,1,0:T(8,128)(2,1)S(1)} %collective-permute-done.refs_0_), channel_id=1, source_target_pairs={{0,8},{8,16},{16,24},{24,0},{32,40},{40,48},{48,56},{56,32},{1,9},... | collective-permute-start | bytes 786440 | tf_op jit(solution)/shard_map/ppermute | solution.py:54
  20.3 12.6 %collective-permute-start.2 = (bf16[2,512,128]{2,1,0:T(8,128)(2,1)S(1)}, bf16[2,512,128]{2,1,0:T(8,128)(2,1)S(1)}, u32[]{:S(2)}, u32[]{:S(2)}) collective-permute-start(bf16[2,512,128]{2,1,0:T(8,128)(2,1)S(1)} %collective-permute-done.refs_0_), channel_id=1, source_target_pairs={{0,24},{8,0},{16,8},{24,16},{32,56},{40,32},{48,40},{56,48},{1,25}... | collective-permute-start | bytes 786440 | tf_op jit(solution)/shard_map/ppermute | solution.py:54
  21.6 16.6 %collective-permute-start.3 = (bf16[2,512,128]{2,1,0:T(8,128)(2,1)S(1)}, bf16[2,512,128]{2,1,0:T(8,128)(2,1)S(1)}, u32[]{:S(2)}, u32[]{:S(2)}) collective-permute-start(bf16[2,512,128]{2,1,0:T(8,128)(2,1)S(1)} %collective-permute-done.refs_0_), channel_id=1, source_target_pairs={{0,16},{8,24},{16,0},{24,8},{32,48},{40,56},{48,32},{56,40},{1,17}... | collective-permute-start | bytes 786440 | tf_op jit(solution)/shard_map/ppermute | solution.py:54
  22.4 1.2 %copy-start = (bf16[1,512,1024]{2,1,0:T(8,128)(2,1)S(1)}, bf16[1,512,1024]{2,1,0:T(8,128)(2,1)}, u32[]{:S(2)}) copy-start(bf16[1,512,1024]{2,1,0:T(8,128)(2,1)} %param.10) | copy-start | bytes 3145732
  23.7 1.2 %copy-start.2 = (bf16[1,512,1024]{2,1,0:T(8,128)(2,1)S(1)}, bf16[1,512,1024]{2,1,0:T(8,128)(2,1)}, u32[]{:S(2)}) copy-start(bf16[1,512,1024]{2,1,0:T(8,128)(2,1)} %param.11) | copy-start | bytes 3145732
  24.9 0.9 copy-start.5
  25.8 1.5 %copy-start.4 = (bf16[4,1024,128]{2,1,0:T(8,128)(2,1)S(1)}, bf16[4,1024,128]{2,1,0:T(8,128)(2,1)}, u32[]{:S(2)}) copy-start(bf16[4,1024,128]{2,1,0:T(8,128)(2,1)} %proj_own_ref.1) | copy-start | bytes 3145732
  25.8 1.5 %copy-start.7 = (bf16[2,2,512,128]{3,2,1,0:T(8,128)(2,1)S(1)}, bf16[2,2,512,128]{3,2,1,0:T(8,128)(2,1)}, u32[]{:S(2)}) copy-start(bf16[2,2,512,128]{3,2,1,0:T(8,128)(2,1)} %get-tuple-element.167.own_ref.refs_0_) | copy-start | bytes 1572868
  27.3 10.9 %copy-start.6 = (f32[512,128]{1,0:T(8,128)S(1)}, f32[512,128]{1,0:T(8,128)}, u32[]{:S(2)}) copy-start(f32[512,128]{1,0:T(8,128)} %get-tuple-element.175.inv_rms_ref.refs_7_) | copy-start | bytes 786436
  27.3 10.9 %copy-start.8 = (f32[4,512,128]{2,1,0:T(8,128)S(1)}, f32[4,512,128]{2,1,0:T(8,128)}, u32[]{:S(2)}) copy-start(f32[4,512,128]{2,1,0:T(8,128)} %get-tuple-element.174.refs_6_) | copy-start | bytes 3145732
  27.4 10.8 %copy-start.9 = (f32[512,128]{1,0:T(8,128)S(1)}, f32[512,128]{1,0:T(8,128)}, u32[]{:S(2)}) copy-start(f32[512,128]{1,0:T(8,128)} %get-tuple-element.176.refs_8_) | copy-start | bytes 786436
  27.4 10.8 %copy-start.10 = (f32[512,128]{1,0:T(8,128)S(1)}, f32[512,128]{1,0:T(8,128)}, u32[]{:S(2)}) copy-start(f32[512,128]{1,0:T(8,128)} %get-tuple-element.178.refs_10_) | copy-start | bytes 786436
  27.4 10.8 %copy-start.12 = (bf16[512,128]{1,0:T(8,128)(2,1)S(1)}, bf16[512,128]{1,0:T(8,128)(2,1)}, u32[]{:S(2)}) copy-start(bf16[512,128]{1,0:T(8,128)(2,1)} %get-tuple-element.177.refs_9_) | copy-start | bytes 393220
  44.2 27.0 %all-to-all-start.1 = ((bf16[16,320,128]{2,1,0:T(8,128)(2,1)}), bf16[16,320,128]{2,1,0:T(8,128)(2,1)S(1)}, u32[]{:S(2)}, u32[]{:S(2)}) async-start(bf16[16,320,128]{2,1,0:T(8,128)(2,1)} %get-tuple-element.194), calls=%async_computation.1 | async-start | bytes 2621440 | tf_op jit(solution)/shard_map/all_to_all | solution.py:37
  48.3 15.9 %copy-start.1 = (bf16[1,512,1024]{2,1,0:T(8,128)(2,1)S(1)}, bf16[1,512,1024]{2,1,0:T(8,128)(2,1)}, u32[]{:S(2)}) copy-start(bf16[1,512,1024]{2,1,0:T(8,128)(2,1)} %param.10) | copy-start | bytes 3145732
  48.4 15.9 %copy-start.3 = (bf16[1,512,1024]{2,1,0:T(8,128)(2,1)S(1)}, bf16[1,512,1024]{2,1,0:T(8,128)(2,1)}, u32[]{:S(2)}) copy-start(bf16[1,512,1024]{2,1,0:T(8,128)(2,1)} %param.11) | copy-start | bytes 3145732
  48.4 15.9 %copy-start.16 = (s32[1,512]{1,0:T(1,128)S(1)}, s32[1,512]{1,0:T(1,128)}, u32[]{:S(2)}) copy-start(s32[1,512]{1,0:T(1,128)} %refs_8_.1) | copy-start | bytes 6148
  48.4 2.5 %collective-permute-start.8 = (bf16[528,512]{1,0:T(8,128)(2,1)S(1)}, bf16[528,512]{1,0:T(8,128)(2,1)S(1)}, u32[]{:S(2)}, u32[]{:S(2)}) collective-permute-start(bf16[528,512]{1,0:T(8,128)(2,1)S(1)} %get-tuple-element.183.own_ref), channel_id=1, source_target_pairs={{0,1},{1,0},{2,3},{3,2},{4,5},{5,4},{6,7},{7,6},{8,9},{9,8},{10,11... | collective-permute-start | bytes 1622024 | tf_op jit(solution)/shard_map/ppermute | solution.py:62
  51.6 8.2 %collective-permute-start.10 = (bf16[528,128]{1,0:T(8,128)(2,1)S(1)}, bf16[528,128]{1,0:T(8,128)(2,1)S(1)}, u32[]{:S(2)}, u32[]{:S(2)}) collective-permute-start(bf16[528,128]{1,0:T(8,128)(2,1)S(1)} %get-tuple-element.188), channel_id=1, source_target_pairs={{0,6},{1,7},{2,0},{3,1},{4,2},{5,3},{6,4},{7,5},{8,14},{9,15},{10,... | collective-permute-start | bytes 405512 | tf_op jit(solution)/shard_map/ppermute | solution.py:58
  54.4 6.0 %collective-permute-start.11 = (bf16[528,128]{1,0:T(8,128)(2,1)S(1)}, bf16[528,128]{1,0:T(8,128)(2,1)S(1)}, u32[]{:S(2)}, u32[]{:S(2)}) collective-permute-start(bf16[528,128]{1,0:T(8,128)(2,1)S(1)} %get-tuple-element.189), channel_id=1, source_target_pairs={{0,4},{1,5},{2,6},{3,7},{4,0},{5,1},{6,2},{7,3},{8,12},{9,13},{10,... | collective-permute-start | bytes 405512 | tf_op jit(solution)/shard_map/ppermute | solution.py:58
  54.7 9.6 %collective-permute-start.9 = (bf16[528,128]{1,0:T(8,128)(2,1)S(1)}, bf16[528,128]{1,0:T(8,128)(2,1)S(1)}, u32[]{:S(2)}, u32[]{:S(2)}) collective-permute-start(bf16[528,128]{1,0:T(8,128)(2,1)S(1)} %get-tuple-element.187), channel_id=1, source_target_pairs={{0,2},{1,3},{2,4},{3,5},{4,6},{5,7},{6,0},{7,1},{8,10},{9,11},{10,... | collective-permute-start | bytes 405512 | tf_op jit(solution)/shard_map/ppermute | solution.py:58
  66.3 11.5 %collective-permute-start.12 = (bf16[4,144,128]{2,1,0:T(8,128)(2,1)S(1)}, bf16[4,144,128]{2,1,0:T(8,128)(2,1)S(1)}, u32[]{:S(2)}, u32[]{:S(2)}) collective-permute-start(bf16[4,144,128]{2,1,0:T(8,128)(2,1)S(1)} %get-tuple-element.191), channel_id=1, source_target_pairs={{0,8},{8,16},{16,24},{24,0},{64,72},{72,80},{80,88},{88,64},{32,40... | collective-permute-start | bytes 442376 | tf_op jit(solution)/shard_map/ppermute | solution.py:49
  68.2 9.6 %collective-permute-start.13 = (bf16[4,144,128]{2,1,0:T(8,128)(2,1)S(1)}, bf16[4,144,128]{2,1,0:T(8,128)(2,1)S(1)}, u32[]{:S(2)}, u32[]{:S(2)}) collective-permute-start(bf16[4,144,128]{2,1,0:T(8,128)(2,1)S(1)} %get-tuple-element.192), channel_id=1, source_target_pairs={{0,24},{8,0},{16,8},{24,16},{64,88},{72,64},{80,72},{88,80},{32,56... | collective-permute-start | bytes 442376 | tf_op jit(solution)/shard_map/ppermute | solution.py:49
  69.5 8.3 %collective-permute-start.14 = (bf16[4,144,128]{2,1,0:T(8,128)(2,1)S(1)}, bf16[4,144,128]{2,1,0:T(8,128)(2,1)S(1)}, u32[]{:S(2)}, u32[]{:S(2)}) collective-permute-start(bf16[4,144,128]{2,1,0:T(8,128)(2,1)S(1)} %get-tuple-element.193), channel_id=1, source_target_pairs={{0,16},{8,24},{16,0},{24,8},{64,80},{72,88},{80,64},{88,72},{32,48... | collective-permute-start | bytes 442376 | tf_op jit(solution)/shard_map/ppermute | solution.py:49
  72.5 29.9 %all-to-all-start.2 = ((bf16[16,320,128]{2,1,0:T(8,128)(2,1)}), bf16[16,320,128]{2,1,0:T(8,128)(2,1)S(1)}, u32[]{:S(2)}, u32[]{:S(2)}) async-start(bf16[16,320,128]{2,1,0:T(8,128)(2,1)} %weight_sum.1), calls=%async_computation.2 | async-start | bytes 2621440 | tf_op jit(solution)/shard_map/all_to_all | solution.py:37
  77.9 19.7 %collective-permute-start.17 = (bf16[4,144,128]{2,1,0:T(8,128)(2,1)S(1)}, bf16[4,144,128]{2,1,0:T(8,128)(2,1)S(1)}, u32[]{:S(2)}, u32[]{:S(2)}) collective-permute-start(bf16[4,144,128]{2,1,0:T(8,128)(2,1)S(1)} %pad_maximum_fusion.3), channel_id=1, source_target_pairs={{0,32},{8,40},{16,48},{24,56},{64,96},{72,104},{80,112},{88,120},{... | collective-permute-start | bytes 442376 | tf_op jit(solution)/shard_map/ppermute | solution.py:49
  80.9 18.5 %collective-permute-start.16 = (bf16[4,144,128]{2,1,0:T(8,128)(2,1)S(1)}, bf16[4,144,128]{2,1,0:T(8,128)(2,1)S(1)}, u32[]{:S(2)}, u32[]{:S(2)}) collective-permute-start(bf16[4,144,128]{2,1,0:T(8,128)(2,1)S(1)} %pad_maximum_fusion.2), channel_id=1, source_target_pairs={{0,96},{8,104},{16,112},{24,120},{64,0},{72,8},{80,16},{88,24},{32... | collective-permute-start | bytes 442376 | tf_op jit(solution)/shard_map/ppermute | solution.py:49
  81.9 20.5 %collective-permute-start.15 = (bf16[4,144,128]{2,1,0:T(8,128)(2,1)S(1)}, bf16[4,144,128]{2,1,0:T(8,128)(2,1)S(1)}, u32[]{:S(2)}, u32[]{:S(2)}) collective-permute-start(bf16[4,144,128]{2,1,0:T(8,128)(2,1)S(1)} %pad_maximum_fusion.1), channel_id=1, source_target_pairs={{0,64},{8,72},{16,80},{24,88},{64,32},{72,40},{80,48},{88,56},{32,... | collective-permute-start | bytes 442376 | tf_op jit(solution)/shard_map/ppermute | solution.py:49

commit v3 on v2

--- a/solution.py
+++ b/solution.py
@@ -282,36 +282,33 @@
     )(lengths, own, mask, proj_own, proj_peer, *others)
 
 
-FAR_INPUTS = 13
-
-
-def far_body(length_ref, *refs, scale):
+FAR_INPUTS = 8
+
+
+def far_body(length_ref, own_ref, mask_ref, *refs, scale):
+    others, refs = refs[:3], refs[3:]
     sources, d_out, parts_out = refs[:FAR_INPUTS], refs[FAR_INPUTS], refs[FAR_INPUTS + 1]
     held = refs[FAR_INPUTS + 2:2 * FAR_INPUTS + 2]
     mixed_ref, d_ref, parts_ref, sems, out_sems = refs[2 * FAR_INPUTS + 2:]
     copies = [pltpu.make_async_copy(source, place, sems.at[n]) for n, (source, place) in enumerate(zip(sources, held))]
     for copy in copies:
         copy.start()
-    own_ref, mask_ref = held[:2]
     rank = lax.axis_index("seq")
-    others, acc_ref = held[2:5], held[5]
-    pre_ref, inv_rms_ref, dmix_ref, upd_ref, inv_cnt_ref, normed_t_ref, grad_t_ref = held[6:]
-    copies[0].wait()
-    copies[1].wait()
+    acc_ref = held[0]
+    pre_ref, inv_rms_ref, dmix_ref, upd_ref, inv_cnt_ref, normed_t_ref, grad_t_ref = held[1:]
     kept = kept_tiles(mask_ref, length_ref, rank, own_ref.shape[2] // BLOCK)
     for index, (dx, other) in enumerate(zip((1, 3, 2), others)):
-        copies[2 + index].wait()
         side, sums = far_sums(rank_at(rank, 1, dx), rank, kept, own_ref, other, scale)
         if index == 0:
-            copies[5].wait()
+            copies[0].wait()
         acc_ref[side, 0] += sums[0]
         acc_ref[side, 1] += sums[1]
-    for copy in copies[6:11]:
+    for copy in copies[1:6]:
         copy.wait()
     pre_grad_body(acc_ref, pre_ref, inv_rms_ref, dmix_ref, upd_ref, inv_cnt_ref, d_ref, mixed_ref, scale=scale)
     leaving = [pltpu.make_async_copy(d_ref, d_out, out_sems.at[0])]
     leaving[0].start()
-    for copy in copies[11:]:
+    for copy in copies[6:]:
         copy.wait()
     half = parts_ref.shape[0] // 2
     for part in range(2):
@@ -326,13 +323,16 @@
 def far_terms(lengths, own, mask, others, acc, pre, inv_rms, dmix, upd, inv_cnt, normed_t, grad_t, owners, scale):
     _, _, tok, col = own.shape
     width = normed_t.shape[0]
-    sources = (own, mask, *others, acc, pre, inv_rms, dmix, upd, inv_cnt, normed_t, grad_t)
+    near_by = (own, mask, *others)
+    sources = (acc, pre, inv_rms, dmix, upd, inv_cnt, normed_t, grad_t)
     return kernel_call(
         functools.partial(far_body, scale=scale),
         (shape_of((tok + EXTRA, 4 * col), BF16), shape_of((owners, 5 * width // owners, col), BF16)),
         "far_terms",
         vmem=40,
-        in_specs=[pl.BlockSpec(memory_space=pltpu.SMEM)] + [pl.BlockSpec(memory_space=pl.ANY)] * len(sources),
+        in_specs=[pl.BlockSpec(memory_space=pltpu.SMEM)]
+        + [pl.BlockSpec(memory_space=pltpu.VMEM)] * len(near_by)
+        + [pl.BlockSpec(memory_space=pl.ANY)] * len(sources),
         out_specs=[pl.BlockSpec(memory_space=pl.ANY)] * 2,
         scratch_shapes=[
             *(pltpu.VMEM(source.shape, source.dtype) for source in sources),
@@ -342,7 +342,7 @@
             pltpu.SemaphoreType.DMA((len(sources),)),
             pltpu.SemaphoreType.DMA((3,)),
         ],
-    )(lengths, *sources)
+    )(lengths, *near_by, *sources)
 
 
 def pre_grad_body(acc_ref, pre_ref, inv_rms_ref, dmix_ref, upd_ref, inv_cnt_ref, d_ref, mixed_ref, *, scale):
@@ -433,7 +433,8 @@
     return kernel_call(weight_sum_body, shape_of(parts.shape, BF16), "weight_sum")(parts)
 
 
-def prepare_body(length_ref, x_ref, cot_ref, gain_ref, inv_rms_ref, normed_t_ref, grad_t_ref):
+def prepare_body(length_ref, x_ref, cot_ref, gain_ref, inv_rms_ref, id_ref,
+                 normed_t_ref, grad_t_ref, rank_ref, slot_ref, item_ref, *, items, room):
     step = x_ref.shape[0]
     normed = (x_ref[...].astype(F32) * inv_rms_ref[:, :1] * gain_ref[...]).astype(BF16)
     normed_t_ref[...] = normed.T
@@ -441,16 +442,26 @@
     valid = lax.broadcasted_iota(jnp.int32, (step, 1), 0) + first < length_ref[0]
     grad_t_ref[...] = jnp.where(valid, cot_ref[...].astype(F32), 0.0).astype(BF16).T
 
-
-def prepare(lengths, x, cot, gain, inv_rms):
+    @pl.when(pl.program_id(0) == 0)
+    def _():
+        slots_for(id_ref, rank_ref, slot_ref, item_ref, items, room)
+
+
+def prepare(lengths, x, cot, gain, inv_rms, ids, items, room):
     tok, width = x.shape
     col = inv_rms.shape[1]
     step = tok // 4
     row = lambda i, n: (i, 0)
     column = lambda i, n: (0, i)
     return kernel_call(
-        prepare_body,
-        (shape_of((width, tok), BF16), shape_of((width, tok), BF16)),
+        functools.partial(prepare_body, items=items, room=room),
+        (
+            shape_of((width, tok), BF16),
+            shape_of((width, tok), BF16),
+            shape_of((1, tok), jnp.int32),
+            shape_of((1, tok), jnp.int32),
+            shape_of((EXTRA, tok), BF16),
+        ),
         "prepare",
         vmem=40,
         grid_spec=pltpu.PrefetchScalarGridSpec(
@@ -461,10 +472,17 @@
                 pl.BlockSpec((step, width), row),
                 pl.BlockSpec((1, width), lambda i, n: (0, 0)),
                 pl.BlockSpec((step, col), row),
+                pl.BlockSpec((1, tok), lambda i, n: (0, 0)),
             ],
-            out_specs=[pl.BlockSpec((width, step), column), pl.BlockSpec((width, step), column)],
+            out_specs=[
+                pl.BlockSpec((width, step), column),
+                pl.BlockSpec((width, step), column),
+                pl.BlockSpec((1, tok), lambda i, n: (0, 0)),
+                pl.BlockSpec((1, tok), lambda i, n: (0, 0)),
+                pl.BlockSpec((EXTRA, tok), lambda i, n: (0, 0)),
+            ],
         ),
-    )(lengths, x, cot, gain.reshape(1, -1), inv_rms)
+    )(lengths, x, cot, gain.reshape(1, -1), inv_rms, ids)
 
 
 def fill_slots(slot_ref, item_ref, value_ref, blocks, owners, extra):
@@ -508,11 +526,11 @@
     item_ref[...] = rows.astype(BF16)
 
 
-def input_grad_body(length_ref, *refs, items):
+def input_grad_body(length_ref, *refs):
     parts = refs[:4]
-    x_any, cot_any, gain_any, inv_rms_ref, id_ref, value_ref = refs[4:10]
-    outs, (rank_ref, item_ref) = refs[10:14], refs[14:16]
-    x_bf_ref, cot_ref, gain_ref, x_ref, slot_ref, sems = refs[16:]
+    x_any, cot_any, gain_any, inv_rms_ref, slot_ref, item_ref, value_ref = refs[4:11]
+    outs = refs[11:15]
+    x_bf_ref, cot_ref, gain_ref, x_ref, sems = refs[15:]
     tok, col = x_ref.shape
     room = outs[0].shape[1] - EXTRA
     mine = pl.ds(pl.multiple_of(lax.axis_index("col") * col, col), col)
@@ -522,7 +540,6 @@
     ]
     for copy in copies:
         copy.start()
-    slots_for(id_ref, rank_ref, slot_ref, item_ref, items, room)
     for copy in copies:
         copy.wait()
     x_ref[...] = x_bf_ref[...].astype(F32) * inv_rms_ref[...]
@@ -555,28 +572,25 @@
     fill_slots(slot_ref, item_ref, value_ref, places, owners, gain_sum + jnp.where(row == 4, rounds, 0.0))
 
 
-def input_grads(lengths, parts, x, cot, gain, inv_rms, ids, items, room):
+def input_grads(lengths, parts, x, cot, gain, inv_rms, slots, item_rows, room):
     tok, col = inv_rms.shape
     whole, anywhere = pl.BlockSpec(memory_space=pltpu.VMEM), pl.BlockSpec(memory_space=pl.ANY)
     return kernel_call(
-        functools.partial(input_grad_body, items=items),
+        input_grad_body,
         (
             shape_of((tok, col), BF16),
             *(shape_of((4, room + EXTRA, col), BF16) for _ in range(4)),
-            shape_of((1, tok), jnp.int32),
-            shape_of((EXTRA, tok), BF16),
         ),
         "input_grads",
-        in_specs=[pl.BlockSpec(memory_space=pltpu.SMEM)] + [whole] * 4 + [anywhere] * 3 + [whole] * 2,
+        in_specs=[pl.BlockSpec(memory_space=pltpu.SMEM)] + [whole] * 4 + [anywhere] * 3 + [whole] * 3,
         scratch_shapes=[
             pltpu.VMEM((tok, col), BF16),
             pltpu.VMEM((tok, col), BF16),
             pltpu.VMEM((1, col), F32),
             pltpu.VMEM((tok, col), F32),
-            pltpu.VMEM((1, tok), jnp.int32),
             pltpu.SemaphoreType.DMA((3,)),
         ],
-    )(lengths, *parts, x, cot, gain.reshape(1, -1), inv_rms, ids)
+    )(lengths, *parts, x, cot, gain.reshape(1, -1), inv_rms, slots, item_rows)
 
 
 def more_body(slot_ref, item_ref, value_ref, out_ref):
@@ -636,7 +650,7 @@
 
 def finish(gots, whole, items):
     owners, rows, col = whole.shape
-    width, steps = 8 * col, 4
+    width, steps = 8 * col, 2
     return kernel_call(
         finish_body,
         (
@@ -691,7 +705,9 @@
 
     proj_peer = move_core(proj_in)
     x_now, cot_now, across = lax.optimization_barrier((x_rows, cot_rows, across))
-    normed_t, grad_t = prepare(lengths, x_now, cot_now, norm_gain, inv_rms)
+    normed_t, grad_t, rank, slots, item_rows = prepare(
+        lengths, x_now, cot_now, norm_gain, inv_rms, item_ids, items, room
+    )
     acc, w_own, w_peer = near_terms(lengths, own, mask, proj_in, proj_peer, [across] + near, scale)
     d_own, shares = far_terms(
         lengths, own, mask, far, acc, pre, inv_rms, dmix, upd, inv_cnt, normed_t, grad_t, owners, scale
@@ -701,9 +717,7 @@
     parts = back_project(d_own, d_peer, w_own, w_peer, col)
     parts = [parts[0]] + [move_y(parts[k], k) for k in (1, 3, 2)]
 
-    d_inputs, *sends, rank, item_rows = input_grads(
-        lengths, parts, x_rows, cot_rows, norm_gain, inv_rms, item_ids, items, room
-    )
+    d_inputs, *sends = input_grads(lengths, parts, x_rows, cot_rows, norm_gain, inv_rms, slots, item_rows, room)
     line = [sends[0]] + [move_plane(sends[k], 0, k) for k in (1, 3, 2)]
     sends = [jnp.stack([block[k] for block in line]) for k in range(4)]
     gots = [sends[0]] + [move_plane(sends[k], k, 0) for k in (1, 3, 2)]

time: 107 us -> 106 us (level)
  no operation moved by 1% of the time
where the time goes in v3:
time: 106 us
  waiting for transfers between devices  38.8 us (37%)
  starting transfers between devices  36.4 us (34%)
  Pallas kernels  24.6 us (23%)
  local copies, waits for them, and re-layouts  3.5 us (3%)
  between operations  1.78 us (2%)
    ppermute x6, waiting for transfers between devices, move_plane(): return lax.ppermute(value, ('dp', 'seq'), pairs)  19.8 us
    ppermute x7, starting transfers between devices, move_seq(): return lax.ppermute(value, 'seq', pairs)  11.3 us
    ppermute x6, starting transfers between devices, move_plane(): return lax.ppermute(value, ('dp', 'seq'), pairs)  9.45 us
    all_to_all x2, starting transfers between devices, swap_plane(): return lax.all_to_all(value, ('dp', 'seq'), 0, 0, tiled=True)  9.38 us
    ppermute x3, waiting for transfers between devices, move_y(): lax.ppermute(value, 'col', [(i, (i // 2 + dy) % 4 * 2 + i % 2) for i in r...  8.86 us
    ppermute x7, waiting for transfers between devices, move_seq(): return lax.ppermute(value, 'seq', pairs)  8.53 us
    pallas_call x1, Pallas kernels, far_terms(): kernel_call(functools.partial(far_body, scale=scale), (shape_of((tok + EX...  5.72 us
    pallas_call x1, Pallas kernels, near_terms(): kernel_call(functools.partial(near_body, scale=scale), (shape_of(own.shap...  5.52 us
  transfers between devices with their start and end apart: 20, of which 10 were waited for; matrix products, arithmetic and copies ran while one was open for 0% of the time, Pallas kernels for 15%

profile of v3, /device:TPU:1, one launch (start us, length us, event | category | flops | bytes accessed | tf_op | source)
XLA Modules:
  0.0 105.8 jit_solution(1836290548887649063)
XLA Ops:
  0.6 1.5 %collective-permute-start.4 = (bf16[4,1024,128]{2,1,0:T(8,128)(2,1)}, bf16[4,1024,128]{2,1,0:T(8,128)(2,1)}, u32[]{:S(2)}, u32[]{:S(2)}) collective-permute-start(bf16[4,1024,128]{2,1,0:T(8,128)(2,1)} %proj_own_ref.1), channel_id=1, source_target_pairs={{0,1},{1,0},{2,3},{3,2},{4,5},{5,4},{6,7},{7,6},{8,9},{9,8},{10,11... | collective-permute-start | bytes 3145736 | tf_op jit(solution)/shard_map/ppermute | solution.py:62
  2.8 4.7 %project.1 = (bf16[2,2,512,128]{3,2,1,0:T(8,128)(2,1)}, bf16[2,512,128]{2,1,0:T(8,128)(2,1)}, bf16[2,512,128]{2,1,0:T(8,128)(2,1)}, bf16[2,512,128]{2,1,0:T(8,12...) custom-call(s32[1]{0:T(128)S(6)} %copy.19.length_ref, ...), custom_call_target="tpu_custom_call" | custom-call | flops 1000 | bytes 1000 | tf_op jit(solution)/shard_map/project/pallas_call | solution.py:130
  7.5 3.8 %collective-permute-start = (bf16[2,512,128]{2,1,0:T(8,128)(2,1)}, bf16[2,512,128]{2,1,0:T(8,128)(2,1)S(1)}, u32[]{:S(2)}, u32[]{:S(2)}) collective-permute-start(bf16[2,512,128]{2,1,0:T(8,128)(2,1)} %get-tuple-element.169), channel_id=1, source_target_pairs={{0,32},{8,40},{16,48},{24,56},{32,0},{40,8},{48,16},{56,24},{1,33}... | collective-permute-start | bytes 786440 | tf_op jit(solution)/shard_map/ppermute | solution.py:54
  11.3 1.2 %collective-permute-start.5 = (bf16[2,512,128]{2,1,0:T(8,128)(2,1)}, bf16[2,512,128]{2,1,0:T(8,128)(2,1)S(1)}, u32[]{:S(2)}, u32[]{:S(2)}) collective-permute-start(bf16[2,512,128]{2,1,0:T(8,128)(2,1)} %get-tuple-element.171), channel_id=1, source_target_pairs={{0,8},{8,16},{16,24},{24,0},{32,40},{40,48},{48,56},{56,32},{1,9},... | collective-permute-start | bytes 786440 | tf_op jit(solution)/shard_map/ppermute | solution.py:54
  12.5 1.5 %collective-permute-start.6 = (bf16[2,512,128]{2,1,0:T(8,128)(2,1)}, bf16[2,512,128]{2,1,0:T(8,128)(2,1)S(1)}, u32[]{:S(2)}, u32[]{:S(2)}) collective-permute-start(bf16[2,512,128]{2,1,0:T(8,128)(2,1)} %get-tuple-element.172), channel_id=1, source_target_pairs={{0,24},{8,0},{16,8},{24,16},{32,56},{40,32},{48,40},{56,48},{1,25}... | collective-permute-start | bytes 786440 | tf_op jit(solution)/shard_map/ppermute | solution.py:54
  14.0 1.5 %collective-permute-start.7 = (bf16[2,512,128]{2,1,0:T(8,128)(2,1)}, bf16[2,512,128]{2,1,0:T(8,128)(2,1)S(1)}, u32[]{:S(2)}, u32[]{:S(2)}) collective-permute-start(bf16[2,512,128]{2,1,0:T(8,128)(2,1)} %get-tuple-element.173), channel_id=1, source_target_pairs={{0,16},{8,24},{16,0},{24,8},{32,48},{40,56},{48,32},{56,40},{1,17}... | collective-permute-start | bytes 786440 | tf_op jit(solution)/shard_map/ppermute | solution.py:54
  15.5 2.7 %collective-permute-done.refs_0_ = bf16[2,512,128]{2,1,0:T(8,128)(2,1)S(1)} collective-permute-done((bf16[2,512,128]{2,1,0:T(8,128)(2,1)}, bf16[2,512,128]{2,1,0:T(8,128)(2,1)S(1)}, u32[]{:S(2)}, u32[]{:S(2)}) %collective-permute-start) | collective-permute-done | bytes 262176 | tf_op jit(solution)/shard_map/ppermute | solution.py:54
  18.2 1.2 %collective-permute-start.1 = (bf16[2,512,128]{2,1,0:T(8,128)(2,1)S(1)}, bf16[2,512,128]{2,1,0:T(8,128)(2,1)S(1)}, u32[]{:S(2)}, u32[]{:S(2)}) collective-permute-start(bf16[2,512,128]{2,1,0:T(8,128)(2,1)S(1)} %collective-permute-done.refs_0_), channel_id=1, source_target_pairs={{0,8},{8,16},{16,24},{24,0},{32,40},{40,48},{48,56},{56,32},{1,9},... | collective-permute-start | bytes 786440 | tf_op jit(solution)/shard_map/ppermute | solution.py:54
  19.4 0.9 collective-permute-done.5.refs_1_
  20.3 1.3 %collective-permute-start.2 = (bf16[2,512,128]{2,1,0:T(8,128)(2,1)S(1)}, bf16[2,512,128]{2,1,0:T(8,128)(2,1)S(1)}, u32[]{:S(2)}, u32[]{:S(2)}) collective-permute-start(bf16[2,512,128]{2,1,0:T(8,128)(2,1)S(1)} %collective-permute-done.refs_0_), channel_id=1, source_target_pairs={{0,24},{8,0},{16,8},{24,16},{32,56},{40,32},{48,40},{56,48},{1,25}... | collective-permute-start | bytes 786440 | tf_op jit(solution)/shard_map/ppermute | solution.py:54
  21.6 0.9 collective-permute-start.3
  22.5 1.2 %copy-done = bf16[1,512,1024]{2,1,0:T(8,128)(2,1)S(1)} copy-done((bf16[1,512,1024]{2,1,0:T(8,128)(2,1)S(1)}, bf16[1,512,1024]{2,1,0:T(8,128)(2,1)}, u32[]{:S(2)}) %copy-start) | copy-done | bytes 1048600
  23.7 1.2 %copy-done.2 = bf16[1,512,1024]{2,1,0:T(8,128)(2,1)S(1)} copy-done((bf16[1,512,1024]{2,1,0:T(8,128)(2,1)S(1)}, bf16[1,512,1024]{2,1,0:T(8,128)(2,1)}, u32[]{:S(2)}) %copy-start.2) | copy-done | bytes 1048600
  24.9 0.9 copy-done.5
  25.9 1.8 %prepare.1 = (bf16[1024,512]{1,0:T(8,128)(2,1)S(1)}, bf16[1024,512]{1,0:T(8,128)(2,1)S(1)}, s32[1,512]{1,0:T(1,128)S(1)}, s32[1,512]{1,0:T(1,128)S(1)}, bf16[16,512]{1,0:T(8,128)(2,1)S(1)}) custom-call(s32[1]{0:T(128)S(6)} %copy.19.length_ref, bf16[512,1024]{1,0:T(8,128)(2,1)S(1)} %bitcast.8, bf16[512,1024]{1,0:T(8,128)(2,1)S(1)} %bitcast.11, ...), custom_call_target="tpu_custom_call" | custom-call | flops 1000 | bytes 1000 | tf_op jit(solution)/shard_map/prepare/pallas_call | solution.py:456
  27.6 0.0 collective-permute-done.7.refs_3_
  27.7 0.0 copy-start.8
  27.7 5.5 %near_terms.1 = (f32[2,2,512,128]{3,2,1,0:T(8,128)S(1)}, bf16[512,512]{1,0:T(8,128)(2,1)S(1)}, bf16[512,512]{1,0:T(8,128)(2,1)S(1)}) custom-call(s32[1]{0:T(128)S(6)} %copy.19.length_ref, bf16[2,2,512,128]{3,2,1,0:T(8,128)(2,1)S(1)} %copy-done.7, s32[32,32]{1,0:T(8,128)S(1)} %bitcast.14, bf16[4,1024,128]{2,1,0:T(8,128)(2,1)S(1)} %copy-done.4, ...), custom_call_target="tpu_custom_call" | custom-call | flops 1000 | bytes 1000 | tf_op jit(solution)/shard_map/near_terms/pallas_call | solution.py:274
  33.3 0.0 collective-permute-done.2.refs_1_
  33.3 4.9 %collective-permute-done.3.refs_2_ = bf16[2,512,128]{2,1,0:T(8,128)(2,1)S(1)} collective-permute-done((bf16[2,512,128]{2,1,0:T(8,128)(2,1)S(1)}, bf16[2,512,128]{2,1,0:T(8,128)(2,1)S(1)}, u32[]{:S(2)}, u32[]{:S(2)}) %collective-permute-start.3) | collective-permute-done | bytes 262176 | tf_op jit(solution)/shard_map/ppermute | solution.py:54
  38.2 5.7 %far_terms.1 = (bf16[528,512]{1,0:T(8,128)(2,1)S(1)}, bf16[16,320,128]{2,1,0:T(8,128)(2,1)}) custom-call(s32[1]{0:T(128)S(6)} %copy.19.length_ref, bf16[2,2,512,128]{3,2,1,0:T(8,128)(2,1)S(1)} %copy-done.7, s32[32,32]{1,0:T(8,128)S(1)} %bitcast.15, bf16[2,512,128]{2,1,0:T(8,128)(2,1)S(1)} %collective-permute-done.1.refs_0_, ...), custom_call_target="tpu_custom_call" | custom-call | flops 1000 | bytes 1000 | tf_op jit(solution)/shard_map/far_terms/pallas_call | solution.py:328
  44.0 4.1 %all-to-all-start.1 = ((bf16[16,320,128]{2,1,0:T(8,128)(2,1)}), bf16[16,320,128]{2,1,0:T(8,128)(2,1)S(1)}, u32[]{:S(2)}, u32[]{:S(2)}) async-start(bf16[16,320,128]{2,1,0:T(8,128)(2,1)} %get-tuple-element.197), calls=%async_computation.1 | async-start | bytes 2621440 | tf_op jit(solution)/shard_map/all_to_all | solution.py:37
  48.1 0.0 copy-start.1
  48.1 0.0 copy-start.3
  48.1 0.9 collective-permute-start.8
  49.0 1.6 %collective-permute-done.8.peer_ref = bf16[528,512]{1,0:T(8,128)(2,1)S(1)} collective-permute-done((bf16[528,512]{1,0:T(8,128)(2,1)S(1)}, bf16[528,512]{1,0:T(8,128)(2,1)S(1)}, u32[]{:S(2)}, u32[]{:S(2)}) %collective-permute-start.8) | collective-permute-done | bytes 540704 | tf_op jit(solution)/shard_map/ppermute | solution.py:62
  50.5 0.7 back_project.1
  51.3 2.8 %collective-permute-start.10 = (bf16[528,128]{1,0:T(8,128)(2,1)S(1)}, bf16[528,128]{1,0:T(8,128)(2,1)S(1)}, u32[]{:S(2)}, u32[]{:S(2)}) collective-permute-start(bf16[528,128]{1,0:T(8,128)(2,1)S(1)} %get-tuple-element.189), channel_id=1, source_target_pairs={{0,6},{1,7},{2,0},{3,1},{4,2},{5,3},{6,4},{7,5},{8,14},{9,15},{10,... | collective-permute-start | bytes 405512 | tf_op jit(solution)/shard_map/ppermute | solution.py:58
  54.1 0.3 collective-permute-start.11
  54.4 0.7 collective-permute-start.9
  55.1 4.3 %collective-permute-done.10.refs_2_ = bf16[528,128]{1,0:T(8,128)(2,1)S(1)} collective-permute-done((bf16[528,128]{1,0:T(8,128)(2,1)S(1)}, bf16[528,128]{1,0:T(8,128)(2,1)S(1)}, u32[]{:S(2)}, u32[]{:S(2)}) %collective-permute-start.10) | collective-permute-done | bytes 135200 | tf_op jit(solution)/shard_map/ppermute | solution.py:58
  59.4 0.6 collective-permute-done.11.refs_3_
  60.1 3.9 %collective-permute-done.9.refs_1_ = bf16[528,128]{1,0:T(8,128)(2,1)S(1)} collective-permute-done((bf16[528,128]{1,0:T(8,128)(2,1)S(1)}, bf16[528,128]{1,0:T(8,128)(2,1)S(1)}, u32[]{:S(2)}, u32[]{:S(2)}) %collective-permute-start.9) | collective-permute-done | bytes 135200 | tf_op jit(solution)/shard_map/ppermute | solution.py:58
  64.0 1.7 %input_grads.1 = (bf16[512,128]{1,0:T(8,128)(2,1)S(1)}, bf16[4,144,128]{2,1,0:T(8,128)(2,1)S(1)}, bf16[4,144,128]{2,1,0:T(8,128)(2,1)S(1)}, bf16[4,144,128]{2,1,0:T(8,128)(2,1)S(1)}, bf16[4,144,128]{2,1,0:T(8,128)(2,1)S(1)}) custom-call(s32[1]{0:T(128)S(6)} %copy.19.length_ref, bf16[528,128]{1,0:T(8,128)(2,1)S(1)} %get-tuple-element.187.refs_0_, ...), custom_call_target="tpu_custom_call" | custom-call | flops 1000 | bytes 1000 | tf_op jit(solution)/shard_map/input_grads/pallas_call | solution.py:578
  65.7 1.9 %collective-permute-start.12 = (bf16[4,144,128]{2,1,0:T(8,128)(2,1)S(1)}, bf16[4,144,128]{2,1,0:T(8,128)(2,1)S(1)}, u32[]{:S(2)}, u32[]{:S(2)}) collective-permute-start(bf16[4,144,128]{2,1,0:T(8,128)(2,1)S(1)} %get-tuple-element.194), channel_id=1, source_target_pairs={{0,8},{8,16},{16,24},{24,0},{64,72},{72,80},{80,88},{88,64},{32,40... | collective-permute-start | bytes 442376 | tf_op jit(solution)/shard_map/ppermute | solution.py:49
  67.6 1.3 %collective-permute-start.13 = (bf16[4,144,128]{2,1,0:T(8,128)(2,1)S(1)}, bf16[4,144,128]{2,1,0:T(8,128)(2,1)S(1)}, u32[]{:S(2)}, u32[]{:S(2)}) collective-permute-start(bf16[4,144,128]{2,1,0:T(8,128)(2,1)S(1)} %get-tuple-element.195), channel_id=1, source_target_pairs={{0,24},{8,0},{16,8},{24,16},{64,88},{72,64},{80,72},{88,80},{32,56... | collective-permute-start | bytes 442376 | tf_op jit(solution)/shard_map/ppermute | solution.py:49
  68.9 1.7 %collective-permute-start.14 = (bf16[4,144,128]{2,1,0:T(8,128)(2,1)S(1)}, bf16[4,144,128]{2,1,0:T(8,128)(2,1)S(1)}, u32[]{:S(2)}, u32[]{:S(2)}) collective-permute-start(bf16[4,144,128]{2,1,0:T(8,128)(2,1)S(1)} %get-tuple-element.196), channel_id=1, source_target_pairs={{0,16},{8,24},{16,0},{24,8},{64,80},{72,88},{80,64},{88,72},{32,48... | collective-permute-start | bytes 442376 | tf_op jit(solution)/shard_map/ppermute | solution.py:49
  70.6 1.3 %weight_sum.1 = bf16[16,320,128]{2,1,0:T(8,128)(2,1)} custom-call(bf16[16,320,128]{2,1,0:T(8,128)(2,1)S(1)} %all-to-all-done.1.parts_ref), custom_call_target="tpu_custom_call" | custom-call | flops 1000 | bytes 1000 | tf_op jit(solution)/shard_map/weight_sum/pallas_call | solution.py:433
  71.9 5.3 %all-to-all-start.2 = ((bf16[16,320,128]{2,1,0:T(8,128)(2,1)}), bf16[16,320,128]{2,1,0:T(8,128)(2,1)S(1)}, u32[]{:S(2)}, u32[]{:S(2)}) async-start(bf16[16,320,128]{2,1,0:T(8,128)(2,1)} %weight_sum.1), calls=%async_computation.2 | async-start | bytes 2621440 | tf_op jit(solution)/shard_map/all_to_all | solution.py:37
  77.2 0.0 collective-permute-done.13
  77.3 2.9 %collective-permute-start.17 = (bf16[4,144,128]{2,1,0:T(8,128)(2,1)S(1)}, bf16[4,144,128]{2,1,0:T(8,128)(2,1)S(1)}, u32[]{:S(2)}, u32[]{:S(2)}) collective-permute-start(bf16[4,144,128]{2,1,0:T(8,128)(2,1)S(1)} %pad_maximum_fusion.3), channel_id=1, source_target_pairs={{0,32},{8,40},{16,48},{24,56},{64,96},{72,104},{80,112},{88,120},{... | collective-permute-start | bytes 442376 | tf_op jit(solution)/shard_map/ppermute | solution.py:49
  80.3 1.0 collective-permute-start.16
  81.2 0.6 collective-permute-start.15
  81.9 15.1 %collective-permute-done.17.refs_3_ = bf16[4,144,128]{2,1,0:T(8,128)(2,1)S(1)} collective-permute-done((bf16[4,144,128]{2,1,0:T(8,128)(2,1)S(1)}, bf16[4,144,128]{2,1,0:T(8,128)(2,1)S(1)}, u32[]{:S(2)}, u32[]{:S(2)}) %collective-permute-start.17) | collective-permute-done | bytes 147488 | tf_op jit(solution)/shard_map/ppermute | solution.py:49
  97.0 1.8 %collective-permute-done.16.refs_2_ = bf16[4,144,128]{2,1,0:T(8,128)(2,1)S(1)} collective-permute-done((bf16[4,144,128]{2,1,0:T(8,128)(2,1)S(1)}, bf16[4,144,128]{2,1,0:T(8,128)(2,1)S(1)}, u32[]{:S(2)}, u32[]{:S(2)}) %collective-permute-start.16) | collective-permute-done | bytes 147488 | tf_op jit(solution)/shard_map/ppermute | solution.py:49
  98.8 3.0 %collective-permute-done.15.refs_1_ = bf16[4,144,128]{2,1,0:T(8,128)(2,1)S(1)} collective-permute-done((bf16[4,144,128]{2,1,0:T(8,128)(2,1)S(1)}, bf16[4,144,128]{2,1,0:T(8,128)(2,1)S(1)}, u32[]{:S(2)}, u32[]{:S(2)}) %collective-permute-start.15) | collective-permute-done | bytes 147488 | tf_op jit(solution)/shard_map/ppermute | solution.py:49
  101.7 3.3 %finish.1 = (f32[4,1024,128]{2,1,0:T(8,128)}, f32[128,1024]{1,0:T(8,128)}, f32[1024,128]{1,0:T(8,128)}, f32[1,128]{1,0:T(1,128)}, s32[1]{0:T(128)}) custom-call(bf16[4,144,128]{2,1,0:T(8,128)(2,1)S(1)} %pad_maximum_fusion.refs_0_, bf16[4,144,128]{2,1,0:T(8,128)(2,1)S(1)} %collective-permute-done.15.refs_1_, ...), custom_call_target="tpu_custom_call" | custom-call | flops 1000 | bytes 1000 | tf_op jit(solution)/shard_map/finish/pallas_call | solution.py:654
  105.0 0.6 while.13
  (40 shorter events, 0.2 us)
Async XLA Ops:
  0.6 27.0 %collective-permute-start.4 = (bf16[4,1024,128]{2,1,0:T(8,128)(2,1)}, bf16[4,1024,128]{2,1,0:T(8,128)(2,1)}, u32[]{:S(2)}, u32[]{:S(2)}) collective-permute-start(bf16[4,1024,128]{2,1,0:T(8,128)(2,1)} %proj_own_ref.1), channel_id=1, source_target_pairs={{0,1},{1,0},{2,3},{3,2},{4,5},{5,4},{6,7},{7,6},{8,9},{9,8},{10,11... | collective-permute-start | bytes 3145736 | tf_op jit(solution)/shard_map/ppermute | solution.py:62
  2.8 19.7 %copy-start.13 = (f32[1024]{0:T(1024)S(1)}, f32[1024]{0:T(1024)}, u32[]{:S(2)}) copy-start(f32[1024]{0:T(1024)} %param.12) | copy-start | bytes 12292
  2.8 19.7 %copy-start.16 = (s32[1,512]{1,0:T(1,128)S(1)}, s32[1,512]{1,0:T(1,128)}, u32[]{:S(2)}) copy-start(s32[1,512]{1,0:T(1,128)} %id_ref.1) | copy-start | bytes 6148
  2.8 24.9 %copy-start.11 = (s32[1,32,32]{2,1,0:T(8,128)S(1)}, s32[1,32,32]{2,1,0:T(8,128)}, u32[]{:S(2)}) copy-start(s32[1,32,32]{2,1,0:T(8,128)} %param.17) | copy-start | bytes 12292
  7.5 10.6 %collective-permute-start = (bf16[2,512,128]{2,1,0:T(8,128)(2,1)}, bf16[2,512,128]{2,1,0:T(8,128)(2,1)S(1)}, u32[]{:S(2)}, u32[]{:S(2)}) collective-permute-start(bf16[2,512,128]{2,1,0:T(8,128)(2,1)} %get-tuple-element.169), channel_id=1, source_target_pairs={{0,32},{8,40},{16,48},{24,56},{32,0},{40,8},{48,16},{56,24},{1,33}... | collective-permute-start | bytes 786440 | tf_op jit(solution)/shard_map/ppermute | solution.py:54
  11.3 9.0 %collective-permute-start.5 = (bf16[2,512,128]{2,1,0:T(8,128)(2,1)}, bf16[2,512,128]{2,1,0:T(8,128)(2,1)S(1)}, u32[]{:S(2)}, u32[]{:S(2)}) collective-permute-start(bf16[2,512,128]{2,1,0:T(8,128)(2,1)} %get-tuple-element.171), channel_id=1, source_target_pairs={{0,8},{8,16},{16,24},{24,0},{32,40},{40,48},{48,56},{56,32},{1,9},... | collective-permute-start | bytes 786440 | tf_op jit(solution)/shard_map/ppermute | solution.py:54
  12.5 9.1 %collective-permute-start.6 = (bf16[2,512,128]{2,1,0:T(8,128)(2,1)}, bf16[2,512,128]{2,1,0:T(8,128)(2,1)S(1)}, u32[]{:S(2)}, u32[]{:S(2)}) collective-permute-start(bf16[2,512,128]{2,1,0:T(8,128)(2,1)} %get-tuple-element.172), channel_id=1, source_target_pairs={{0,24},{8,0},{16,8},{24,16},{32,56},{40,32},{48,40},{56,48},{1,25}... | collective-permute-start | bytes 786440 | tf_op jit(solution)/shard_map/ppermute | solution.py:54
  14.0 13.7 %collective-permute-start.7 = (bf16[2,512,128]{2,1,0:T(8,128)(2,1)}, bf16[2,512,128]{2,1,0:T(8,128)(2,1)S(1)}, u32[]{:S(2)}, u32[]{:S(2)}) collective-permute-start(bf16[2,512,128]{2,1,0:T(8,128)(2,1)} %get-tuple-element.173), channel_id=1, source_target_pairs={{0,16},{8,24},{16,0},{24,8},{32,48},{40,56},{48,32},{56,40},{1,17}... | collective-permute-start | bytes 786440 | tf_op jit(solution)/shard_map/ppermute | solution.py:54
  18.2 15.1 %collective-permute-start.1 = (bf16[2,512,128]{2,1,0:T(8,128)(2,1)S(1)}, bf16[2,512,128]{2,1,0:T(8,128)(2,1)S(1)}, u32[]{:S(2)}, u32[]{:S(2)}) collective-permute-start(bf16[2,512,128]{2,1,0:T(8,128)(2,1)S(1)} %collective-permute-done.refs_0_), channel_id=1, source_target_pairs={{0,8},{8,16},{16,24},{24,0},{32,40},{40,48},{48,56},{56,32},{1,9},... | collective-permute-start | bytes 786440 | tf_op jit(solution)/shard_map/ppermute | solution.py:54
  20.3 13.0 %collective-permute-start.2 = (bf16[2,512,128]{2,1,0:T(8,128)(2,1)S(1)}, bf16[2,512,128]{2,1,0:T(8,128)(2,1)S(1)}, u32[]{:S(2)}, u32[]{:S(2)}) collective-permute-start(bf16[2,512,128]{2,1,0:T(8,128)(2,1)S(1)} %collective-permute-done.refs_0_), channel_id=1, source_target_pairs={{0,24},{8,0},{16,8},{24,16},{32,56},{40,32},{48,40},{56,48},{1,25}... | collective-permute-start | bytes 786440 | tf_op jit(solution)/shard_map/ppermute | solution.py:54
  21.6 16.6 %collective-permute-start.3 = (bf16[2,512,128]{2,1,0:T(8,128)(2,1)S(1)}, bf16[2,512,128]{2,1,0:T(8,128)(2,1)S(1)}, u32[]{:S(2)}, u32[]{:S(2)}) collective-permute-start(bf16[2,512,128]{2,1,0:T(8,128)(2,1)S(1)} %collective-permute-done.refs_0_), channel_id=1, source_target_pairs={{0,16},{8,24},{16,0},{24,8},{32,48},{40,56},{48,32},{56,40},{1,17}... | collective-permute-start | bytes 786440 | tf_op jit(solution)/shard_map/ppermute | solution.py:54
  22.5 1.2 %copy-start = (bf16[1,512,1024]{2,1,0:T(8,128)(2,1)S(1)}, bf16[1,512,1024]{2,1,0:T(8,128)(2,1)}, u32[]{:S(2)}) copy-start(bf16[1,512,1024]{2,1,0:T(8,128)(2,1)} %param.10) | copy-start | bytes 3145732
  23.7 1.2 %copy-start.2 = (bf16[1,512,1024]{2,1,0:T(8,128)(2,1)S(1)}, bf16[1,512,1024]{2,1,0:T(8,128)(2,1)}, u32[]{:S(2)}) copy-start(bf16[1,512,1024]{2,1,0:T(8,128)(2,1)} %param.11) | copy-start | bytes 3145732
  24.9 0.9 copy-start.5
  25.9 1.8 %copy-start.4 = (bf16[4,1024,128]{2,1,0:T(8,128)(2,1)S(1)}, bf16[4,1024,128]{2,1,0:T(8,128)(2,1)}, u32[]{:S(2)}) copy-start(bf16[4,1024,128]{2,1,0:T(8,128)(2,1)} %proj_own_ref.1) | copy-start | bytes 3145732
  25.9 1.8 %copy-start.7 = (bf16[2,2,512,128]{3,2,1,0:T(8,128)(2,1)S(1)}, bf16[2,2,512,128]{3,2,1,0:T(8,128)(2,1)}, u32[]{:S(2)}) copy-start(bf16[2,2,512,128]{3,2,1,0:T(8,128)(2,1)} %get-tuple-element.168.own_ref) | copy-start | bytes 1572868
  27.7 10.5 %copy-start.6 = (f32[512,128]{1,0:T(8,128)S(1)}, f32[512,128]{1,0:T(8,128)}, u32[]{:S(2)}) copy-start(f32[512,128]{1,0:T(8,128)} %get-tuple-element.176.inv_rms_ref.refs_5_.refs_7_) | copy-start | bytes 786436
  27.7 10.5 %copy-start.8 = (f32[4,512,128]{2,1,0:T(8,128)S(1)}, f32[4,512,128]{2,1,0:T(8,128)}, u32[]{:S(2)}) copy-start(f32[4,512,128]{2,1,0:T(8,128)} %get-tuple-element.175.refs_4_) | copy-start | bytes 3145732
  27.7 10.5 %copy-start.9 = (f32[512,128]{1,0:T(8,128)S(1)}, f32[512,128]{1,0:T(8,128)}, u32[]{:S(2)}) copy-start(f32[512,128]{1,0:T(8,128)} %get-tuple-element.177.refs_6_) | copy-start | bytes 786436
  27.7 10.5 %copy-start.10 = (f32[512,128]{1,0:T(8,128)S(1)}, f32[512,128]{1,0:T(8,128)}, u32[]{:S(2)}) copy-start(f32[512,128]{1,0:T(8,128)} %get-tuple-element.179.refs_8_) | copy-start | bytes 786436
  27.7 10.5 %copy-start.12 = (bf16[512,128]{1,0:T(8,128)(2,1)S(1)}, bf16[512,128]{1,0:T(8,128)(2,1)}, u32[]{:S(2)}) copy-start(bf16[512,128]{1,0:T(8,128)(2,1)} %get-tuple-element.178.refs_7_) | copy-start | bytes 393220
  44.0 26.6 %all-to-all-start.1 = ((bf16[16,320,128]{2,1,0:T(8,128)(2,1)}), bf16[16,320,128]{2,1,0:T(8,128)(2,1)S(1)}, u32[]{:S(2)}, u32[]{:S(2)}) async-start(bf16[16,320,128]{2,1,0:T(8,128)(2,1)} %get-tuple-element.197), calls=%async_computation.1 | async-start | bytes 2621440 | tf_op jit(solution)/shard_map/all_to_all | solution.py:37
  48.1 15.9 %copy-start.1 = (bf16[1,512,1024]{2,1,0:T(8,128)(2,1)S(1)}, bf16[1,512,1024]{2,1,0:T(8,128)(2,1)}, u32[]{:S(2)}) copy-start(bf16[1,512,1024]{2,1,0:T(8,128)(2,1)} %param.10) | copy-start | bytes 3145732
  48.1 15.9 %copy-start.3 = (bf16[1,512,1024]{2,1,0:T(8,128)(2,1)S(1)}, bf16[1,512,1024]{2,1,0:T(8,128)(2,1)}, u32[]{:S(2)}) copy-start(bf16[1,512,1024]{2,1,0:T(8,128)(2,1)} %param.11) | copy-start | bytes 3145732
  48.1 2.4 %collective-permute-start.8 = (bf16[528,512]{1,0:T(8,128)(2,1)S(1)}, bf16[528,512]{1,0:T(8,128)(2,1)S(1)}, u32[]{:S(2)}, u32[]{:S(2)}) collective-permute-start(bf16[528,512]{1,0:T(8,128)(2,1)S(1)} %get-tuple-element.184.own_ref), channel_id=1, source_target_pairs={{0,1},{1,0},{2,3},{3,2},{4,5},{5,4},{6,7},{7,6},{8,9},{9,8},{10,11... | collective-permute-start | bytes 1622024 | tf_op jit(solution)/shard_map/ppermute | solution.py:62
  51.3 8.2 %collective-permute-start.10 = (bf16[528,128]{1,0:T(8,128)(2,1)S(1)}, bf16[528,128]{1,0:T(8,128)(2,1)S(1)}, u32[]{:S(2)}, u32[]{:S(2)}) collective-permute-start(bf16[528,128]{1,0:T(8,128)(2,1)S(1)} %get-tuple-element.189), channel_id=1, source_target_pairs={{0,6},{1,7},{2,0},{3,1},{4,2},{5,3},{6,4},{7,5},{8,14},{9,15},{10,... | collective-permute-start | bytes 405512 | tf_op jit(solution)/shard_map/ppermute | solution.py:58
  54.1 6.0 %collective-permute-start.11 = (bf16[528,128]{1,0:T(8,128)(2,1)S(1)}, bf16[528,128]{1,0:T(8,128)(2,1)S(1)}, u32[]{:S(2)}, u32[]{:S(2)}) collective-permute-start(bf16[528,128]{1,0:T(8,128)(2,1)S(1)} %get-tuple-element.190), channel_id=1, source_target_pairs={{0,4},{1,5},{2,6},{3,7},{4,0},{5,1},{6,2},{7,3},{8,12},{9,13},{10,... | collective-permute-start | bytes 405512 | tf_op jit(solution)/shard_map/ppermute | solution.py:58
  54.4 9.6 %collective-permute-start.9 = (bf16[528,128]{1,0:T(8,128)(2,1)S(1)}, bf16[528,128]{1,0:T(8,128)(2,1)S(1)}, u32[]{:S(2)}, u32[]{:S(2)}) collective-permute-start(bf16[528,128]{1,0:T(8,128)(2,1)S(1)} %get-tuple-element.188), channel_id=1, source_target_pairs={{0,2},{1,3},{2,4},{3,5},{4,6},{5,7},{6,0},{7,1},{8,10},{9,11},{10,... | collective-permute-start | bytes 405512 | tf_op jit(solution)/shard_map/ppermute | solution.py:58
  65.7 11.5 %collective-permute-start.12 = (bf16[4,144,128]{2,1,0:T(8,128)(2,1)S(1)}, bf16[4,144,128]{2,1,0:T(8,128)(2,1)S(1)}, u32[]{:S(2)}, u32[]{:S(2)}) collective-permute-start(bf16[4,144,128]{2,1,0:T(8,128)(2,1)S(1)} %get-tuple-element.194), channel_id=1, source_target_pairs={{0,8},{8,16},{16,24},{24,0},{64,72},{72,80},{80,88},{88,64},{32,40... | collective-permute-start | bytes 442376 | tf_op jit(solution)/shard_map/ppermute | solution.py:49
  67.6 9.6 %collective-permute-start.13 = (bf16[4,144,128]{2,1,0:T(8,128)(2,1)S(1)}, bf16[4,144,128]{2,1,0:T(8,128)(2,1)S(1)}, u32[]{:S(2)}, u32[]{:S(2)}) collective-permute-start(bf16[4,144,128]{2,1,0:T(8,128)(2,1)S(1)} %get-tuple-element.195), channel_id=1, source_target_pairs={{0,24},{8,0},{16,8},{24,16},{64,88},{72,64},{80,72},{88,80},{32,56... | collective-permute-start | bytes 442376 | tf_op jit(solution)/shard_map/ppermute | solution.py:49
  68.9 8.3 %collective-permute-start.14 = (bf16[4,144,128]{2,1,0:T(8,128)(2,1)S(1)}, bf16[4,144,128]{2,1,0:T(8,128)(2,1)S(1)}, u32[]{:S(2)}, u32[]{:S(2)}) collective-permute-start(bf16[4,144,128]{2,1,0:T(8,128)(2,1)S(1)} %get-tuple-element.196), channel_id=1, source_target_pairs={{0,16},{8,24},{16,0},{24,8},{64,80},{72,88},{80,64},{88,72},{32,48... | collective-permute-start | bytes 442376 | tf_op jit(solution)/shard_map/ppermute | solution.py:49
  71.9 29.9 %all-to-all-start.2 = ((bf16[16,320,128]{2,1,0:T(8,128)(2,1)}), bf16[16,320,128]{2,1,0:T(8,128)(2,1)S(1)}, u32[]{:S(2)}, u32[]{:S(2)}) async-start(bf16[16,320,128]{2,1,0:T(8,128)(2,1)} %weight_sum.1), calls=%async_computation.2 | async-start | bytes 2621440 | tf_op jit(solution)/shard_map/all_to_all | solution.py:37
  77.3 19.7 %collective-permute-start.17 = (bf16[4,144,128]{2,1,0:T(8,128)(2,1)S(1)}, bf16[4,144,128]{2,1,0:T(8,128)(2,1)S(1)}, u32[]{:S(2)}, u32[]{:S(2)}) collective-permute-start(bf16[4,144,128]{2,1,0:T(8,128)(2,1)S(1)} %pad_maximum_fusion.3), channel_id=1, source_target_pairs={{0,32},{8,40},{16,48},{24,56},{64,96},{72,104},{80,112},{88,120},{... | collective-permute-start | bytes 442376 | tf_op jit(solution)/shard_map/ppermute | solution.py:49
  80.3 18.5 %collective-permute-start.16 = (bf16[4,144,128]{2,1,0:T(8,128)(2,1)S(1)}, bf16[4,144,128]{2,1,0:T(8,128)(2,1)S(1)}, u32[]{:S(2)}, u32[]{:S(2)}) collective-permute-start(bf16[4,144,128]{2,1,0:T(8,128)(2,1)S(1)} %pad_maximum_fusion.2), channel_id=1, source_target_pairs={{0,96},{8,104},{16,112},{24,120},{64,0},{72,8},{80,16},{88,24},{32... | collective-permute-start | bytes 442376 | tf_op jit(solution)/shard_map/ppermute | solution.py:49
  81.2 20.5 %collective-permute-start.15 = (bf16[4,144,128]{2,1,0:T(8,128)(2,1)S(1)}, bf16[4,144,128]{2,1,0:T(8,128)(2,1)S(1)}, u32[]{:S(2)}, u32[]{:S(2)}) collective-permute-start(bf16[4,144,128]{2,1,0:T(8,128)(2,1)S(1)} %pad_maximum_fusion.1), channel_id=1, source_target_pairs={{0,64},{8,72},{16,80},{24,88},{64,32},{72,40},{80,48},{88,56},{32,... | collective-permute-start | bytes 442376 | tf_op jit(solution)/shard_map/ppermute | solution.py:49

commit v4 on v3

--- a/solution.py
+++ b/solution.py
@@ -619,60 +619,54 @@
     return total
 
 
-def finish_body(*refs):
-    gots, whole_ref, (in_ref, out_ref, table_out, gain_ref, rounds_ref, table_ref, sems) = refs[:4], refs[4], refs[5:]
-    step = pl.program_id(0)
-    count, (_, rows, col) = table_ref.shape[1], whole_ref.shape
+def place_body(whole_ref, in_ref, out_ref):
+    count, rows, col = whole_ref.shape
     share = rows // 5
     lasts = []
-    for index in range(whole_ref.shape[0]):
+    for index in range(count):
         for c in range(4):
             in_ref[c, pl.ds(index * share, share), :] = whole_ref[index, pl.ds(c * share, share), :].astype(F32)
         lasts.append(whole_ref[index, pl.ds(4 * share, share), :].astype(F32))
     out_ref[...] = jnp.concatenate(lasts, axis=0).T
+
+
+def place_weights(whole):
+    owners, rows, col = whole.shape
+    width, steps = 8 * col, 2
+    return kernel_call(
+        place_body,
+        (shape_of((4, width, col), F32), shape_of((col, width), F32)),
+        "place_weights",
+        grid=(steps,),
+        in_specs=[pl.BlockSpec((owners // steps, rows, col), lambda i: (i, 0, 0))],
+        out_specs=[
+            pl.BlockSpec((4, width // steps, col), lambda i: (0, i, 0)),
+            pl.BlockSpec((col, width // steps), lambda i: (0, i)),
+        ],
+    )(whole)
+
+
+def table_body(*refs):
+    gots, (table_ref, gain_ref, rounds_ref) = refs[:4], refs[4:]
+    count = 2 * BLOCK
     blocks = [got.at[index] for got in gots for index in range(got.shape[0])]
-    table_ref[step] = rows_total(blocks, step * count, count)
-
-    def leaving(index):
-        return pltpu.make_async_copy(table_ref.at[index], table_out.at[pl.ds(index * count, count)], sems.at[index])
-
-    leaving(step).start()
+    for first in range(0, table_ref.shape[0], count):
+        table_ref[pl.ds(first, count), :] = rows_total(blocks, first, count)
     extra = [block[pl.ds(BLOCK, EXTRA), :].astype(F32) for block in blocks]
     total = functools.reduce(lambda a, b: a + b, extra)
     gain_ref[...] = total[0:1] + total[1:2]
     rounds_ref[0] = jnp.max(functools.reduce(jnp.maximum, extra)[4:5]).astype(jnp.int32)
 
-    @pl.when(step == pl.num_programs(0) - 1)
-    def _():
-        for index in range(table_ref.shape[0]):
-            leaving(index).wait()
-
-
-def finish(gots, whole, items):
-    owners, rows, col = whole.shape
-    width, steps = 8 * col, 2
+
+def table_grads(gots, items):
+    col = gots[0].shape[2]
+    whole = pl.BlockSpec(memory_space=pltpu.VMEM)
     return kernel_call(
-        finish_body,
-        (
-            shape_of((4, width, col), F32),
-            shape_of((col, width), F32),
-            shape_of((items, col), F32),
-            shape_of((1, col), F32),
-            shape_of((1,), jnp.int32),
-        ),
-        "finish",
-        grid=(steps,),
-        in_specs=[pl.BlockSpec(got.shape, lambda i: (0, 0, 0)) for got in gots]
-        + [pl.BlockSpec((owners // steps, rows, col), lambda i: (i, 0, 0))],
-        out_specs=[
-            pl.BlockSpec((4, width // steps, col), lambda i: (0, i, 0)),
-            pl.BlockSpec((col, width // steps), lambda i: (0, i)),
-            pl.BlockSpec(memory_space=pltpu.HBM),
-            pl.BlockSpec((1, col), lambda i: (0, 0)),
-            pl.BlockSpec(memory_space=pltpu.SMEM),
-        ],
-        scratch_shapes=[pltpu.VMEM((steps, items // steps, col), F32), pltpu.SemaphoreType.DMA((steps,))],
-    )(*gots, whole)
+        table_body,
+        (shape_of((items, col), F32), shape_of((1, col), F32), shape_of((1,), jnp.int32)),
+        "table_grads",
+        out_specs=[whole, whole, pl.BlockSpec(memory_space=pltpu.SMEM)],
+    )(*gots)
 
 
 def more_table_body(got_ref, table_ref, out_ref):
@@ -721,7 +715,9 @@
     line = [sends[0]] + [move_plane(sends[k], 0, k) for k in (1, 3, 2)]
     sends = [jnp.stack([block[k] for block in line]) for k in range(4)]
     gots = [sends[0]] + [move_plane(sends[k], k, 0) for k in (1, 3, 2)]
-    grad_in_w, grad_out_w, table, gain, rounds = finish(gots, swap_plane(weight_sum(shares)), items)
+    grad_in_w, grad_out_w = place_weights(swap_plane(weight_sum(shares)))
+    grad_out_w, *gots = lax.optimization_barrier((grad_out_w, *gots))
+    table, gain, rounds = table_grads(gots, items)
 
     def another(state):
         turn, total = state

time: 106 us -> 105 us (level)
  waiting for transfers between devices: 38.8 us -> 37.2 us
    ppermute x6, waiting for transfers between devices: 19.8 us -> 3.78 us  [move_plane(): return lax.ppermute(value, ('dp', 'seq'), pairs)]
    all_to_all x2, waiting for transfers between devices: 0.01 us -> 14.5 us  [swap_plane(): return lax.all_to_all(value, ('dp', 'seq'), 0, 0, tiled=True)]
    pallas_call x1 -> x2, Pallas kernels: 3.25 us -> 3.64 us  [the longest x1 2.05 us: table_grads(): kernel_call(table_body, (shape_of((items, col), F32), shape_of((1, col),...]
  transfers between devices with their start and end apart: 20 -> 20, of which waited for: 10 -> 10; matrix products, arithmetic and copies ran while one was open for 0% -> 0% of each run, Pallas kernels for 15% -> 16%
where the time goes in v4:
time: 105 us
  waiting for transfers between devices  37.2 us (35%)
  starting transfers between devices  36.4 us (35%)
  Pallas kernels  25 us (24%)
  local copies, waits for them, and re-layouts  3.5 us (3%)
  between operations  1.78 us (2%)
    all_to_all x2, waiting for transfers between devices, swap_plane(): return lax.all_to_all(value, ('dp', 'seq'), 0, 0, tiled=True)  14.5 us
    ppermute x7, starting transfers between devices, move_seq(): return lax.ppermute(value, 'seq', pairs)  11.3 us
    ppermute x6, starting transfers between devices, move_plane(): return lax.ppermute(value, ('dp', 'seq'), pairs)  9.45 us
    all_to_all x2, starting transfers between devices, swap_plane(): return lax.all_to_all(value, ('dp', 'seq'), 0, 0, tiled=True)  9.39 us
    ppermute x3, waiting for transfers between devices, move_y(): lax.ppermute(value, 'col', [(i, (i // 2 + dy) % 4 * 2 + i % 2) for i in r...  8.86 us
    ppermute x7, waiting for transfers between devices, move_seq(): return lax.ppermute(value, 'seq', pairs)  8.52 us
    pallas_call x1, Pallas kernels, far_terms(): kernel_call(functools.partial(far_body, scale=scale), (shape_of((tok + EX...  5.72 us
    pallas_call x1, Pallas kernels, near_terms(): kernel_call(functools.partial(near_body, scale=scale), (shape_of(own.shap...  5.52 us
  transfers between devices with their start and end apart: 20, of which 10 were waited for; matrix products, arithmetic and copies ran while one was open for 0% of the time, Pallas kernels for 16%

profile of v4, /device:TPU:1, one launch (start us, length us, event | category | flops | bytes accessed | tf_op | source)
XLA Modules:
  0.0 104.6 jit_solution(4878975569926280856)
XLA Ops:
  0.6 1.5 %collective-permute-start.4 = (bf16[4,1024,128]{2,1,0:T(8,128)(2,1)}, bf16[4,1024,128]{2,1,0:T(8,128)(2,1)}, u32[]{:S(2)}, u32[]{:S(2)}) collective-permute-start(bf16[4,1024,128]{2,1,0:T(8,128)(2,1)} %proj_own_ref.1), channel_id=1, source_target_pairs={{0,1},{1,0},{2,3},{3,2},{4,5},{5,4},{6,7},{7,6},{8,9},{9,8},{10,11... | collective-permute-start | bytes 3145736 | tf_op jit(solution)/shard_map/ppermute | solution.py:62
  2.8 4.7 %project.1 = (bf16[2,2,512,128]{3,2,1,0:T(8,128)(2,1)}, bf16[2,512,128]{2,1,0:T(8,128)(2,1)}, bf16[2,512,128]{2,1,0:T(8,128)(2,1)}, bf16[2,512,128]{2,1,0:T(8,12...) custom-call(s32[1]{0:T(128)S(6)} %copy.19.length_ref, ...), custom_call_target="tpu_custom_call" | custom-call | flops 1000 | bytes 1000 | tf_op jit(solution)/shard_map/project/pallas_call | solution.py:130
  7.5 3.8 %collective-permute-start = (bf16[2,512,128]{2,1,0:T(8,128)(2,1)}, bf16[2,512,128]{2,1,0:T(8,128)(2,1)S(1)}, u32[]{:S(2)}, u32[]{:S(2)}) collective-permute-start(bf16[2,512,128]{2,1,0:T(8,128)(2,1)} %get-tuple-element.174), channel_id=1, source_target_pairs={{0,32},{8,40},{16,48},{24,56},{32,0},{40,8},{48,16},{56,24},{1,33}... | collective-permute-start | bytes 786440 | tf_op jit(solution)/shard_map/ppermute | solution.py:54
  11.3 1.2 %collective-permute-start.5 = (bf16[2,512,128]{2,1,0:T(8,128)(2,1)}, bf16[2,512,128]{2,1,0:T(8,128)(2,1)S(1)}, u32[]{:S(2)}, u32[]{:S(2)}) collective-permute-start(bf16[2,512,128]{2,1,0:T(8,128)(2,1)} %get-tuple-element.176), channel_id=1, source_target_pairs={{0,8},{8,16},{16,24},{24,0},{32,40},{40,48},{48,56},{56,32},{1,9},... | collective-permute-start | bytes 786440 | tf_op jit(solution)/shard_map/ppermute | solution.py:54
  12.5 1.5 %collective-permute-start.6 = (bf16[2,512,128]{2,1,0:T(8,128)(2,1)}, bf16[2,512,128]{2,1,0:T(8,128)(2,1)S(1)}, u32[]{:S(2)}, u32[]{:S(2)}) collective-permute-start(bf16[2,512,128]{2,1,0:T(8,128)(2,1)} %get-tuple-element.177), channel_id=1, source_target_pairs={{0,24},{8,0},{16,8},{24,16},{32,56},{40,32},{48,40},{56,48},{1,25}... | collective-permute-start | bytes 786440 | tf_op jit(solution)/shard_map/ppermute | solution.py:54
  13.9 1.5 %collective-permute-start.7 = (bf16[2,512,128]{2,1,0:T(8,128)(2,1)}, bf16[2,512,128]{2,1,0:T(8,128)(2,1)S(1)}, u32[]{:S(2)}, u32[]{:S(2)}) collective-permute-start(bf16[2,512,128]{2,1,0:T(8,128)(2,1)} %get-tuple-element.178), channel_id=1, source_target_pairs={{0,16},{8,24},{16,0},{24,8},{32,48},{40,56},{48,32},{56,40},{1,17}... | collective-permute-start | bytes 786440 | tf_op jit(solution)/shard_map/ppermute | solution.py:54
  15.5 2.7 %collective-permute-done.refs_0_ = bf16[2,512,128]{2,1,0:T(8,128)(2,1)S(1)} collective-permute-done((bf16[2,512,128]{2,1,0:T(8,128)(2,1)}, bf16[2,512,128]{2,1,0:T(8,128)(2,1)S(1)}, u32[]{:S(2)}, u32[]{:S(2)}) %collective-permute-start) | collective-permute-done | bytes 262176 | tf_op jit(solution)/shard_map/ppermute | solution.py:54
  18.1 1.2 %collective-permute-start.1 = (bf16[2,512,128]{2,1,0:T(8,128)(2,1)S(1)}, bf16[2,512,128]{2,1,0:T(8,128)(2,1)S(1)}, u32[]{:S(2)}, u32[]{:S(2)}) collective-permute-start(bf16[2,512,128]{2,1,0:T(8,128)(2,1)S(1)} %collective-permute-done.refs_0_), channel_id=1, source_target_pairs={{0,8},{8,16},{16,24},{24,0},{32,40},{40,48},{48,56},{56,32},{1,9},... | collective-permute-start | bytes 786440 | tf_op jit(solution)/shard_map/ppermute | solution.py:54
  19.4 0.9 collective-permute-done.5.refs_1_
  20.3 1.3 %collective-permute-start.2 = (bf16[2,512,128]{2,1,0:T(8,128)(2,1)S(1)}, bf16[2,512,128]{2,1,0:T(8,128)(2,1)S(1)}, u32[]{:S(2)}, u32[]{:S(2)}) collective-permute-start(bf16[2,512,128]{2,1,0:T(8,128)(2,1)S(1)} %collective-permute-done.refs_0_), channel_id=1, source_target_pairs={{0,24},{8,0},{16,8},{24,16},{32,56},{40,32},{48,40},{56,48},{1,25}... | collective-permute-start | bytes 786440 | tf_op jit(solution)/shard_map/ppermute | solution.py:54
  21.6 0.0 collective-permute-done.6.refs_2_
  21.6 0.9 collective-permute-start.3
  22.4 1.2 %copy-done = bf16[1,512,1024]{2,1,0:T(8,128)(2,1)S(1)} copy-done((bf16[1,512,1024]{2,1,0:T(8,128)(2,1)S(1)}, bf16[1,512,1024]{2,1,0:T(8,128)(2,1)}, u32[]{:S(2)}) %copy-start) | copy-done | bytes 1048600
  23.7 1.2 %copy-done.2 = bf16[1,512,1024]{2,1,0:T(8,128)(2,1)S(1)} copy-done((bf16[1,512,1024]{2,1,0:T(8,128)(2,1)S(1)}, bf16[1,512,1024]{2,1,0:T(8,128)(2,1)}, u32[]{:S(2)}) %copy-start.2) | copy-done | bytes 1048600
  24.9 0.9 copy-done.5
  25.8 1.8 %prepare.1 = (bf16[1024,512]{1,0:T(8,128)(2,1)S(1)}, bf16[1024,512]{1,0:T(8,128)(2,1)S(1)}, s32[1,512]{1,0:T(1,128)S(1)}, s32[1,512]{1,0:T(1,128)S(1)}, bf16[16,512]{1,0:T(8,128)(2,1)S(1)}) custom-call(s32[1]{0:T(128)S(6)} %copy.19.length_ref, bf16[512,1024]{1,0:T(8,128)(2,1)S(1)} %bitcast.8, bf16[512,1024]{1,0:T(8,128)(2,1)S(1)} %bitcast.11, ...), custom_call_target="tpu_custom_call" | custom-call | flops 1000 | bytes 1000 | tf_op jit(solution)/shard_map/prepare/pallas_call | solution.py:456
  27.6 0.0 collective-permute-done.7.refs_3_
  27.7 0.0 copy-start.8
  27.7 5.5 %near_terms.1 = (f32[2,2,512,128]{3,2,1,0:T(8,128)S(1)}, bf16[512,512]{1,0:T(8,128)(2,1)S(1)}, bf16[512,512]{1,0:T(8,128)(2,1)S(1)}) custom-call(s32[1]{0:T(128)S(6)} %copy.19.length_ref, bf16[2,2,512,128]{3,2,1,0:T(8,128)(2,1)S(1)} %copy-done.7, s32[32,32]{1,0:T(8,128)S(1)} %bitcast.14, bf16[4,1024,128]{2,1,0:T(8,128)(2,1)S(1)} %copy-done.4, ...), custom_call_target="tpu_custom_call" | custom-call | flops 1000 | bytes 1000 | tf_op jit(solution)/shard_map/near_terms/pallas_call | solution.py:274
  33.3 4.9 %collective-permute-done.3.refs_2_ = bf16[2,512,128]{2,1,0:T(8,128)(2,1)S(1)} collective-permute-done((bf16[2,512,128]{2,1,0:T(8,128)(2,1)S(1)}, bf16[2,512,128]{2,1,0:T(8,128)(2,1)S(1)}, u32[]{:S(2)}, u32[]{:S(2)}) %collective-permute-start.3) | collective-permute-done | bytes 262176 | tf_op jit(solution)/shard_map/ppermute | solution.py:54
  38.2 5.7 %far_terms.1 = (bf16[528,512]{1,0:T(8,128)(2,1)S(1)}, bf16[16,320,128]{2,1,0:T(8,128)(2,1)}) custom-call(s32[1]{0:T(128)S(6)} %copy.19.length_ref, bf16[2,2,512,128]{3,2,1,0:T(8,128)(2,1)S(1)} %copy-done.7, s32[32,32]{1,0:T(8,128)S(1)} %bitcast.15, bf16[2,512,128]{2,1,0:T(8,128)(2,1)S(1)} %collective-permute-done.1.refs_0_, ...), custom_call_target="tpu_custom_call" | custom-call | flops 1000 | bytes 1000 | tf_op jit(solution)/shard_map/far_terms/pallas_call | solution.py:328
  43.9 4.1 %all-to-all-start.1 = ((bf16[16,320,128]{2,1,0:T(8,128)(2,1)}), bf16[16,320,128]{2,1,0:T(8,128)(2,1)S(1)}, u32[]{:S(2)}, u32[]{:S(2)}) async-start(bf16[16,320,128]{2,1,0:T(8,128)(2,1)} %get-tuple-element.189), calls=%async_computation.1 | async-start | bytes 2621440 | tf_op jit(solution)/shard_map/all_to_all | solution.py:37
  48.0 0.0 copy-start.1
  48.1 0.0 copy-start.3
  48.1 0.9 collective-permute-start.8
  48.9 1.6 %collective-permute-done.8.peer_ref = bf16[528,512]{1,0:T(8,128)(2,1)S(1)} collective-permute-done((bf16[528,512]{1,0:T(8,128)(2,1)S(1)}, bf16[528,512]{1,0:T(8,128)(2,1)S(1)}, u32[]{:S(2)}, u32[]{:S(2)}) %collective-permute-start.8) | collective-permute-done | bytes 540704 | tf_op jit(solution)/shard_map/ppermute | solution.py:62
  50.5 0.7 back_project.1
  51.2 2.8 %collective-permute-start.10 = (bf16[528,128]{1,0:T(8,128)(2,1)S(1)}, bf16[528,128]{1,0:T(8,128)(2,1)S(1)}, u32[]{:S(2)}, u32[]{:S(2)}) collective-permute-start(bf16[528,128]{1,0:T(8,128)(2,1)S(1)} %get-tuple-element.197), channel_id=1, source_target_pairs={{0,6},{1,7},{2,0},{3,1},{4,2},{5,3},{6,4},{7,5},{8,14},{9,15},{10,... | collective-permute-start | bytes 405512 | tf_op jit(solution)/shard_map/ppermute | solution.py:58
  54.0 0.4 collective-permute-start.11
  54.4 0.7 collective-permute-start.9
  55.1 4.3 %collective-permute-done.10.refs_2_ = bf16[528,128]{1,0:T(8,128)(2,1)S(1)} collective-permute-done((bf16[528,128]{1,0:T(8,128)(2,1)S(1)}, bf16[528,128]{1,0:T(8,128)(2,1)S(1)}, u32[]{:S(2)}, u32[]{:S(2)}) %collective-permute-start.10) | collective-permute-done | bytes 135200 | tf_op jit(solution)/shard_map/ppermute | solution.py:58
  59.4 0.6 collective-permute-done.11.refs_3_
  60.0 3.9 %collective-permute-done.9.refs_1_ = bf16[528,128]{1,0:T(8,128)(2,1)S(1)} collective-permute-done((bf16[528,128]{1,0:T(8,128)(2,1)S(1)}, bf16[528,128]{1,0:T(8,128)(2,1)S(1)}, u32[]{:S(2)}, u32[]{:S(2)}) %collective-permute-start.9) | collective-permute-done | bytes 135200 | tf_op jit(solution)/shard_map/ppermute | solution.py:58
  63.9 1.7 %input_grads.1 = (bf16[512,128]{1,0:T(8,128)(2,1)S(1)}, bf16[4,144,128]{2,1,0:T(8,128)(2,1)S(1)}, bf16[4,144,128]{2,1,0:T(8,128)(2,1)S(1)}, bf16[4,144,128]{2,1,0:T(8,128)(2,1)S(1)}, bf16[4,144,128]{2,1,0:T(8,128)(2,1)S(1)}) custom-call(s32[1]{0:T(128)S(6)} %copy.19.length_ref, bf16[528,128]{1,0:T(8,128)(2,1)S(1)} %get-tuple-element.195.refs_0_, ...), custom_call_target="tpu_custom_call" | custom-call | flops 1000 | bytes 1000 | tf_op jit(solution)/shard_map/input_grads/pallas_call | solution.py:578
  65.6 1.9 %collective-permute-start.12 = (bf16[4,144,128]{2,1,0:T(8,128)(2,1)S(1)}, bf16[4,144,128]{2,1,0:T(8,128)(2,1)S(1)}, u32[]{:S(2)}, u32[]{:S(2)}) collective-permute-start(bf16[4,144,128]{2,1,0:T(8,128)(2,1)S(1)} %get-tuple-element.202), channel_id=1, source_target_pairs={{0,8},{8,16},{16,24},{24,0},{64,72},{72,80},{80,88},{88,64},{32,40... | collective-permute-start | bytes 442376 | tf_op jit(solution)/shard_map/ppermute | solution.py:49
  67.6 1.3 %collective-permute-start.13 = (bf16[4,144,128]{2,1,0:T(8,128)(2,1)S(1)}, bf16[4,144,128]{2,1,0:T(8,128)(2,1)S(1)}, u32[]{:S(2)}, u32[]{:S(2)}) collective-permute-start(bf16[4,144,128]{2,1,0:T(8,128)(2,1)S(1)} %get-tuple-element.203), channel_id=1, source_target_pairs={{0,24},{8,0},{16,8},{24,16},{64,88},{72,64},{80,72},{88,80},{32,56... | collective-permute-start | bytes 442376 | tf_op jit(solution)/shard_map/ppermute | solution.py:49
  68.9 1.7 %collective-permute-start.14 = (bf16[4,144,128]{2,1,0:T(8,128)(2,1)S(1)}, bf16[4,144,128]{2,1,0:T(8,128)(2,1)S(1)}, u32[]{:S(2)}, u32[]{:S(2)}) collective-permute-start(bf16[4,144,128]{2,1,0:T(8,128)(2,1)S(1)} %get-tuple-element.204), channel_id=1, source_target_pairs={{0,16},{8,24},{16,0},{24,8},{64,80},{72,88},{80,64},{88,72},{32,48... | collective-permute-start | bytes 442376 | tf_op jit(solution)/shard_map/ppermute | solution.py:49
  70.5 1.3 %weight_sum.1 = bf16[16,320,128]{2,1,0:T(8,128)(2,1)} custom-call(bf16[16,320,128]{2,1,0:T(8,128)(2,1)S(1)} %all-to-all-done.1.parts_ref), custom_call_target="tpu_custom_call" | custom-call | flops 1000 | bytes 1000 | tf_op jit(solution)/shard_map/weight_sum/pallas_call | solution.py:433
  71.8 5.3 %all-to-all-start.2 = ((bf16[16,320,128]{2,1,0:T(8,128)(2,1)}), bf16[16,320,128]{2,1,0:T(8,128)(2,1)S(1)}, u32[]{:S(2)}, u32[]{:S(2)}) async-start(bf16[16,320,128]{2,1,0:T(8,128)(2,1)} %weight_sum.1), calls=%async_computation.2 | async-start | bytes 2621440 | tf_op jit(solution)/shard_map/all_to_all | solution.py:37
  77.2 2.9 %collective-permute-start.17 = (bf16[4,144,128]{2,1,0:T(8,128)(2,1)S(1)}, bf16[4,144,128]{2,1,0:T(8,128)(2,1)S(1)}, u32[]{:S(2)}, u32[]{:S(2)}) collective-permute-start(bf16[4,144,128]{2,1,0:T(8,128)(2,1)S(1)} %pad_maximum_fusion.3), channel_id=1, source_target_pairs={{0,32},{8,40},{16,48},{24,56},{64,96},{72,104},{80,112},{88,120},{... | collective-permute-start | bytes 442376 | tf_op jit(solution)/shard_map/ppermute | solution.py:49
  80.2 1.0 collective-permute-start.16
  81.2 0.6 collective-permute-start.15
  81.9 14.5 %all-to-all-done.2.whole_ref = bf16[16,320,128]{2,1,0:T(8,128)(2,1)S(1)} async-done(((bf16[16,320,128]{2,1,0:T(8,128)(2,1)}), bf16[16,320,128]{2,1,0:T(8,128)(2,1)S(1)}, u32[]{:S(2)}, u32[]{:S(2)}) %all-to-all-start.2) | async-done | bytes 1310752 | tf_op jit(solution)/shard_map/all_to_all | solution.py:37
  96.3 1.6 %place_weights.1 = (f32[4,1024,128]{2,1,0:T(8,128)}, f32[128,1024]{1,0:T(8,128)}) custom-call(bf16[16,320,128]{2,1,0:T(8,128)(2,1)S(1)} %all-to-all-done.2.whole_ref), custom_call_target="tpu_custom_call" | custom-call | flops 1000 | bytes 1000 | tf_op jit(solution)/shard_map/place_weights/pallas_call | solution.py:636
  97.9 0.8 collective-permute-done.16.refs_2_
  98.7 3.0 %collective-permute-done.15.refs_1_ = bf16[4,144,128]{2,1,0:T(8,128)(2,1)S(1)} collective-permute-done((bf16[4,144,128]{2,1,0:T(8,128)(2,1)S(1)}, bf16[4,144,128]{2,1,0:T(8,128)(2,1)S(1)}, u32[]{:S(2)}, u32[]{:S(2)}) %collective-permute-start.15) | collective-permute-done | bytes 147488 | tf_op jit(solution)/shard_map/ppermute | solution.py:49
  101.7 2.0 %table_grads.1 = (f32[1024,128]{1,0:T(8,128)}, f32[1,128]{1,0:T(1,128)}, s32[1]{0:T(128)}) custom-call(bf16[4,144,128]{2,1,0:T(8,128)(2,1)S(1)} %pad_maximum_fusion.refs_0_, bf16[4,144,128]{2,1,0:T(8,128)(2,1)S(1)} %collective-permute-done.15.refs_1_, bf16[4,144,128]{2,1,0:T(8,128)(2,1)S(1)} %collective-permute-done.16.refs_2_, ...), custom_call_target="tpu_custom_call" | custom-call | flops 1000 | bytes 1000 | tf_op jit(solution)/shard_map/table_grads/pallas_call | solution.py:664
  103.8 0.6 while.13
  (41 shorter events, 0.2 us)
Async XLA Ops:
  0.6 27.0 %collective-permute-start.4 = (bf16[4,1024,128]{2,1,0:T(8,128)(2,1)}, bf16[4,1024,128]{2,1,0:T(8,128)(2,1)}, u32[]{:S(2)}, u32[]{:S(2)}) collective-permute-start(bf16[4,1024,128]{2,1,0:T(8,128)(2,1)} %proj_own_ref.1), channel_id=1, source_target_pairs={{0,1},{1,0},{2,3},{3,2},{4,5},{5,4},{6,7},{7,6},{8,9},{9,8},{10,11... | collective-permute-start | bytes 3145736 | tf_op jit(solution)/shard_map/ppermute | solution.py:62
  2.8 19.6 %copy-start.13 = (f32[1024]{0:T(1024)S(1)}, f32[1024]{0:T(1024)}, u32[]{:S(2)}) copy-start(f32[1024]{0:T(1024)} %param.12) | copy-start | bytes 12292
  2.8 19.6 %copy-start.16 = (s32[1,512]{1,0:T(1,128)S(1)}, s32[1,512]{1,0:T(1,128)}, u32[]{:S(2)}) copy-start(s32[1,512]{1,0:T(1,128)} %id_ref.1) | copy-start | bytes 6148
  2.8 24.8 %copy-start.11 = (s32[1,32,32]{2,1,0:T(8,128)S(1)}, s32[1,32,32]{2,1,0:T(8,128)}, u32[]{:S(2)}) copy-start(s32[1,32,32]{2,1,0:T(8,128)} %param.17) | copy-start | bytes 12292
  7.5 10.6 %collective-permute-start = (bf16[2,512,128]{2,1,0:T(8,128)(2,1)}, bf16[2,512,128]{2,1,0:T(8,128)(2,1)S(1)}, u32[]{:S(2)}, u32[]{:S(2)}) collective-permute-start(bf16[2,512,128]{2,1,0:T(8,128)(2,1)} %get-tuple-element.174), channel_id=1, source_target_pairs={{0,32},{8,40},{16,48},{24,56},{32,0},{40,8},{48,16},{56,24},{1,33}... | collective-permute-start | bytes 786440 | tf_op jit(solution)/shard_map/ppermute | solution.py:54
  11.3 9.0 %collective-permute-start.5 = (bf16[2,512,128]{2,1,0:T(8,128)(2,1)}, bf16[2,512,128]{2,1,0:T(8,128)(2,1)S(1)}, u32[]{:S(2)}, u32[]{:S(2)}) collective-permute-start(bf16[2,512,128]{2,1,0:T(8,128)(2,1)} %get-tuple-element.176), channel_id=1, source_target_pairs={{0,8},{8,16},{16,24},{24,0},{32,40},{40,48},{48,56},{56,32},{1,9},... | collective-permute-start | bytes 786440 | tf_op jit(solution)/shard_map/ppermute | solution.py:54
  12.5 9.1 %collective-permute-start.6 = (bf16[2,512,128]{2,1,0:T(8,128)(2,1)}, bf16[2,512,128]{2,1,0:T(8,128)(2,1)S(1)}, u32[]{:S(2)}, u32[]{:S(2)}) collective-permute-start(bf16[2,512,128]{2,1,0:T(8,128)(2,1)} %get-tuple-element.177), channel_id=1, source_target_pairs={{0,24},{8,0},{16,8},{24,16},{32,56},{40,32},{48,40},{56,48},{1,25}... | collective-permute-start | bytes 786440 | tf_op jit(solution)/shard_map/ppermute | solution.py:54
  13.9 13.7 %collective-permute-start.7 = (bf16[2,512,128]{2,1,0:T(8,128)(2,1)}, bf16[2,512,128]{2,1,0:T(8,128)(2,1)S(1)}, u32[]{:S(2)}, u32[]{:S(2)}) collective-permute-start(bf16[2,512,128]{2,1,0:T(8,128)(2,1)} %get-tuple-element.178), channel_id=1, source_target_pairs={{0,16},{8,24},{16,0},{24,8},{32,48},{40,56},{48,32},{56,40},{1,17}... | collective-permute-start | bytes 786440 | tf_op jit(solution)/shard_map/ppermute | solution.py:54
  18.1 15.1 %collective-permute-start.1 = (bf16[2,512,128]{2,1,0:T(8,128)(2,1)S(1)}, bf16[2,512,128]{2,1,0:T(8,128)(2,1)S(1)}, u32[]{:S(2)}, u32[]{:S(2)}) collective-permute-start(bf16[2,512,128]{2,1,0:T(8,128)(2,1)S(1)} %collective-permute-done.refs_0_), channel_id=1, source_target_pairs={{0,8},{8,16},{16,24},{24,0},{32,40},{40,48},{48,56},{56,32},{1,9},... | collective-permute-start | bytes 786440 | tf_op jit(solution)/shard_map/ppermute | solution.py:54
  20.3 13.0 %collective-permute-start.2 = (bf16[2,512,128]{2,1,0:T(8,128)(2,1)S(1)}, bf16[2,512,128]{2,1,0:T(8,128)(2,1)S(1)}, u32[]{:S(2)}, u32[]{:S(2)}) collective-permute-start(bf16[2,512,128]{2,1,0:T(8,128)(2,1)S(1)} %collective-permute-done.refs_0_), channel_id=1, source_target_pairs={{0,24},{8,0},{16,8},{24,16},{32,56},{40,32},{48,40},{56,48},{1,25}... | collective-permute-start | bytes 786440 | tf_op jit(solution)/shard_map/ppermute | solution.py:54
  21.6 16.6 %collective-permute-start.3 = (bf16[2,512,128]{2,1,0:T(8,128)(2,1)S(1)}, bf16[2,512,128]{2,1,0:T(8,128)(2,1)S(1)}, u32[]{:S(2)}, u32[]{:S(2)}) collective-permute-start(bf16[2,512,128]{2,1,0:T(8,128)(2,1)S(1)} %collective-permute-done.refs_0_), channel_id=1, source_target_pairs={{0,16},{8,24},{16,0},{24,8},{32,48},{40,56},{48,32},{56,40},{1,17}... | collective-permute-start | bytes 786440 | tf_op jit(solution)/shard_map/ppermute | solution.py:54
  22.4 1.2 %copy-start = (bf16[1,512,1024]{2,1,0:T(8,128)(2,1)S(1)}, bf16[1,512,1024]{2,1,0:T(8,128)(2,1)}, u32[]{:S(2)}) copy-start(bf16[1,512,1024]{2,1,0:T(8,128)(2,1)} %param.10) | copy-start | bytes 3145732
  23.7 1.2 %copy-start.2 = (bf16[1,512,1024]{2,1,0:T(8,128)(2,1)S(1)}, bf16[1,512,1024]{2,1,0:T(8,128)(2,1)}, u32[]{:S(2)}) copy-start(bf16[1,512,1024]{2,1,0:T(8,128)(2,1)} %param.11) | copy-start | bytes 3145732
  24.9 0.9 copy-start.5
  25.8 1.8 %copy-start.4 = (bf16[4,1024,128]{2,1,0:T(8,128)(2,1)S(1)}, bf16[4,1024,128]{2,1,0:T(8,128)(2,1)}, u32[]{:S(2)}) copy-start(bf16[4,1024,128]{2,1,0:T(8,128)(2,1)} %proj_own_ref.1) | copy-start | bytes 3145732
  25.8 1.8 %copy-start.7 = (bf16[2,2,512,128]{3,2,1,0:T(8,128)(2,1)S(1)}, bf16[2,2,512,128]{3,2,1,0:T(8,128)(2,1)}, u32[]{:S(2)}) copy-start(bf16[2,2,512,128]{3,2,1,0:T(8,128)(2,1)} %get-tuple-element.173.own_ref) | copy-start | bytes 1572868
  27.7 10.5 %copy-start.6 = (f32[512,128]{1,0:T(8,128)S(1)}, f32[512,128]{1,0:T(8,128)}, u32[]{:S(2)}) copy-start(f32[512,128]{1,0:T(8,128)} %get-tuple-element.181.inv_rms_ref.refs_5_.refs_7_) | copy-start | bytes 786436
  27.7 10.5 %copy-start.8 = (f32[4,512,128]{2,1,0:T(8,128)S(1)}, f32[4,512,128]{2,1,0:T(8,128)}, u32[]{:S(2)}) copy-start(f32[4,512,128]{2,1,0:T(8,128)} %get-tuple-element.180.refs_4_) | copy-start | bytes 3145732
  27.7 10.5 %copy-start.9 = (f32[512,128]{1,0:T(8,128)S(1)}, f32[512,128]{1,0:T(8,128)}, u32[]{:S(2)}) copy-start(f32[512,128]{1,0:T(8,128)} %get-tuple-element.182.refs_6_) | copy-start | bytes 786436
  27.7 10.5 %copy-start.10 = (f32[512,128]{1,0:T(8,128)S(1)}, f32[512,128]{1,0:T(8,128)}, u32[]{:S(2)}) copy-start(f32[512,128]{1,0:T(8,128)} %get-tuple-element.184.refs_8_) | copy-start | bytes 786436
  27.7 10.5 %copy-start.12 = (bf16[512,128]{1,0:T(8,128)(2,1)S(1)}, bf16[512,128]{1,0:T(8,128)(2,1)}, u32[]{:S(2)}) copy-start(bf16[512,128]{1,0:T(8,128)(2,1)} %get-tuple-element.183.refs_7_) | copy-start | bytes 393220
  43.9 26.6 %all-to-all-start.1 = ((bf16[16,320,128]{2,1,0:T(8,128)(2,1)}), bf16[16,320,128]{2,1,0:T(8,128)(2,1)S(1)}, u32[]{:S(2)}, u32[]{:S(2)}) async-start(bf16[16,320,128]{2,1,0:T(8,128)(2,1)} %get-tuple-element.189), calls=%async_computation.1 | async-start | bytes 2621440 | tf_op jit(solution)/shard_map/all_to_all | solution.py:37
  48.0 15.9 %copy-start.1 = (bf16[1,512,1024]{2,1,0:T(8,128)(2,1)S(1)}, bf16[1,512,1024]{2,1,0:T(8,128)(2,1)}, u32[]{:S(2)}) copy-start(bf16[1,512,1024]{2,1,0:T(8,128)(2,1)} %param.10) | copy-start | bytes 3145732
  48.1 15.9 %copy-start.3 = (bf16[1,512,1024]{2,1,0:T(8,128)(2,1)S(1)}, bf16[1,512,1024]{2,1,0:T(8,128)(2,1)}, u32[]{:S(2)}) copy-start(bf16[1,512,1024]{2,1,0:T(8,128)(2,1)} %param.11) | copy-start | bytes 3145732
  48.1 2.4 %collective-permute-start.8 = (bf16[528,512]{1,0:T(8,128)(2,1)S(1)}, bf16[528,512]{1,0:T(8,128)(2,1)S(1)}, u32[]{:S(2)}, u32[]{:S(2)}) collective-permute-start(bf16[528,512]{1,0:T(8,128)(2,1)S(1)} %get-tuple-element.192.own_ref), channel_id=1, source_target_pairs={{0,1},{1,0},{2,3},{3,2},{4,5},{5,4},{6,7},{7,6},{8,9},{9,8},{10,11... | collective-permute-start | bytes 1622024 | tf_op jit(solution)/shard_map/ppermute | solution.py:62
  51.2 8.1 %collective-permute-start.10 = (bf16[528,128]{1,0:T(8,128)(2,1)S(1)}, bf16[528,128]{1,0:T(8,128)(2,1)S(1)}, u32[]{:S(2)}, u32[]{:S(2)}) collective-permute-start(bf16[528,128]{1,0:T(8,128)(2,1)S(1)} %get-tuple-element.197), channel_id=1, source_target_pairs={{0,6},{1,7},{2,0},{3,1},{4,2},{5,3},{6,4},{7,5},{8,14},{9,15},{10,... | collective-permute-start | bytes 405512 | tf_op jit(solution)/shard_map/ppermute | solution.py:58
  54.0 6.0 %collective-permute-start.11 = (bf16[528,128]{1,0:T(8,128)(2,1)S(1)}, bf16[528,128]{1,0:T(8,128)(2,1)S(1)}, u32[]{:S(2)}, u32[]{:S(2)}) collective-permute-start(bf16[528,128]{1,0:T(8,128)(2,1)S(1)} %get-tuple-element.198), channel_id=1, source_target_pairs={{0,4},{1,5},{2,6},{3,7},{4,0},{5,1},{6,2},{7,3},{8,12},{9,13},{10,... | collective-permute-start | bytes 405512 | tf_op jit(solution)/shard_map/ppermute | solution.py:58
  54.4 9.5 %collective-permute-start.9 = (bf16[528,128]{1,0:T(8,128)(2,1)S(1)}, bf16[528,128]{1,0:T(8,128)(2,1)S(1)}, u32[]{:S(2)}, u32[]{:S(2)}) collective-permute-start(bf16[528,128]{1,0:T(8,128)(2,1)S(1)} %get-tuple-element.196), channel_id=1, source_target_pairs={{0,2},{1,3},{2,4},{3,5},{4,6},{5,7},{6,0},{7,1},{8,10},{9,11},{10,... | collective-permute-start | bytes 405512 | tf_op jit(solution)/shard_map/ppermute | solution.py:58
  65.6 11.5 %collective-permute-start.12 = (bf16[4,144,128]{2,1,0:T(8,128)(2,1)S(1)}, bf16[4,144,128]{2,1,0:T(8,128)(2,1)S(1)}, u32[]{:S(2)}, u32[]{:S(2)}) collective-permute-start(bf16[4,144,128]{2,1,0:T(8,128)(2,1)S(1)} %get-tuple-element.202), channel_id=1, source_target_pairs={{0,8},{8,16},{16,24},{24,0},{64,72},{72,80},{80,88},{88,64},{32,40... | collective-permute-start | bytes 442376 | tf_op jit(solution)/shard_map/ppermute | solution.py:49
  67.6 9.6 %collective-permute-start.13 = (bf16[4,144,128]{2,1,0:T(8,128)(2,1)S(1)}, bf16[4,144,128]{2,1,0:T(8,128)(2,1)S(1)}, u32[]{:S(2)}, u32[]{:S(2)}) collective-permute-start(bf16[4,144,128]{2,1,0:T(8,128)(2,1)S(1)} %get-tuple-element.203), channel_id=1, source_target_pairs={{0,24},{8,0},{16,8},{24,16},{64,88},{72,64},{80,72},{88,80},{32,56... | collective-permute-start | bytes 442376 | tf_op jit(solution)/shard_map/ppermute | solution.py:49
  68.9 8.3 %collective-permute-start.14 = (bf16[4,144,128]{2,1,0:T(8,128)(2,1)S(1)}, bf16[4,144,128]{2,1,0:T(8,128)(2,1)S(1)}, u32[]{:S(2)}, u32[]{:S(2)}) collective-permute-start(bf16[4,144,128]{2,1,0:T(8,128)(2,1)S(1)} %get-tuple-element.204), channel_id=1, source_target_pairs={{0,16},{8,24},{16,0},{24,8},{64,80},{72,88},{80,64},{88,72},{32,48... | collective-permute-start | bytes 442376 | tf_op jit(solution)/shard_map/ppermute | solution.py:49
  71.8 24.5 %all-to-all-start.2 = ((bf16[16,320,128]{2,1,0:T(8,128)(2,1)}), bf16[16,320,128]{2,1,0:T(8,128)(2,1)S(1)}, u32[]{:S(2)}, u32[]{:S(2)}) async-start(bf16[16,320,128]{2,1,0:T(8,128)(2,1)} %weight_sum.1), calls=%async_computation.2 | async-start | bytes 2621440 | tf_op jit(solution)/shard_map/all_to_all | solution.py:37
  77.2 20.7 %collective-permute-start.17 = (bf16[4,144,128]{2,1,0:T(8,128)(2,1)S(1)}, bf16[4,144,128]{2,1,0:T(8,128)(2,1)S(1)}, u32[]{:S(2)}, u32[]{:S(2)}) collective-permute-start(bf16[4,144,128]{2,1,0:T(8,128)(2,1)S(1)} %pad_maximum_fusion.3), channel_id=1, source_target_pairs={{0,32},{8,40},{16,48},{24,56},{64,96},{72,104},{80,112},{88,120},{... | collective-permute-start | bytes 442376 | tf_op jit(solution)/shard_map/ppermute | solution.py:49
  80.2 18.5 %collective-permute-start.16 = (bf16[4,144,128]{2,1,0:T(8,128)(2,1)S(1)}, bf16[4,144,128]{2,1,0:T(8,128)(2,1)S(1)}, u32[]{:S(2)}, u32[]{:S(2)}) collective-permute-start(bf16[4,144,128]{2,1,0:T(8,128)(2,1)S(1)} %pad_maximum_fusion.2), channel_id=1, source_target_pairs={{0,96},{8,104},{16,112},{24,120},{64,0},{72,8},{80,16},{88,24},{32... | collective-permute-start | bytes 442376 | tf_op jit(solution)/shard_map/ppermute | solution.py:49
  81.2 20.5 %collective-permute-start.15 = (bf16[4,144,128]{2,1,0:T(8,128)(2,1)S(1)}, bf16[4,144,128]{2,1,0:T(8,128)(2,1)S(1)}, u32[]{:S(2)}, u32[]{:S(2)}) collective-permute-start(bf16[4,144,128]{2,1,0:T(8,128)(2,1)S(1)} %pad_maximum_fusion.1), channel_id=1, source_target_pairs={{0,64},{8,72},{16,80},{24,88},{64,32},{72,40},{80,48},{88,56},{32,... | collective-permute-start | bytes 442376 | tf_op jit(solution)/shard_map/ppermute | solution.py:49

commit v5 on v4

--- a/solution.py
+++ b/solution.py
@@ -709,10 +709,10 @@
     d_peer = move_core(d_own)
     shares = swap_plane(shares)
     parts = back_project(d_own, d_peer, w_own, w_peer, col)
-    parts = [parts[0]] + [move_y(parts[k], k) for k in (1, 3, 2)]
+    parts = [parts[0]] + [move_y(parts[k], k) for k in (2, 1, 3)]
 
     d_inputs, *sends = input_grads(lengths, parts, x_rows, cot_rows, norm_gain, inv_rms, slots, item_rows, room)
-    line = [sends[0]] + [move_plane(sends[k], 0, k) for k in (1, 3, 2)]
+    line = [sends[0]] + [move_plane(sends[k], 0, k) for k in (2, 1, 3)]
     sends = [jnp.stack([block[k] for block in line]) for k in range(4)]
     gots = [sends[0]] + [move_plane(sends[k], k, 0) for k in (1, 3, 2)]
     grad_in_w, grad_out_w = place_weights(swap_plane(weight_sum(shares)))

time: 105 us -> 102 us (0.971)
  waiting for transfers between devices: 37.2 us -> 33.8 us
    ppermute x3, waiting for transfers between devices: 8.86 us -> 5.76 us  [move_y(): lax.ppermute(value, 'col', [(i, (i // 2 + dy) % 4 * 2 + i % 2) for i in r...]
    ppermute x6, starting transfers between devices: 9.45 us -> 10.7 us  [move_plane(): return lax.ppermute(value, ('dp', 'seq'), pairs)]
    all_to_all x2, starting transfers between devices: 9.39 us -> 8.17 us  [swap_plane(): return lax.all_to_all(value, ('dp', 'seq'), 0, 0, tiled=True)]
    all_to_all x2, waiting for transfers between devices: 14.5 us -> 13.3 us  [swap_plane(): return lax.all_to_all(value, ('dp', 'seq'), 0, 0, tiled=True)]
  transfers between devices with their start and end apart: 20 -> 20, of which waited for: 10 -> 9; matrix products, arithmetic and copies ran while one was open for 0% -> 0% of each run, Pallas kernels for 16% -> 17%
where the time goes in v5:
time: 102 us
  starting transfers between devices  37 us (36%)
  waiting for transfers between devices  33.8 us (33%)
  Pallas kernels  25 us (25%)
  local copies, waits for them, and re-layouts  3.5 us (3%)
  between operations  1.78 us (2%)
    all_to_all x2, waiting for transfers between devices, swap_plane(): return lax.all_to_all(value, ('dp', 'seq'), 0, 0, tiled=True)  13.3 us
    ppermute x7, starting transfers between devices, move_seq(): return lax.ppermute(value, 'seq', pairs)  11.3 us
    ppermute x6, starting transfers between devices, move_plane(): return lax.ppermute(value, ('dp', 'seq'), pairs)  10.7 us
    ppermute x7, waiting for transfers between devices, move_seq(): return lax.ppermute(value, 'seq', pairs)  8.52 us
    all_to_all x2, starting transfers between devices, swap_plane(): return lax.all_to_all(value, ('dp', 'seq'), 0, 0, tiled=True)  8.17 us
    ppermute x3, waiting for transfers between devices, move_y(): lax.ppermute(value, 'col', [(i, (i // 2 + dy) % 4 * 2 + i % 2) for i in r...  5.76 us
    pallas_call x1, Pallas kernels, far_terms(): kernel_call(functools.partial(far_body, scale=scale), (shape_of((tok + EX...  5.72 us
    pallas_call x1, Pallas kernels, near_terms(): kernel_call(functools.partial(near_body, scale=scale), (shape_of(own.shap...  5.52 us
  transfers between devices with their start and end apart: 20, of which 9 were waited for; matrix products, arithmetic and copies ran while one was open for 0% of the time, Pallas kernels for 17%

profile of v5, /device:TPU:1, one launch (start us, length us, event | category | flops | bytes accessed | tf_op | source)
XLA Modules:
  0.0 101.8 jit_solution(3784875764415872860)
XLA Ops:
  0.6 1.5 %collective-permute-start.4 = (bf16[4,1024,128]{2,1,0:T(8,128)(2,1)}, bf16[4,1024,128]{2,1,0:T(8,128)(2,1)}, u32[]{:S(2)}, u32[]{:S(2)}) collective-permute-start(bf16[4,1024,128]{2,1,0:T(8,128)(2,1)} %proj_own_ref.1), channel_id=1, source_target_pairs={{0,1},{1,0},{2,3},{3,2},{4,5},{5,4},{6,7},{7,6},{8,9},{9,8},{10,11... | collective-permute-start | bytes 3145736 | tf_op jit(solution)/shard_map/ppermute | solution.py:62
  2.8 4.7 %project.1 = (bf16[2,2,512,128]{3,2,1,0:T(8,128)(2,1)}, bf16[2,512,128]{2,1,0:T(8,128)(2,1)}, bf16[2,512,128]{2,1,0:T(8,128)(2,1)}, bf16[2,512,128]{2,1,0:T(8,12...) custom-call(s32[1]{0:T(128)S(6)} %copy.19.length_ref, ...), custom_call_target="tpu_custom_call" | custom-call | flops 1000 | bytes 1000 | tf_op jit(solution)/shard_map/project/pallas_call | solution.py:130
  7.5 3.8 %collective-permute-start = (bf16[2,512,128]{2,1,0:T(8,128)(2,1)}, bf16[2,512,128]{2,1,0:T(8,128)(2,1)S(1)}, u32[]{:S(2)}, u32[]{:S(2)}) collective-permute-start(bf16[2,512,128]{2,1,0:T(8,128)(2,1)} %get-tuple-element.174), channel_id=1, source_target_pairs={{0,32},{8,40},{16,48},{24,56},{32,0},{40,8},{48,16},{56,24},{1,33}... | collective-permute-start | bytes 786440 | tf_op jit(solution)/shard_map/ppermute | solution.py:54
  11.3 1.2 %collective-permute-start.5 = (bf16[2,512,128]{2,1,0:T(8,128)(2,1)}, bf16[2,512,128]{2,1,0:T(8,128)(2,1)S(1)}, u32[]{:S(2)}, u32[]{:S(2)}) collective-permute-start(bf16[2,512,128]{2,1,0:T(8,128)(2,1)} %get-tuple-element.176), channel_id=1, source_target_pairs={{0,8},{8,16},{16,24},{24,0},{32,40},{40,48},{48,56},{56,32},{1,9},... | collective-permute-start | bytes 786440 | tf_op jit(solution)/shard_map/ppermute | solution.py:54
  12.5 1.5 %collective-permute-start.6 = (bf16[2,512,128]{2,1,0:T(8,128)(2,1)}, bf16[2,512,128]{2,1,0:T(8,128)(2,1)S(1)}, u32[]{:S(2)}, u32[]{:S(2)}) collective-permute-start(bf16[2,512,128]{2,1,0:T(8,128)(2,1)} %get-tuple-element.177), channel_id=1, source_target_pairs={{0,24},{8,0},{16,8},{24,16},{32,56},{40,32},{48,40},{56,48},{1,25}... | collective-permute-start | bytes 786440 | tf_op jit(solution)/shard_map/ppermute | solution.py:54
  13.9 1.5 %collective-permute-start.7 = (bf16[2,512,128]{2,1,0:T(8,128)(2,1)}, bf16[2,512,128]{2,1,0:T(8,128)(2,1)S(1)}, u32[]{:S(2)}, u32[]{:S(2)}) collective-permute-start(bf16[2,512,128]{2,1,0:T(8,128)(2,1)} %get-tuple-element.178), channel_id=1, source_target_pairs={{0,16},{8,24},{16,0},{24,8},{32,48},{40,56},{48,32},{56,40},{1,17}... | collective-permute-start | bytes 786440 | tf_op jit(solution)/shard_map/ppermute | solution.py:54
  15.5 2.7 %collective-permute-done.refs_0_ = bf16[2,512,128]{2,1,0:T(8,128)(2,1)S(1)} collective-permute-done((bf16[2,512,128]{2,1,0:T(8,128)(2,1)}, bf16[2,512,128]{2,1,0:T(8,128)(2,1)S(1)}, u32[]{:S(2)}, u32[]{:S(2)}) %collective-permute-start) | collective-permute-done | bytes 262176 | tf_op jit(solution)/shard_map/ppermute | solution.py:54
  18.1 1.2 %collective-permute-start.1 = (bf16[2,512,128]{2,1,0:T(8,128)(2,1)S(1)}, bf16[2,512,128]{2,1,0:T(8,128)(2,1)S(1)}, u32[]{:S(2)}, u32[]{:S(2)}) collective-permute-start(bf16[2,512,128]{2,1,0:T(8,128)(2,1)S(1)} %collective-permute-done.refs_0_), channel_id=1, source_target_pairs={{0,8},{8,16},{16,24},{24,0},{32,40},{40,48},{48,56},{56,32},{1,9},... | collective-permute-start | bytes 786440 | tf_op jit(solution)/shard_map/ppermute | solution.py:54
  19.4 0.9 collective-permute-done.5.refs_1_
  20.3 1.3 %collective-permute-start.2 = (bf16[2,512,128]{2,1,0:T(8,128)(2,1)S(1)}, bf16[2,512,128]{2,1,0:T(8,128)(2,1)S(1)}, u32[]{:S(2)}, u32[]{:S(2)}) collective-permute-start(bf16[2,512,128]{2,1,0:T(8,128)(2,1)S(1)} %collective-permute-done.refs_0_), channel_id=1, source_target_pairs={{0,24},{8,0},{16,8},{24,16},{32,56},{40,32},{48,40},{56,48},{1,25}... | collective-permute-start | bytes 786440 | tf_op jit(solution)/shard_map/ppermute | solution.py:54
  21.6 0.9 collective-permute-start.3
  22.4 1.2 %copy-done = bf16[1,512,1024]{2,1,0:T(8,128)(2,1)S(1)} copy-done((bf16[1,512,1024]{2,1,0:T(8,128)(2,1)S(1)}, bf16[1,512,1024]{2,1,0:T(8,128)(2,1)}, u32[]{:S(2)}) %copy-start) | copy-done | bytes 1048600
  23.7 1.2 %copy-done.2 = bf16[1,512,1024]{2,1,0:T(8,128)(2,1)S(1)} copy-done((bf16[1,512,1024]{2,1,0:T(8,128)(2,1)S(1)}, bf16[1,512,1024]{2,1,0:T(8,128)(2,1)}, u32[]{:S(2)}) %copy-start.2) | copy-done | bytes 1048600
  24.9 0.9 copy-done.5
  25.8 1.8 %prepare.1 = (bf16[1024,512]{1,0:T(8,128)(2,1)S(1)}, bf16[1024,512]{1,0:T(8,128)(2,1)S(1)}, s32[1,512]{1,0:T(1,128)S(1)}, s32[1,512]{1,0:T(1,128)S(1)}, bf16[16,512]{1,0:T(8,128)(2,1)S(1)}) custom-call(s32[1]{0:T(128)S(6)} %copy.19.length_ref, bf16[512,1024]{1,0:T(8,128)(2,1)S(1)} %bitcast.8, bf16[512,1024]{1,0:T(8,128)(2,1)S(1)} %bitcast.11, ...), custom_call_target="tpu_custom_call" | custom-call | flops 1000 | bytes 1000 | tf_op jit(solution)/shard_map/prepare/pallas_call | solution.py:456
  27.6 0.0 collective-permute-done.7.refs_3_
  27.7 0.0 copy-start.8
  27.7 5.5 %near_terms.1 = (f32[2,2,512,128]{3,2,1,0:T(8,128)S(1)}, bf16[512,512]{1,0:T(8,128)(2,1)S(1)}, bf16[512,512]{1,0:T(8,128)(2,1)S(1)}) custom-call(s32[1]{0:T(128)S(6)} %copy.19.length_ref, bf16[2,2,512,128]{3,2,1,0:T(8,128)(2,1)S(1)} %copy-done.7, s32[32,32]{1,0:T(8,128)S(1)} %bitcast.14, bf16[4,1024,128]{2,1,0:T(8,128)(2,1)S(1)} %copy-done.4, ...), custom_call_target="tpu_custom_call" | custom-call | flops 1000 | bytes 1000 | tf_op jit(solution)/shard_map/near_terms/pallas_call | solution.py:274
  33.2 0.0 collective-permute-done.1.refs_0_
  33.3 4.9 %collective-permute-done.3.refs_2_ = bf16[2,512,128]{2,1,0:T(8,128)(2,1)S(1)} collective-permute-done((bf16[2,512,128]{2,1,0:T(8,128)(2,1)S(1)}, bf16[2,512,128]{2,1,0:T(8,128)(2,1)S(1)}, u32[]{:S(2)}, u32[]{:S(2)}) %collective-permute-start.3) | collective-permute-done | bytes 262176 | tf_op jit(solution)/shard_map/ppermute | solution.py:54
  38.2 5.7 %far_terms.1 = (bf16[528,512]{1,0:T(8,128)(2,1)S(1)}, bf16[16,320,128]{2,1,0:T(8,128)(2,1)}) custom-call(s32[1]{0:T(128)S(6)} %copy.19.length_ref, bf16[2,2,512,128]{3,2,1,0:T(8,128)(2,1)S(1)} %copy-done.7, s32[32,32]{1,0:T(8,128)S(1)} %bitcast.15, bf16[2,512,128]{2,1,0:T(8,128)(2,1)S(1)} %collective-permute-done.1.refs_0_, ...), custom_call_target="tpu_custom_call" | custom-call | flops 1000 | bytes 1000 | tf_op jit(solution)/shard_map/far_terms/pallas_call | solution.py:328
  43.9 4.1 %all-to-all-start.1 = ((bf16[16,320,128]{2,1,0:T(8,128)(2,1)}), bf16[16,320,128]{2,1,0:T(8,128)(2,1)S(1)}, u32[]{:S(2)}, u32[]{:S(2)}) async-start(bf16[16,320,128]{2,1,0:T(8,128)(2,1)} %get-tuple-element.189), calls=%async_computation.1 | async-start | bytes 2621440 | tf_op jit(solution)/shard_map/all_to_all | solution.py:37
  48.0 0.0 copy-start.1
  48.1 0.0 copy-start.3
  48.1 0.9 collective-permute-start.8
  48.9 1.6 %collective-permute-done.8.peer_ref = bf16[528,512]{1,0:T(8,128)(2,1)S(1)} collective-permute-done((bf16[528,512]{1,0:T(8,128)(2,1)S(1)}, bf16[528,512]{1,0:T(8,128)(2,1)S(1)}, u32[]{:S(2)}, u32[]{:S(2)}) %collective-permute-start.8) | collective-permute-done | bytes 540704 | tf_op jit(solution)/shard_map/ppermute | solution.py:62
  50.5 0.7 back_project.1
  51.2 1.4 %collective-permute-start.10 = (bf16[528,128]{1,0:T(8,128)(2,1)S(1)}, bf16[528,128]{1,0:T(8,128)(2,1)S(1)}, u32[]{:S(2)}, u32[]{:S(2)}) collective-permute-start(bf16[528,128]{1,0:T(8,128)(2,1)S(1)} %get-tuple-element.197), channel_id=1, source_target_pairs={{0,2},{1,3},{2,4},{3,5},{4,6},{5,7},{6,0},{7,1},{8,10},{9,11},{10,... | collective-permute-start | bytes 405512 | tf_op jit(solution)/shard_map/ppermute | solution.py:58
  52.6 1.5 %collective-permute-start.11 = (bf16[528,128]{1,0:T(8,128)(2,1)S(1)}, bf16[528,128]{1,0:T(8,128)(2,1)S(1)}, u32[]{:S(2)}, u32[]{:S(2)}) collective-permute-start(bf16[528,128]{1,0:T(8,128)(2,1)S(1)} %get-tuple-element.198), channel_id=1, source_target_pairs={{0,6},{1,7},{2,0},{3,1},{4,2},{5,3},{6,4},{7,5},{8,14},{9,15},{10,... | collective-permute-start | bytes 405512 | tf_op jit(solution)/shard_map/ppermute | solution.py:58
  54.1 1.6 %collective-permute-start.9 = (bf16[528,128]{1,0:T(8,128)(2,1)S(1)}, bf16[528,128]{1,0:T(8,128)(2,1)S(1)}, u32[]{:S(2)}, u32[]{:S(2)}) collective-permute-start(bf16[528,128]{1,0:T(8,128)(2,1)S(1)} %get-tuple-element.196), channel_id=1, source_target_pairs={{0,4},{1,5},{2,6},{3,7},{4,0},{5,1},{6,2},{7,3},{8,12},{9,13},{10,... | collective-permute-start | bytes 405512 | tf_op jit(solution)/shard_map/ppermute | solution.py:58
  55.7 1.7 %collective-permute-done.10.refs_2_ = bf16[528,128]{1,0:T(8,128)(2,1)S(1)} collective-permute-done((bf16[528,128]{1,0:T(8,128)(2,1)S(1)}, bf16[528,128]{1,0:T(8,128)(2,1)S(1)}, u32[]{:S(2)}, u32[]{:S(2)}) %collective-permute-start.10) | collective-permute-done | bytes 135200 | tf_op jit(solution)/shard_map/ppermute | solution.py:58
  57.4 4.0 %collective-permute-done.9.refs_1_ = bf16[528,128]{1,0:T(8,128)(2,1)S(1)} collective-permute-done((bf16[528,128]{1,0:T(8,128)(2,1)S(1)}, bf16[528,128]{1,0:T(8,128)(2,1)S(1)}, u32[]{:S(2)}, u32[]{:S(2)}) %collective-permute-start.9) | collective-permute-done | bytes 135200 | tf_op jit(solution)/shard_map/ppermute | solution.py:58
  61.4 1.7 %input_grads.1 = (bf16[512,128]{1,0:T(8,128)(2,1)S(1)}, bf16[4,144,128]{2,1,0:T(8,128)(2,1)S(1)}, bf16[4,144,128]{2,1,0:T(8,128)(2,1)S(1)}, bf16[4,144,128]{2,1,0:T(8,128)(2,1)S(1)}, bf16[4,144,128]{2,1,0:T(8,128)(2,1)S(1)}) custom-call(s32[1]{0:T(128)S(6)} %copy.19.length_ref, bf16[528,128]{1,0:T(8,128)(2,1)S(1)} %get-tuple-element.195.refs_0_, ...), custom_call_target="tpu_custom_call" | custom-call | flops 1000 | bytes 1000 | tf_op jit(solution)/shard_map/input_grads/pallas_call | solution.py:578
  63.1 3.4 %collective-permute-start.12 = (bf16[4,144,128]{2,1,0:T(8,128)(2,1)S(1)}, bf16[4,144,128]{2,1,0:T(8,128)(2,1)S(1)}, u32[]{:S(2)}, u32[]{:S(2)}) collective-permute-start(bf16[4,144,128]{2,1,0:T(8,128)(2,1)S(1)} %get-tuple-element.202), channel_id=1, source_target_pairs={{0,16},{8,24},{16,0},{24,8},{64,80},{72,88},{80,64},{88,72},{32,48... | collective-permute-start | bytes 442376 | tf_op jit(solution)/shard_map/ppermute | solution.py:49
  66.6 0.3 collective-permute-start.13
  66.9 2.4 %collective-permute-start.14 = (bf16[4,144,128]{2,1,0:T(8,128)(2,1)S(1)}, bf16[4,144,128]{2,1,0:T(8,128)(2,1)S(1)}, u32[]{:S(2)}, u32[]{:S(2)}) collective-permute-start(bf16[4,144,128]{2,1,0:T(8,128)(2,1)S(1)} %get-tuple-element.204), channel_id=1, source_target_pairs={{0,24},{8,0},{16,8},{24,16},{64,88},{72,64},{80,72},{88,80},{32,56... | collective-permute-start | bytes 442376 | tf_op jit(solution)/shard_map/ppermute | solution.py:49
  69.3 0.0 all-to-all-done.1.parts_ref
  69.3 1.3 %weight_sum.1 = bf16[16,320,128]{2,1,0:T(8,128)(2,1)} custom-call(bf16[16,320,128]{2,1,0:T(8,128)(2,1)S(1)} %all-to-all-done.1.parts_ref), custom_call_target="tpu_custom_call" | custom-call | flops 1000 | bytes 1000 | tf_op jit(solution)/shard_map/weight_sum/pallas_call | solution.py:433
  70.6 4.1 %all-to-all-start.2 = ((bf16[16,320,128]{2,1,0:T(8,128)(2,1)}), bf16[16,320,128]{2,1,0:T(8,128)(2,1)S(1)}, u32[]{:S(2)}, u32[]{:S(2)}) async-start(bf16[16,320,128]{2,1,0:T(8,128)(2,1)} %weight_sum.1), calls=%async_computation.2 | async-start | bytes 2621440 | tf_op jit(solution)/shard_map/all_to_all | solution.py:37
  74.8 2.9 %collective-permute-start.17 = (bf16[4,144,128]{2,1,0:T(8,128)(2,1)S(1)}, bf16[4,144,128]{2,1,0:T(8,128)(2,1)S(1)}, u32[]{:S(2)}, u32[]{:S(2)}) collective-permute-start(bf16[4,144,128]{2,1,0:T(8,128)(2,1)S(1)} %pad_maximum_fusion.3), channel_id=1, source_target_pairs={{0,32},{8,40},{16,48},{24,56},{64,96},{72,104},{80,112},{88,120},{... | collective-permute-start | bytes 442376 | tf_op jit(solution)/shard_map/ppermute | solution.py:49
  77.7 1.0 collective-permute-start.16
  78.7 0.6 collective-permute-start.15
  79.4 13.3 %all-to-all-done.2.whole_ref = bf16[16,320,128]{2,1,0:T(8,128)(2,1)S(1)} async-done(((bf16[16,320,128]{2,1,0:T(8,128)(2,1)}), bf16[16,320,128]{2,1,0:T(8,128)(2,1)S(1)}, u32[]{:S(2)}, u32[]{:S(2)}) %all-to-all-start.2) | async-done | bytes 1310752 | tf_op jit(solution)/shard_map/all_to_all | solution.py:37
  92.7 1.6 %place_weights.1 = (f32[4,1024,128]{2,1,0:T(8,128)}, f32[128,1024]{1,0:T(8,128)}) custom-call(bf16[16,320,128]{2,1,0:T(8,128)(2,1)S(1)} %all-to-all-done.2.whole_ref), custom_call_target="tpu_custom_call" | custom-call | flops 1000 | bytes 1000 | tf_op jit(solution)/shard_map/place_weights/pallas_call | solution.py:636
  94.3 2.1 %collective-permute-done.16.refs_2_ = bf16[4,144,128]{2,1,0:T(8,128)(2,1)S(1)} collective-permute-done((bf16[4,144,128]{2,1,0:T(8,128)(2,1)S(1)}, bf16[4,144,128]{2,1,0:T(8,128)(2,1)S(1)}, u32[]{:S(2)}, u32[]{:S(2)}) %collective-permute-start.16) | collective-permute-done | bytes 147488 | tf_op jit(solution)/shard_map/ppermute | solution.py:49
  96.4 2.4 %collective-permute-done.15.refs_1_ = bf16[4,144,128]{2,1,0:T(8,128)(2,1)S(1)} collective-permute-done((bf16[4,144,128]{2,1,0:T(8,128)(2,1)S(1)}, bf16[4,144,128]{2,1,0:T(8,128)(2,1)S(1)}, u32[]{:S(2)}, u32[]{:S(2)}) %collective-permute-start.15) | collective-permute-done | bytes 147488 | tf_op jit(solution)/shard_map/ppermute | solution.py:49
  98.9 2.0 %table_grads.1 = (f32[1024,128]{1,0:T(8,128)}, f32[1,128]{1,0:T(1,128)}, s32[1]{0:T(128)}) custom-call(bf16[4,144,128]{2,1,0:T(8,128)(2,1)S(1)} %pad_maximum_fusion.refs_0_, bf16[4,144,128]{2,1,0:T(8,128)(2,1)S(1)} %collective-permute-done.15.refs_1_, bf16[4,144,128]{2,1,0:T(8,128)(2,1)S(1)} %collective-permute-done.16.refs_2_, ...), custom_call_target="tpu_custom_call" | custom-call | flops 1000 | bytes 1000 | tf_op jit(solution)/shard_map/table_grads/pallas_call | solution.py:664
  100.9 0.6 while.13
  (41 shorter events, 0.2 us)
Async XLA Ops:
  0.6 27.0 %collective-permute-start.4 = (bf16[4,1024,128]{2,1,0:T(8,128)(2,1)}, bf16[4,1024,128]{2,1,0:T(8,128)(2,1)}, u32[]{:S(2)}, u32[]{:S(2)}) collective-permute-start(bf16[4,1024,128]{2,1,0:T(8,128)(2,1)} %proj_own_ref.1), channel_id=1, source_target_pairs={{0,1},{1,0},{2,3},{3,2},{4,5},{5,4},{6,7},{7,6},{8,9},{9,8},{10,11... | collective-permute-start | bytes 3145736 | tf_op jit(solution)/shard_map/ppermute | solution.py:62
  2.8 19.6 %copy-start.13 = (f32[1024]{0:T(1024)S(1)}, f32[1024]{0:T(1024)}, u32[]{:S(2)}) copy-start(f32[1024]{0:T(1024)} %param.12) | copy-start | bytes 12292
  2.8 19.6 %copy-start.16 = (s32[1,512]{1,0:T(1,128)S(1)}, s32[1,512]{1,0:T(1,128)}, u32[]{:S(2)}) copy-start(s32[1,512]{1,0:T(1,128)} %id_ref.1) | copy-start | bytes 6148
  2.8 24.8 %copy-start.11 = (s32[1,32,32]{2,1,0:T(8,128)S(1)}, s32[1,32,32]{2,1,0:T(8,128)}, u32[]{:S(2)}) copy-start(s32[1,32,32]{2,1,0:T(8,128)} %param.17) | copy-start | bytes 12292
  7.5 10.6 %collective-permute-start = (bf16[2,512,128]{2,1,0:T(8,128)(2,1)}, bf16[2,512,128]{2,1,0:T(8,128)(2,1)S(1)}, u32[]{:S(2)}, u32[]{:S(2)}) collective-permute-start(bf16[2,512,128]{2,1,0:T(8,128)(2,1)} %get-tuple-element.174), channel_id=1, source_target_pairs={{0,32},{8,40},{16,48},{24,56},{32,0},{40,8},{48,16},{56,24},{1,33}... | collective-permute-start | bytes 786440 | tf_op jit(solution)/shard_map/ppermute | solution.py:54
  11.3 9.0 %collective-permute-start.5 = (bf16[2,512,128]{2,1,0:T(8,128)(2,1)}, bf16[2,512,128]{2,1,0:T(8,128)(2,1)S(1)}, u32[]{:S(2)}, u32[]{:S(2)}) collective-permute-start(bf16[2,512,128]{2,1,0:T(8,128)(2,1)} %get-tuple-element.176), channel_id=1, source_target_pairs={{0,8},{8,16},{16,24},{24,0},{32,40},{40,48},{48,56},{56,32},{1,9},... | collective-permute-start | bytes 786440 | tf_op jit(solution)/shard_map/ppermute | solution.py:54
  12.5 9.1 %collective-permute-start.6 = (bf16[2,512,128]{2,1,0:T(8,128)(2,1)}, bf16[2,512,128]{2,1,0:T(8,128)(2,1)S(1)}, u32[]{:S(2)}, u32[]{:S(2)}) collective-permute-start(bf16[2,512,128]{2,1,0:T(8,128)(2,1)} %get-tuple-element.177), channel_id=1, source_target_pairs={{0,24},{8,0},{16,8},{24,16},{32,56},{40,32},{48,40},{56,48},{1,25}... | collective-permute-start | bytes 786440 | tf_op jit(solution)/shard_map/ppermute | solution.py:54
  13.9 13.7 %collective-permute-start.7 = (bf16[2,512,128]{2,1,0:T(8,128)(2,1)}, bf16[2,512,128]{2,1,0:T(8,128)(2,1)S(1)}, u32[]{:S(2)}, u32[]{:S(2)}) collective-permute-start(bf16[2,512,128]{2,1,0:T(8,128)(2,1)} %get-tuple-element.178), channel_id=1, source_target_pairs={{0,16},{8,24},{16,0},{24,8},{32,48},{40,56},{48,32},{56,40},{1,17}... | collective-permute-start | bytes 786440 | tf_op jit(solution)/shard_map/ppermute | solution.py:54
  18.1 15.1 %collective-permute-start.1 = (bf16[2,512,128]{2,1,0:T(8,128)(2,1)S(1)}, bf16[2,512,128]{2,1,0:T(8,128)(2,1)S(1)}, u32[]{:S(2)}, u32[]{:S(2)}) collective-permute-start(bf16[2,512,128]{2,1,0:T(8,128)(2,1)S(1)} %collective-permute-done.refs_0_), channel_id=1, source_target_pairs={{0,8},{8,16},{16,24},{24,0},{32,40},{40,48},{48,56},{56,32},{1,9},... | collective-permute-start | bytes 786440 | tf_op jit(solution)/shard_map/ppermute | solution.py:54
  20.3 13.0 %collective-permute-start.2 = (bf16[2,512,128]{2,1,0:T(8,128)(2,1)S(1)}, bf16[2,512,128]{2,1,0:T(8,128)(2,1)S(1)}, u32[]{:S(2)}, u32[]{:S(2)}) collective-permute-start(bf16[2,512,128]{2,1,0:T(8,128)(2,1)S(1)} %collective-permute-done.refs_0_), channel_id=1, source_target_pairs={{0,24},{8,0},{16,8},{24,16},{32,56},{40,32},{48,40},{56,48},{1,25}... | collective-permute-start | bytes 786440 | tf_op jit(solution)/shard_map/ppermute | solution.py:54
  21.6 16.6 %collective-permute-start.3 = (bf16[2,512,128]{2,1,0:T(8,128)(2,1)S(1)}, bf16[2,512,128]{2,1,0:T(8,128)(2,1)S(1)}, u32[]{:S(2)}, u32[]{:S(2)}) collective-permute-start(bf16[2,512,128]{2,1,0:T(8,128)(2,1)S(1)} %collective-permute-done.refs_0_), channel_id=1, source_target_pairs={{0,16},{8,24},{16,0},{24,8},{32,48},{40,56},{48,32},{56,40},{1,17}... | collective-permute-start | bytes 786440 | tf_op jit(solution)/shard_map/ppermute | solution.py:54
  22.4 1.2 %copy-start = (bf16[1,512,1024]{2,1,0:T(8,128)(2,1)S(1)}, bf16[1,512,1024]{2,1,0:T(8,128)(2,1)}, u32[]{:S(2)}) copy-start(bf16[1,512,1024]{2,1,0:T(8,128)(2,1)} %param.10) | copy-start | bytes 3145732
  23.7 1.2 %copy-start.2 = (bf16[1,512,1024]{2,1,0:T(8,128)(2,1)S(1)}, bf16[1,512,1024]{2,1,0:T(8,128)(2,1)}, u32[]{:S(2)}) copy-start(bf16[1,512,1024]{2,1,0:T(8,128)(2,1)} %param.11) | copy-start | bytes 3145732
  24.9 0.9 copy-start.5
  25.8 1.8 %copy-start.4 = (bf16[4,1024,128]{2,1,0:T(8,128)(2,1)S(1)}, bf16[4,1024,128]{2,1,0:T(8,128)(2,1)}, u32[]{:S(2)}) copy-start(bf16[4,1024,128]{2,1,0:T(8,128)(2,1)} %proj_own_ref.1) | copy-start | bytes 3145732
  25.8 1.8 %copy-start.7 = (bf16[2,2,512,128]{3,2,1,0:T(8,128)(2,1)S(1)}, bf16[2,2,512,128]{3,2,1,0:T(8,128)(2,1)}, u32[]{:S(2)}) copy-start(bf16[2,2,512,128]{3,2,1,0:T(8,128)(2,1)} %get-tuple-element.173.own_ref) | copy-start | bytes 1572868
  27.7 10.5 %copy-start.6 = (f32[512,128]{1,0:T(8,128)S(1)}, f32[512,128]{1,0:T(8,128)}, u32[]{:S(2)}) copy-start(f32[512,128]{1,0:T(8,128)} %get-tuple-element.181.inv_rms_ref.refs_5_.refs_7_) | copy-start | bytes 786436
  27.7 10.5 %copy-start.8 = (f32[4,512,128]{2,1,0:T(8,128)S(1)}, f32[4,512,128]{2,1,0:T(8,128)}, u32[]{:S(2)}) copy-start(f32[4,512,128]{2,1,0:T(8,128)} %get-tuple-element.180.refs_4_) | copy-start | bytes 3145732
  27.7 10.5 %copy-start.9 = (f32[512,128]{1,0:T(8,128)S(1)}, f32[512,128]{1,0:T(8,128)}, u32[]{:S(2)}) copy-start(f32[512,128]{1,0:T(8,128)} %get-tuple-element.182.refs_6_) | copy-start | bytes 786436
  27.7 10.5 %copy-start.10 = (f32[512,128]{1,0:T(8,128)S(1)}, f32[512,128]{1,0:T(8,128)}, u32[]{:S(2)}) copy-start(f32[512,128]{1,0:T(8,128)} %get-tuple-element.184.refs_8_) | copy-start | bytes 786436
  27.7 10.5 %copy-start.12 = (bf16[512,128]{1,0:T(8,128)(2,1)S(1)}, bf16[512,128]{1,0:T(8,128)(2,1)}, u32[]{:S(2)}) copy-start(bf16[512,128]{1,0:T(8,128)(2,1)} %get-tuple-element.183.refs_7_) | copy-start | bytes 393220
  43.9 25.3 %all-to-all-start.1 = ((bf16[16,320,128]{2,1,0:T(8,128)(2,1)}), bf16[16,320,128]{2,1,0:T(8,128)(2,1)S(1)}, u32[]{:S(2)}, u32[]{:S(2)}) async-start(bf16[16,320,128]{2,1,0:T(8,128)(2,1)} %get-tuple-element.189), calls=%async_computation.1 | async-start | bytes 2621440 | tf_op jit(solution)/shard_map/all_to_all | solution.py:37
  48.0 13.4 %copy-start.1 = (bf16[1,512,1024]{2,1,0:T(8,128)(2,1)S(1)}, bf16[1,512,1024]{2,1,0:T(8,128)(2,1)}, u32[]{:S(2)}) copy-start(bf16[1,512,1024]{2,1,0:T(8,128)(2,1)} %param.10) | copy-start | bytes 3145732
  48.1 13.4 %copy-start.3 = (bf16[1,512,1024]{2,1,0:T(8,128)(2,1)S(1)}, bf16[1,512,1024]{2,1,0:T(8,128)(2,1)}, u32[]{:S(2)}) copy-start(bf16[1,512,1024]{2,1,0:T(8,128)(2,1)} %param.11) | copy-start | bytes 3145732
  48.1 2.4 %collective-permute-start.8 = (bf16[528,512]{1,0:T(8,128)(2,1)S(1)}, bf16[528,512]{1,0:T(8,128)(2,1)S(1)}, u32[]{:S(2)}, u32[]{:S(2)}) collective-permute-start(bf16[528,512]{1,0:T(8,128)(2,1)S(1)} %get-tuple-element.192.own_ref), channel_id=1, source_target_pairs={{0,1},{1,0},{2,3},{3,2},{4,5},{5,4},{6,7},{7,6},{8,9},{9,8},{10,11... | collective-permute-start | bytes 1622024 | tf_op jit(solution)/shard_map/ppermute | solution.py:62
  51.2 6.2 %collective-permute-start.10 = (bf16[528,128]{1,0:T(8,128)(2,1)S(1)}, bf16[528,128]{1,0:T(8,128)(2,1)S(1)}, u32[]{:S(2)}, u32[]{:S(2)}) collective-permute-start(bf16[528,128]{1,0:T(8,128)(2,1)S(1)} %get-tuple-element.197), channel_id=1, source_target_pairs={{0,2},{1,3},{2,4},{3,5},{4,6},{5,7},{6,0},{7,1},{8,10},{9,11},{10,... | collective-permute-start | bytes 405512 | tf_op jit(solution)/shard_map/ppermute | solution.py:58
  52.6 4.8 %collective-permute-start.11 = (bf16[528,128]{1,0:T(8,128)(2,1)S(1)}, bf16[528,128]{1,0:T(8,128)(2,1)S(1)}, u32[]{:S(2)}, u32[]{:S(2)}) collective-permute-start(bf16[528,128]{1,0:T(8,128)(2,1)S(1)} %get-tuple-element.198), channel_id=1, source_target_pairs={{0,6},{1,7},{2,0},{3,1},{4,2},{5,3},{6,4},{7,5},{8,14},{9,15},{10,... | collective-permute-start | bytes 405512 | tf_op jit(solution)/shard_map/ppermute | solution.py:58
  54.1 7.3 %collective-permute-start.9 = (bf16[528,128]{1,0:T(8,128)(2,1)S(1)}, bf16[528,128]{1,0:T(8,128)(2,1)S(1)}, u32[]{:S(2)}, u32[]{:S(2)}) collective-permute-start(bf16[528,128]{1,0:T(8,128)(2,1)S(1)} %get-tuple-element.196), channel_id=1, source_target_pairs={{0,4},{1,5},{2,6},{3,7},{4,0},{5,1},{6,2},{7,3},{8,12},{9,13},{10,... | collective-permute-start | bytes 405512 | tf_op jit(solution)/shard_map/ppermute | solution.py:58
  63.1 11.5 %collective-permute-start.12 = (bf16[4,144,128]{2,1,0:T(8,128)(2,1)S(1)}, bf16[4,144,128]{2,1,0:T(8,128)(2,1)S(1)}, u32[]{:S(2)}, u32[]{:S(2)}) collective-permute-start(bf16[4,144,128]{2,1,0:T(8,128)(2,1)S(1)} %get-tuple-element.202), channel_id=1, source_target_pairs={{0,16},{8,24},{16,0},{24,8},{64,80},{72,88},{80,64},{88,72},{32,48... | collective-permute-start | bytes 442376 | tf_op jit(solution)/shard_map/ppermute | solution.py:49
  66.6 8.1 %collective-permute-start.13 = (bf16[4,144,128]{2,1,0:T(8,128)(2,1)S(1)}, bf16[4,144,128]{2,1,0:T(8,128)(2,1)S(1)}, u32[]{:S(2)}, u32[]{:S(2)}) collective-permute-start(bf16[4,144,128]{2,1,0:T(8,128)(2,1)S(1)} %get-tuple-element.203), channel_id=1, source_target_pairs={{0,8},{8,16},{16,24},{24,0},{64,72},{72,80},{80,88},{88,64},{32,40... | collective-permute-start | bytes 442376 | tf_op jit(solution)/shard_map/ppermute | solution.py:49
  66.9 7.8 %collective-permute-start.14 = (bf16[4,144,128]{2,1,0:T(8,128)(2,1)S(1)}, bf16[4,144,128]{2,1,0:T(8,128)(2,1)S(1)}, u32[]{:S(2)}, u32[]{:S(2)}) collective-permute-start(bf16[4,144,128]{2,1,0:T(8,128)(2,1)S(1)} %get-tuple-element.204), channel_id=1, source_target_pairs={{0,24},{8,0},{16,8},{24,16},{64,88},{72,64},{80,72},{88,80},{32,56... | collective-permute-start | bytes 442376 | tf_op jit(solution)/shard_map/ppermute | solution.py:49
  70.6 22.2 %all-to-all-start.2 = ((bf16[16,320,128]{2,1,0:T(8,128)(2,1)}), bf16[16,320,128]{2,1,0:T(8,128)(2,1)S(1)}, u32[]{:S(2)}, u32[]{:S(2)}) async-start(bf16[16,320,128]{2,1,0:T(8,128)(2,1)} %weight_sum.1), calls=%async_computation.2 | async-start | bytes 2621440 | tf_op jit(solution)/shard_map/all_to_all | solution.py:37
  74.8 19.5 %collective-permute-start.17 = (bf16[4,144,128]{2,1,0:T(8,128)(2,1)S(1)}, bf16[4,144,128]{2,1,0:T(8,128)(2,1)S(1)}, u32[]{:S(2)}, u32[]{:S(2)}) collective-permute-start(bf16[4,144,128]{2,1,0:T(8,128)(2,1)S(1)} %pad_maximum_fusion.3), channel_id=1, source_target_pairs={{0,32},{8,40},{16,48},{24,56},{64,96},{72,104},{80,112},{88,120},{... | collective-permute-start | bytes 442376 | tf_op jit(solution)/shard_map/ppermute | solution.py:49
  77.7 18.7 %collective-permute-start.16 = (bf16[4,144,128]{2,1,0:T(8,128)(2,1)S(1)}, bf16[4,144,128]{2,1,0:T(8,128)(2,1)S(1)}, u32[]{:S(2)}, u32[]{:S(2)}) collective-permute-start(bf16[4,144,128]{2,1,0:T(8,128)(2,1)S(1)} %pad_maximum_fusion.2), channel_id=1, source_target_pairs={{0,96},{8,104},{16,112},{24,120},{64,0},{72,8},{80,16},{88,24},{32... | collective-permute-start | bytes 442376 | tf_op jit(solution)/shard_map/ppermute | solution.py:49
  78.7 20.2 %collective-permute-start.15 = (bf16[4,144,128]{2,1,0:T(8,128)(2,1)S(1)}, bf16[4,144,128]{2,1,0:T(8,128)(2,1)S(1)}, u32[]{:S(2)}, u32[]{:S(2)}) collective-permute-start(bf16[4,144,128]{2,1,0:T(8,128)(2,1)S(1)} %pad_maximum_fusion.1), channel_id=1, source_target_pairs={{0,64},{8,72},{16,80},{24,88},{64,32},{72,40},{80,48},{88,56},{32,... | collective-permute-start | bytes 442376 | tf_op jit(solution)/shard_map/ppermute | solution.py:49
